TPU v7x, 32 devices: a whole 2x2x4 slice. The times are simulated.
32 devices in a mesh: chan: 8 (over z, y), win: 4 (over x, core).
Axes of the slice: x: 2, y: 2, z: 4, core: 2. Of those that a mesh axis runs over, the one named last changes fastest.
Arguments:
- traces: float32 [64, 49152], P('chan', 'win')
- offsets: int32 [4], P('win'), may hold values from 0 to 4096
- pair_source: int32 [8, 24], P('chan'), may hold values from 0 to 7
- pair_recv: int32 [8, 24], P('chan'), may hold values from 0 to 7
- pair_hop: int32 [8, 24], P('chan'), may hold values from 0 to 6, never falling along the last dimension, each value on 1 to 6 neighbouring positions
- pair_owner: int32 [192, 1], P('chan'), may hold values from 0 to 7; in each aligned block of 24 rows (0 to 23, 24 to 47, ...) at most 6 rows name the same one
Outputs:
- stacks: float32 [384, 2, 2048], P('chan', None, 'win')
Inputs may be any that keep to these rules, and one draw needn't show every extreme that they name: `pair_hop`: within each block the pairs are ordered by offset index; every offset index has 1 to 6 pairs in a block, and some has exactly 6. `pair_owner`: at most 6 pairs of one block feed one owner, and some owner gets exactly 6.
All inputs are finite; a program needn't handle non-finite values.
Results may differ from a plain program's by a relative error of at most 0.022.
Values may be sent and summed in bfloat16 or wider, within the bound.
No kernel may reach another device: no remote copies, remote signals or barrier semaphores. Data moves between devices by JAX's collectives and lax.ppermute only.
A program may use at most 128 MiB of HBM per device.

v0:
```python
import math

import jax
import jax.numpy as jnp
from jax import lax
from jax.sharding import PartitionSpec as P

NT = 8192
F = 2048
SMOOTH_HALF = 32
FX = 2112


def shifted(value, axis, by):
    peers = lax.axis_size(axis)
    return lax.ppermute(value, axis, [(i, (i + by) % peers) for i in range(peers)])


def transform(rows_data):
    count_rows = rows_data.shape[0]
    quarter = NT // 4
    outer_count = FX // 4
    corner = jnp.arange(4, dtype=jnp.int32)
    phase_four = (corner[:, None] * corner[None, :] % 4).astype(jnp.float32) * (math.pi / 2.0)
    cos_four = jnp.cos(phase_four)
    sin_four = jnp.sin(phase_four)
    folded = rows_data.reshape(count_rows, 4, quarter)
    first_real = jnp.einsum("rab,ak->rkb", folded, cos_four, precision=lax.Precision.HIGHEST)
    first_imag = -jnp.einsum("rab,ak->rkb", folded, sin_four, precision=lax.Precision.HIGHEST)
    inner = jnp.arange(quarter, dtype=jnp.int32)
    twist = (corner[:, None] * inner[None, :] % NT).astype(jnp.float32) * (2.0 * math.pi / NT)
    twist_cos = jnp.cos(twist)
    twist_sin = jnp.sin(twist)
    mixed_real = (first_real * twist_cos + first_imag * twist_sin).reshape(count_rows * 4, quarter)
    mixed_imag = (first_imag * twist_cos - first_real * twist_sin).reshape(count_rows * 4, quarter)
    outer = jnp.arange(outer_count, dtype=jnp.int32)
    table = (inner[:, None] * outer[None, :] % quarter).astype(jnp.float32) * (
        2.0 * math.pi / quarter
    )
    table_cos = jnp.cos(table)
    table_sin = jnp.sin(table)
    high = lax.Precision.HIGHEST
    out_real = jnp.dot(mixed_real, table_cos, precision=high) + jnp.dot(
        mixed_imag, table_sin, precision=high
    )
    out_imag = jnp.dot(mixed_imag, table_cos, precision=high) - jnp.dot(
        mixed_real, table_sin, precision=high
    )
    out_real = (
        out_real.reshape(count_rows, 4, outer_count).transpose(0, 2, 1).reshape(count_rows, FX)
    )
    out_imag = (
        out_imag.reshape(count_rows, 4, outer_count).transpose(0, 2, 1).reshape(count_rows, FX)
    )
    return (out_real, out_imag)


def whiten(segment):
    centred = segment - jnp.mean(segment, axis=1, keepdims=True)
    positions = jnp.arange(NT, dtype=jnp.int32).astype(jnp.float32)
    taper = 0.5 - 0.5 * jnp.cos(2.0 * math.pi / NT * positions)
    real_part, imag_part = transform(centred * taper)
    power = real_part * real_part + imag_part * imag_part
    level = lax.reduce_window(
        power, jnp.zeros((), power.dtype), lax.add, (1, 2 * SMOOTH_HALF + 1), (1, 1), "VALID"
    ) / (2 * SMOOTH_HALF + 1)
    scale = lax.rsqrt(level + 1e-06)
    kept_real = real_part[:, SMOOTH_HALF : SMOOTH_HALF + F] * scale
    kept_imag = imag_part[:, SMOOTH_HALF : SMOOTH_HALF + F] * scale
    return jnp.stack([kept_real, kept_imag], axis=1).astype(jnp.bfloat16)


def forward_move(carried):
    return shifted(carried, "chan", 1)


def local(traces, offsets, pair_source, pair_recv, pair_hop, pair_owner):
    chan_count = lax.axis_size("chan")
    local_channels = traces.shape[0]
    local_windows = offsets.shape[0]
    pair_slots = pair_source.shape[1]
    reach_blocks = min(8, (chan_count - 1) // 2)
    offset_count = 2 * reach_blocks + 1
    run_rows = 2 * pair_slots // offset_count
    capacity = 2 * ((pair_slots + chan_count - 1) // chan_count)
    segment = jnp.stack([lax.dynamic_slice_in_dim(traces, offsets[0], NT, 1)], axis=1)
    white = whiten(segment.reshape(local_channels * local_windows, NT))
    white = white.reshape(local_channels, local_windows, 2, F)
    source_list = pair_source.reshape(-1)
    receiver_list = pair_recv.reshape(-1)
    hop_list = pair_hop.reshape(-1)
    owner_list = pair_owner.reshape(-1)
    offset_ids = jnp.arange(offset_count, dtype=jnp.int32)
    starts = jnp.sum((hop_list[None, :] < offset_ids[:, None]).astype(jnp.int32), axis=1)

    def offset_terms(carried, offset_index):
        before = jnp.take(starts, offset_index)
        positions = before + jnp.arange(run_rows, dtype=jnp.int32)
        clipped = jnp.minimum(positions, pair_slots - 1)
        source_rows = jnp.take(white, jnp.take(source_list, clipped), axis=0).astype(jnp.float32)
        receiver_rows = jnp.take(carried, jnp.take(receiver_list, clipped), axis=0).astype(
            jnp.float32
        )
        real_part = jnp.sum(
            source_rows[:, :, 0] * receiver_rows[:, :, 0]
            + source_rows[:, :, 1] * receiver_rows[:, :, 1],
            axis=1,
        )
        imag_part = jnp.sum(
            source_rows[:, :, 0] * receiver_rows[:, :, 1]
            - source_rows[:, :, 1] * receiver_rows[:, :, 0],
            axis=1,
        )
        return jnp.stack([real_part, imag_part], axis=1)

    local_terms = offset_terms(white, jnp.int32(reach_blocks))

    def advance(carried, index):
        carried = forward_move(carried)
        offset_index = jnp.where(
            index <= reach_blocks, reach_blocks - index, reach_blocks + chan_count - index
        )
        offset_index = jnp.clip(offset_index, 0, offset_count - 1)
        return (carried, offset_terms(carried, offset_index))

    unused, moved_terms = lax.scan(advance, white, jnp.arange(1, chan_count, dtype=jnp.int32))
    collected = jnp.concatenate([local_terms[None], moved_terms], axis=0)
    position = jnp.where(
        hop_list == reach_blocks,
        0,
        jnp.where(
            hop_list < reach_blocks, reach_blocks - hop_list, reach_blocks + chan_count - hop_list
        ),
    )
    rank = jnp.arange(pair_slots, dtype=jnp.int32) - jnp.take(starts, hop_list)
    flat_rows = position * run_rows + rank
    band = collected.shape[-1]
    totals = jnp.take(collected.reshape(-1, 2, band), flat_rows, axis=0)
    partial_value = lax.optimization_barrier(totals.astype(jnp.bfloat16))
    onehot = (owner_list[:, None] == jnp.arange(chan_count, dtype=jnp.int32)[None, :]).astype(
        jnp.int32
    )
    earlier = jnp.cumsum(onehot, axis=0) - onehot
    slot = jnp.sum(earlier * onehot, axis=1)
    target = owner_list * capacity + slot
    dispatch = jnp.arange(chan_count * capacity, dtype=jnp.int32)[:, None] == target[None, :]
    outgoing = jnp.dot(
        dispatch.astype(jnp.bfloat16),
        partial_value.reshape(pair_slots, 2 * F),
        preferred_element_type=jnp.float32,
    )
    outgoing = outgoing.astype(jnp.bfloat16).reshape(chan_count, capacity, 2, F)
    arrived = lax.all_to_all(outgoing, "chan", split_axis=0, concat_axis=0, tiled=True)
    summed = lax.psum_scatter(
        arrived.astype(jnp.float32).astype(jnp.bfloat16), "win", scatter_dimension=3, tiled=True
    ).astype(jnp.float32)
    return summed.reshape(chan_count * capacity, 2, summed.shape[3])


def solution(mesh):
    placed = (
        P("chan", "win"),
        P("win"),
        P("chan", None),
        P("chan", None),
        P("chan", None),
        P("chan", None),
    )
    return jax.shard_map(
        local, mesh=mesh, in_specs=placed, out_specs=P("chan", None, "win"), check_vma=False
    )
```

profile of v0, /device:TPU:0, one launch (start us, length us, event | category | flops | bytes accessed | tf_op | source)
XLA Modules:
  0.0 357.2 jit_solution(12462076705590564885)
XLA Ops:
  11.7 1.2 dynamic-slice_reduce_fusion
  13.0 1.1 subtract_multiply_fusion
  15.7 22.8 %fusion.13 = f32[32,528]{1,0:T(8,128)S(1)} fusion(f32[32,2048]{1,0:T(8,128)S(1)} %reshape.523), kind=kOutput, calls=%fused_computation.40 | convolution fusion | flops 430374912 | bytes 329728 | tf_op jit(solution)/shard_map/dot_general | solution.py:43
  38.5 22.5 %fusion.11 = f32[32,528]{1,0:T(8,128)S(1)} fusion(f32[32,2048]{1,0:T(8,128)S(1)} %reshape.524), kind=kOutput, calls=%fused_computation.39 | convolution fusion | flops 430374912 | bytes 329728 | tf_op jit(solution)/shard_map/dot_general | solution.py:46
  61.0 23.2 %fusion.19 = f32[32,528]{1,0:T(8,128)S(1)} fusion(f32[32,528]{1,0:T(8,128)S(1)} %fusion.13, f32[32,2048]{1,0:T(8,128)S(1)} %reshape.524), kind=kOutput, calls=%fused_computation.44 | convolution fusion | flops 430391808 | bytes 397312 | tf_op jit(solution)/shard_map/dot_general | solution.py:43
  84.2 22.8 %fusion.22 = f32[32,528]{1,0:T(8,128)S(1)} fusion(f32[32,528]{1,0:T(8,128)S(1)} %fusion.11, f32[32,2048]{1,0:T(8,128)S(1)} %reshape.523), kind=kOutput, calls=%fused_computation.45 | convolution fusion | flops 430391808 | bytes 397312 | tf_op jit(solution)/shard_map/dot_general | solution.py:46
  107.9 1.1 slice.80
  111.8 1.5 copy.62
  114.0 18.3 %reduce_window.7 = f32[8,2048]{1,0:T(8,128)S(1)} reduce-window(f32[8,2112]{1,0:T(8,128)S(1)} %copy.49, f32[]{:T(128)} %constant.165.clone.1), window={size=1x65}, to_apply=%region_4.5 | reduce-window | flops 1048576 | bytes 133124 | tf_op jit(solution)/shard_map/reduce_window | solution.py:64
  134.8 66.8 %while.14 = (s32[]{:T(128)}, bf16[8,1,2,2048]{3,2,1,0:T(2,128)(2,1)S(1)}, bf16[7,6,2,2048]{3,2,1,0:T(2,128)(2,1)}, s32[7]{0:T(128)S(1)}, s32[7]{0:T(128)S(1)}, /...) while((s32[]{:T(128)}, ...), condition=%wide.region_6.9_spmd, body=%wide.region_5.8_spmd.sunk | while | flops 298204 | bytes 1241809 | solution.py:126
  134.8 3.0 collective-permute-start
  145.6 1.6 collective-permute-start
  154.9 1.6 collective-permute-start
  164.2 1.6 collective-permute-start
  173.5 1.6 collective-permute-start
  182.8 1.6 collective-permute-start
  192.1 1.6 collective-permute-start
  201.6 1.5 pad_maximum_fusion
  204.9 14.4 %all_to_all.5 = bf16[8,6,2,2048]{3,2,1,0:T(2,128)(2,1)S(1)} all-to-all(bf16[8,6,2,2048]{3,2,1,0:T(2,128)(2,1)S(1)} %reshape.533), channel_id=1, replica_groups=mesh['chan'=8,'win'=4] {'chan'}, dimensions={0} | all-to-all | bytes 786432 | tf_op jit(solution)/shard_map/all_to_all | solution.py:153
  219.3 45.6 %copy.59 = bf16[8,6,2,2048]{2,1,0,3:T(8,128)(2,1)} copy(bf16[8,6,2,2048]{3,2,1,0:T(2,128)(2,1)S(1)} %all_to_all.5) | data formatting | bytes 786432
  264.8 40.0 %reshape.703 = bf16[2048,96]{1,0:T(8,128)(2,1)} reshape(bf16[2048,8,6,2]{3,2,1,0:T(8,128)(2,1)} %bitcast.129) | data formatting | bytes 786432
  304.8 20.5 %reduce-scatter.4.cloned.1.call-done = bf16[512,96]{1,0:T(8,128)(2,1)} async-done(((bf16[2048,96]{1,0:T(8,128)(2,1)}), bf16[512,96]{1,0:T(8,128)(2,1)}) %reduce-scatter.4.cloned.1.call-update) | async-done | bytes 98320
  325.3 15.7 %reshape.704 = bf16[512,8,6,2]{3,2,1,0:T(8,128)(2,1)} reshape(bf16[512,96]{1,0:T(8,128)(2,1)} %reduce-scatter.4.cloned.1.call-done) | data formatting | bytes 196608
  341.0 8.2 %copy.60 = bf16[8,6,2,512]{3,2,1,0:T(2,128)(2,1)S(1)} copy(bf16[8,6,2,512]{2,1,0,3:T(8,128)(2,1)} %bitcast.130) | data formatting | bytes 196608
  (181 shorter events, 50.4 us)
Async XLA Ops:
  6.5 318.8 %reduce-scatter.4.cloned.1.call-start = ((), (), s32[]{:S(2)}) async-start(), calls=%async_computation.2 | async-start | bytes 655360
  107.0 2.9 copy-start.1
  107.0 3.5 copy-start
  109.0 25.2 %copy-start.2 = (s32[24,1]{0,1:T(1,128)S(1)}, s32[24,1]{0,1:T(1,128)}, u32[]{:S(2)}) copy-start(s32[24,1]{0,1:T(1,128)} %param.17) | copy-start | bytes 292
  134.8 8.9 %collective-permute-start = (bf16[8,1,2,2048]{3,2,1,0:T(2,128)(2,1)S(1)}, bf16[8,1,2,2048]{3,2,1,0:T(2,128)(2,1)S(1)}, u32[]{:S(2)}, u32[]{:S(2)}) collective-permute-start(bf16[8,1,2,2048]{3,2,1,0:T(2,128)(2,1)S(1)} %get-tuple-element.222), channel_id=1, source_target_pairs={{0,4},{4,8},{8,12},{12,16},{16,20},{20,24},{24,28},{28,0},{1,5},{5... | collective-permute-start | bytes 196616 | tf_op jit(solution)/shard_map/while/body/eval_jaxpr/ppermute | solution.py:16
  145.6 7.5 %collective-permute-start = (bf16[8,1,2,2048]{3,2,1,0:T(2,128)(2,1)S(1)}, bf16[8,1,2,2048]{3,2,1,0:T(2,128)(2,1)S(1)}, u32[]{:S(2)}, u32[]{:S(2)}) collective-permute-start(bf16[8,1,2,2048]{3,2,1,0:T(2,128)(2,1)S(1)} %get-tuple-element.222), channel_id=1, source_target_pairs={{0,4},{4,8},{8,12},{12,16},{16,20},{20,24},{24,28},{28,0},{1,5},{5... | collective-permute-start | bytes 196616 | tf_op jit(solution)/shard_map/while/body/eval_jaxpr/ppermute | solution.py:16
  154.9 7.5 %collective-permute-start = (bf16[8,1,2,2048]{3,2,1,0:T(2,128)(2,1)S(1)}, bf16[8,1,2,2048]{3,2,1,0:T(2,128)(2,1)S(1)}, u32[]{:S(2)}, u32[]{:S(2)}) collective-permute-start(bf16[8,1,2,2048]{3,2,1,0:T(2,128)(2,1)S(1)} %get-tuple-element.222), channel_id=1, source_target_pairs={{0,4},{4,8},{8,12},{12,16},{16,20},{20,24},{24,28},{28,0},{1,5},{5... | collective-permute-start | bytes 196616 | tf_op jit(solution)/shard_map/while/body/eval_jaxpr/ppermute | solution.py:16
  164.2 7.5 %collective-permute-start = (bf16[8,1,2,2048]{3,2,1,0:T(2,128)(2,1)S(1)}, bf16[8,1,2,2048]{3,2,1,0:T(2,128)(2,1)S(1)}, u32[]{:S(2)}, u32[]{:S(2)}) collective-permute-start(bf16[8,1,2,2048]{3,2,1,0:T(2,128)(2,1)S(1)} %get-tuple-element.222), channel_id=1, source_target_pairs={{0,4},{4,8},{8,12},{12,16},{16,20},{20,24},{24,28},{28,0},{1,5},{5... | collective-permute-start | bytes 196616 | tf_op jit(solution)/shard_map/while/body/eval_jaxpr/ppermute | solution.py:16
  173.5 7.5 %collective-permute-start = (bf16[8,1,2,2048]{3,2,1,0:T(2,128)(2,1)S(1)}, bf16[8,1,2,2048]{3,2,1,0:T(2,128)(2,1)S(1)}, u32[]{:S(2)}, u32[]{:S(2)}) collective-permute-start(bf16[8,1,2,2048]{3,2,1,0:T(2,128)(2,1)S(1)} %get-tuple-element.222), channel_id=1, source_target_pairs={{0,4},{4,8},{8,12},{12,16},{16,20},{20,24},{24,28},{28,0},{1,5},{5... | collective-permute-start | bytes 196616 | tf_op jit(solution)/shard_map/while/body/eval_jaxpr/ppermute | solution.py:16
  182.8 7.5 %collective-permute-start = (bf16[8,1,2,2048]{3,2,1,0:T(2,128)(2,1)S(1)}, bf16[8,1,2,2048]{3,2,1,0:T(2,128)(2,1)S(1)}, u32[]{:S(2)}, u32[]{:S(2)}) collective-permute-start(bf16[8,1,2,2048]{3,2,1,0:T(2,128)(2,1)S(1)} %get-tuple-element.222), channel_id=1, source_target_pairs={{0,4},{4,8},{8,12},{12,16},{16,20},{20,24},{24,28},{28,0},{1,5},{5... | collective-permute-start | bytes 196616 | tf_op jit(solution)/shard_map/while/body/eval_jaxpr/ppermute | solution.py:16
  192.1 7.5 %collective-permute-start = (bf16[8,1,2,2048]{3,2,1,0:T(2,128)(2,1)S(1)}, bf16[8,1,2,2048]{3,2,1,0:T(2,128)(2,1)S(1)}, u32[]{:S(2)}, u32[]{:S(2)}) collective-permute-start(bf16[8,1,2,2048]{3,2,1,0:T(2,128)(2,1)S(1)} %get-tuple-element.222), channel_id=1, source_target_pairs={{0,4},{4,8},{8,12},{12,16},{16,20},{20,24},{24,28},{28,0},{1,5},{5... | collective-permute-start | bytes 196616 | tf_op jit(solution)/shard_map/while/body/eval_jaxpr/ppermute | solution.py:16
Sparse Core Ops, SparseCore 0:
  304.9 20.3 reduce-scatter.3
where the time goes:
time: 361 us; the launch traced here: 357 us
  local copies, waits for them, and re-layouts  146 us (40%)
  matrix products  92.9 us (26%)
  other arithmetic  36.3 us (10%)
  waiting for transfers between devices  20.6 us (6%)
  loops' own time  19.4 us (5%)
  between operations  14.6 us (4%)
  blocking collectives  14.4 us (4%)
  starting transfers between devices  12.5 us (3%)
    unnamed x15, local copies, waits for them, and re-layouts  112 us
    dot_general x1, matrix products, transform(): jnp.dot(mixed_imag, table_sin, precision=high)  23.2 us
    dot_general x1, matrix products, transform(): jnp.dot(mixed_real, table_sin, precision=high)  22.8 us
    dot_general x1, matrix products, transform(): jnp.dot(mixed_real, table_cos, precision=high)  22.8 us
    dot_general x1, matrix products, transform(): jnp.dot(mixed_imag, table_cos, precision=high)  22.5 us
    unnamed x2, waiting for transfers between devices  20.6 us
    another operation x1, loops' own time, local(): lax.scan(advance, white, jnp.arange(1, chan_count, dtype=jnp.int32))  19.4 us
    another operation x1, other arithmetic, whiten(): lax.reduce_window(power, jnp.zeros((), power.dtype), lax.add, (1, 2 * SMO...  18.3 us
  transfers between devices with their start and end apart: 8, of which 1 were waited for; matrix products, arithmetic and copies ran while one was open for 6% of the time, Pallas kernels for 0%

commit v1 on v0

v1 whole, which is shorter than its diff:
```python
import functools
import math

import jax
import jax.numpy as jnp
import numpy as np
from jax import lax
from jax.experimental import pallas as pl
from jax.experimental.pallas import tpu as pltpu
from jax.sharding import PartitionSpec as P

NT = 8192
F = 2048
SMOOTH_HALF = 32
LANES = 128
HIGH = NT // LANES
ROWS = F // LANES
GRID_ROWS = 24
F32 = jnp.float32
BF16 = jnp.bfloat16
HIGHEST = lax.Precision.HIGHEST


def tables():
    lane = np.arange(LANES)
    high = np.arange(HIGH)
    first = 2 * np.pi / HIGH * (np.outer(np.arange(HIGH) + SMOOTH_HALF, high) % HIGH)
    first = np.concatenate([np.cos(first), -np.sin(first)], axis=0)
    twist = 2 * np.pi / NT * (np.outer(lane + SMOOTH_HALF, lane) % NT)
    twist = np.stack([np.cos(twist), -np.sin(twist)])
    grid_row = np.arange(GRID_ROWS) - 1
    second = 2 * np.pi / HIGH * (np.outer(grid_row, lane) % HIGH)
    cos, sin = np.cos(second), -np.sin(second)
    live = (np.arange(GRID_ROWS) < ROWS + 2)[:, None]
    cos, sin = cos * live, sin * live
    second = np.concatenate(
        [np.concatenate([cos, -sin], axis=1), np.concatenate([sin, cos], axis=1)], axis=0
    )
    phase = 2 * np.pi / NT * np.arange(NT).reshape(HIGH, LANES)
    wave = np.stack([np.cos(phase), np.sin(phase)])
    source = np.arange(3 * LANES)[:, None] - LANES
    band = np.abs(source - lane[None, :]) <= SMOOTH_HALF
    return (
        first.astype(np.float32),
        twist.astype(np.float32),
        second.astype(np.float32),
        wave.astype(np.float32),
        band.astype(jnp.bfloat16),
    )


def split(value):
    top = value.astype(BF16)
    return top, (value - top.astype(F32)).astype(BF16)


def whiten_kernel(
    scalars, traces, source, receiver, hop, owner, first, twist, second, wave, band, *rest
):
    outs, (centred, grid_real, grid_imag, white) = rest[:-4], rest[-4:]
    windows = len(outs) - 1
    channels = traces.shape[0]
    offset, me = scalars[0], scalars[1]

    lane = lax.broadcasted_iota(jnp.int32, (channels, LANES), 1)
    total = jnp.zeros((channels, LANES), F32)
    blocks = []
    spare = traces.shape[1] // LANES - HIGH
    for i in range(HIGH):
        piece = traces[:, i * LANES : (i + 1) * LANES]
        if i < spare:
            later = traces[:, (i + HIGH) * LANES : (i + HIGH + 1) * LANES]
            piece = jnp.where(lane + i * LANES >= offset, piece, later)
        centred[i * channels : (i + 1) * channels, :] = piece
        total = total + piece
    mean = jnp.sum(total, axis=1, keepdims=True) * (1.0 / NT)
    centred[...] = centred[...] - jnp.tile(mean, (HIGH, 1))

    angle = jnp.full((8, LANES), offset, jnp.int32).astype(F32) * (2.0 * math.pi / NT)
    cos_off = jnp.cos(angle)[0:1, :]
    sin_off = jnp.sin(angle)[0:1, :]
    taper = 0.5 - 0.5 * (wave[0] * cos_off + wave[1] * sin_off)
    segment = jnp.concatenate(
        [centred[pl.ds(c, HIGH, stride=channels), :] * taper for c in range(channels)], axis=1
    )
    inner = jnp.dot(first[...], segment, precision=HIGHEST, preferred_element_type=F32)
    twist_cos, twist_sin = twist[0], twist[1]
    for c in range(channels):
        real = inner[:HIGH, c * LANES : (c + 1) * LANES]
        imag = inner[HIGH:, c * LANES : (c + 1) * LANES]
        real = jnp.concatenate([real, real], axis=0)
        imag = jnp.concatenate([imag, imag], axis=0)
        mixed = jnp.concatenate(
            [real * twist_cos - imag * twist_sin, real * twist_sin + imag * twist_cos], axis=1
        )
        bins = lax.dot_general(
            second[...],
            mixed,
            (((1,), (1,)), ((), ())),
            precision=HIGHEST,
            preferred_element_type=F32,
        )
        grid_real[pl.ds(c, GRID_ROWS, stride=channels), :] = bins[:GRID_ROWS]
        grid_imag[pl.ds(c, GRID_ROWS, stride=channels), :] = bins[GRID_ROWS:]

    live = (ROWS + 2) * channels
    real, imag = grid_real[:live, :], grid_imag[:live, :]
    power = (real * real + imag * imag) * (1.0 / (2 * SMOOTH_HALF + 1))
    place = lax.broadcasted_iota(jnp.int32, (channels, LANES), 1)
    head = jnp.where(place >= LANES - SMOOTH_HALF, power[:channels], 0.0)
    tail = jnp.where(place < SMOOTH_HALF, power[live - channels :], 0.0)
    power = jnp.concatenate([head, power[channels : live - channels], tail], axis=0)
    top, low = split(power)
    count = ROWS * channels
    around = [
        piece[i * channels : i * channels + count] for piece in (top, low) for i in range(3)
    ]
    level = jnp.dot(jnp.concatenate(around[:3], axis=1), band[...], preferred_element_type=F32)
    level += jnp.dot(jnp.concatenate(around[3:], axis=1), band[...], preferred_element_type=F32)
    scale = lax.rsqrt(level + 1e-06)
    kept_real = real[channels : channels + count] * scale
    kept_imag = imag[channels : channels + count] * scale
    part = ROWS // windows
    for i in range(ROWS):
        rows = slice(i * channels, (i + 1) * channels)
        tile = jnp.concatenate([kept_real[rows], kept_imag[rows]], axis=0).astype(BF16)
        white[i // part, :, (i % part) * LANES : (i % part + 1) * LANES] = tile
    for k in range(windows):
        outs[k][...] = white[me ^ k]
    fields = [f[...].astype(F32) for f in (source, receiver, hop, owner)]
    fields.append(jnp.zeros((2 * channels - 4, fields[0].shape[1]), F32))
    fields = jnp.concatenate(fields, axis=0)
    fields = jnp.concatenate(
        [fields, jnp.zeros((2 * channels, LANES - fields.shape[1]), F32)], axis=1
    )
    outs[windows][...] = fields.astype(BF16)


def stack_kernel(blocks, windows, capacity, reach, pair_slots, scalars, *rest):
    gathered, out = rest[:-1], rest[-1]
    me = scalars[0]
    height = gathered[0].shape[0]
    channels = height // 2
    width = (gathered[0].shape[1] - LANES) // windows
    slots = blocks * capacity
    meta = jnp.concatenate([g[:, windows * width :] for g in gathered], axis=0)

    row = lax.broadcasted_iota(jnp.int32, (slots, LANES), 0)
    lane = lax.broadcasted_iota(jnp.int32, (slots, LANES), 1)
    block = jnp.zeros((slots, LANES), jnp.int32)
    for b in range(1, blocks):
        block = block + (row >= b * capacity).astype(jnp.int32)
    slot = row - block * capacity

    def pick(index, size):
        spot = lax.broadcasted_iota(jnp.int32, (slots, size), 1)
        index = jnp.concatenate([index] * (size // LANES), axis=1)
        return jnp.where(spot == index, 1.0, 0.0).astype(BF16)

    base = (block ^ me) * height
    depth = blocks * height
    table = jnp.dot(
        jnp.concatenate([pick(base + i, depth) for i in range(4)], axis=0),
        meta,
        preferred_element_type=F32,
    )
    source, receiver, hop, owner = [table[i * slots : (i + 1) * slots] for i in range(4)]
    mine = jnp.where((owner == me.astype(F32)) & (lane < pair_slots), 1.0, 0.0)
    above = lax.broadcasted_iota(jnp.int32, (LANES, LANES), 0)
    below = lax.broadcasted_iota(jnp.int32, (LANES, LANES), 1)
    earlier = jnp.where(above < below, 1.0, 0.0).astype(BF16)
    rank = jnp.dot(mine.astype(BF16), earlier, preferred_element_type=F32)
    chosen = jnp.where(rank == slot.astype(F32), mine, 0.0)

    def value_of(field):
        return jnp.sum(chosen * field, axis=1, keepdims=True).astype(jnp.int32)

    filled = jnp.sum(chosen, axis=1, keepdims=True) > 0.5
    target = block + value_of(hop) - reach
    target = jnp.where(target < 0, target + blocks, target)
    target = jnp.where(target >= blocks, target - blocks, target)
    source_row = base + value_of(source)
    receiver_row = (target ^ me) * height + value_of(receiver)
    source_row = jnp.where(filled, source_row, -depth)
    receiver_row = jnp.where(filled, receiver_row, -depth)
    choice = jnp.concatenate(
        [
            pick(source_row, depth),
            pick(source_row + channels, depth),
            pick(receiver_row, depth),
            pick(receiver_row + channels, depth),
        ],
        axis=0,
    )
    real = jnp.zeros((slots, width), F32)
    imag = jnp.zeros((slots, width), F32)
    for w in range(windows):
        white = jnp.concatenate([g[:, w * width : (w + 1) * width] for g in gathered], axis=0)
        rows = jnp.dot(choice, white, preferred_element_type=F32)
        sr, si, rr, ri = [rows[i * slots : (i + 1) * slots] for i in range(4)]
        real += sr * rr + si * ri
        imag += sr * ri - si * rr
    parts = width // LANES
    for i in range(parts):
        lanes = slice(i * LANES, (i + 1) * LANES)
        out[pl.ds(2 * i, slots, stride=2 * parts), :] = real[:, lanes]
        out[pl.ds(2 * i + 1, slots, stride=2 * parts), :] = imag[:, lanes]


def swapped(value, axis, bits):
    peers = lax.axis_size(axis)
    return lax.ppermute(value, axis, [(i, i ^ bits) for i in range(peers)])


def local(traces, offsets, pair_source, pair_recv, pair_hop, pair_owner):
    blocks = lax.axis_size("chan")
    windows = lax.axis_size("win")
    channels = traces.shape[0]
    pair_slots = pair_source.shape[1]
    reach = min(8, (blocks - 1) // 2)
    capacity = 2 * ((pair_slots + blocks - 1) // blocks)
    width = F // windows
    vmem = pl.BlockSpec(memory_space=pltpu.VMEM)
    smem = pl.BlockSpec(memory_space=pltpu.SMEM)
    height = 2 * channels

    scalars = jnp.stack([offsets[0], lax.axis_index("win").astype(jnp.int32)])
    constants = [jnp.asarray(t) for t in tables()]
    pieces = pl.pallas_call(
        whiten_kernel,
        out_shape=[jax.ShapeDtypeStruct((height, width), BF16)] * windows
        + [jax.ShapeDtypeStruct((height, LANES), BF16)],
        in_specs=[smem] + [vmem] * 10,
        out_specs=[vmem] * (windows + 1),
        scratch_shapes=[
            pltpu.VMEM((HIGH * channels, LANES), F32),
            pltpu.VMEM((GRID_ROWS * channels, LANES), F32),
            pltpu.VMEM((GRID_ROWS * channels, LANES), F32),
            pltpu.VMEM((windows, height, width), BF16),
        ],
        compiler_params=pltpu.CompilerParams(vmem_limit_bytes=32 << 20),
        name="whiten",
    )(scalars, traces, pair_source, pair_recv, pair_hop, pair_owner.reshape(1, -1), *constants)
    moved = [pieces[0]] + [swapped(pieces[k], "win", k) for k in range(1, windows)]
    packed = jnp.concatenate(moved + [pieces[windows]], axis=1)

    gathered = {0: packed}
    for k in range(2, blocks, 2):
        gathered[k] = swapped(packed, "chan", k)
    for k in range(0, blocks, 2):
        gathered[k + 1] = swapped(gathered[k], "chan", 1)

    stacked = pl.pallas_call(
        functools.partial(stack_kernel, blocks, windows, capacity, reach, pair_slots),
        out_shape=jax.ShapeDtypeStruct((blocks * capacity * 2 * width // LANES, LANES), F32),
        in_specs=[smem] + [vmem] * blocks,
        out_specs=vmem,
        compiler_params=pltpu.CompilerParams(vmem_limit_bytes=32 << 20),
        name="stack",
    )(
        lax.axis_index("chan").astype(jnp.int32).reshape(1),
        *[gathered[k] for k in range(blocks)],
    )
    stacked = stacked.reshape(blocks * capacity, width // LANES, 2, LANES)
    return stacked.transpose(0, 2, 1, 3).reshape(blocks * capacity, 2, width)


def solution(mesh):
    placed = (
        P("chan", "win"),
        P("win"),
        P("chan", None),
        P("chan", None),
        P("chan", None),
        P("chan", None),
    )
    return jax.shard_map(
        local, mesh=mesh, in_specs=placed, out_specs=P("chan", None, "win"), check_vma=False
    )
```

time: 361 us -> 33 us (0.09)
  local copies, waits for them, and re-layouts: 146 us -> 5.97 us
  matrix products: 92.9 us -> 0 us
  other arithmetic: 36.3 us -> 0.08 us
  loops' own time: 19.4 us -> 0 us
  blocking collectives: 14.4 us -> 0 us
  between operations: 14.6 us -> 0.69 us
  waiting for transfers between devices: 20.6 us -> 9.26 us
  Pallas kernels: 0 us -> 4.06 us
    unnamed x15 -> x24, local copies, waits for them, and re-layouts: 112 us -> 5.96 us
    dot_general x7 -> x0, matrix products: 92.9 us -> none  [the longest x1 23.2 us: transform(): jnp.dot(mixed_imag, table_sin, precision=high)]
    gather x34 -> x0, local copies, waits for them, and re-layouts: 22.4 us -> none  [the longest x8 5.2 us: offset_terms(): jnp.take(white, jnp.take(source_list, clipped), axis=0).astype(jnp.float32)]
    unnamed x2 -> x0, waiting for transfers between devices: 20.6 us -> none
    another operation x1 -> x0, loops' own time: 19.4 us -> none  [local(): lax.scan(advance, white, jnp.arange(1, chan_count, dtype=jnp.int32))]
    another operation x4 -> x1, other arithmetic: 18.4 us -> 0.08 us  [local(): scalars = jnp.stack([offsets[0], lax.axis_index('win').astype(jnp.int32)])]
    all_to_all x1 -> x0, blocking collectives: 14.4 us -> none  [local(): lax.all_to_all(outgoing, 'chan', split_axis=0, concat_axis=0, tiled=True)]
    ppermute x7 -> x10, waiting for transfers between devices: 0.02 us -> 9.26 us  [swapped(): return lax.ppermute(value, axis, [(i, i ^ bits) for i in range(peers)])]
  transfers between devices with their start and end apart: 8 -> 10, of which waited for: 1 -> 6; matrix products, arithmetic and copies ran while one was open for 6% -> 0% of each run, Pallas kernels for 0% -> 0%
where the time goes in v1:
time: 33 us; the launch traced here: 32.7 us
  starting transfers between devices  12.6 us (38%)
  waiting for transfers between devices  9.26 us (28%)
  local copies, waits for them, and re-layouts  5.97 us (18%)
  Pallas kernels  4.06 us (12%)
  between operations  0.69 us (2%)
    ppermute x10, starting transfers between devices, swapped(): return lax.ppermute(value, axis, [(i, i ^ bits) for i in range(peers)])  12.6 us
    ppermute x10, waiting for transfers between devices, swapped(): return lax.ppermute(value, axis, [(i, i ^ bits) for i in range(peers)])  9.26 us
    unnamed x24, local copies, waits for them, and re-layouts  5.96 us
    pallas_call x1, Pallas kernels, local(): pl.pallas_call(whiten_kernel, out_shape=[jax.ShapeDtypeStruct((height, wi...  2.66 us
    pallas_call x1, Pallas kernels, local(): pl.pallas_call(functools.partial(stack_kernel, blocks, windows, capacity,...  1.39 us
  transfers between devices with their start and end apart: 10, of which 6 were waited for; matrix products, arithmetic and copies ran while one was open for 0% of the time, Pallas kernels for 0%

profile of v1, /device:TPU:0, one launch (start us, length us, event | category | flops | bytes accessed | tf_op | source)
XLA Modules:
  0.0 32.7 jit_solution(14916718815564003742)
XLA Ops:
  0.7 0.6 %copy-done.9 = s32[24,1]{0,1:T(1,128)S(1)} copy-done((s32[24,1]{0,1:T(1,128)S(1)}, s32[24,1]{0,1:T(1,128)}, u32[]{:S(2)}) %copy-start.9) | copy-done | bytes 120
  1.3 0.1 copy-done.6
  1.4 1.0 %copy-done = f32[8,12288]{1,0:T(8,128)S(1)} copy-done((f32[8,12288]{1,0:T(8,128)S(1)}, f32[8,12288]{1,0:T(8,128)}, u32[]{:S(2)}) %copy-start) | copy-done | bytes 393240
  2.4 0.9 %copy-done.1 = f32[2,128,128]{2,1,0:T(8,128)S(1)} copy-done((f32[2,128,128]{2,1,0:T(8,128)S(1)}, f32[2,128,128]{2,1,0:T(8,128)}, u32[]{:S(2)}) %copy-start.1) | copy-done | bytes 131096
  3.3 0.9 %copy-done.2 = bf16[384,128]{1,0:T(8,128)(2,1)S(1)} copy-done((bf16[384,128]{1,0:T(8,128)(2,1)S(1)}, bf16[384,128]{1,0:T(8,128)(2,1)}, u32[]{:S(2)}) %copy-start.2) | copy-done | bytes 98328
  4.2 0.8 %copy-done.3 = f32[2,64,128]{2,1,0:T(8,128)S(1)} copy-done((f32[2,64,128]{2,1,0:T(8,128)S(1)}, f32[2,64,128]{2,1,0:T(8,128)}, u32[]{:S(2)}) %copy-start.3) | copy-done | bytes 65560
  5.1 0.8 %copy-done.4 = f32[128,64]{1,0:T(8,128)S(1)} copy-done((f32[128,64]{1,0:T(8,128)S(1)}, f32[128,64]{1,0:T(8,128)}, u32[]{:S(2)}) %copy-start.4) | copy-done | bytes 32792
  5.9 0.8 %copy-done.5 = f32[48,256]{1,0:T(8,128)S(1)} copy-done((f32[48,256]{1,0:T(8,128)S(1)}, f32[48,256]{1,0:T(8,128)}, u32[]{:S(2)}) %copy-start.5) | copy-done | bytes 49176
  6.7 2.7 %whiten.1 = (bf16[16,512]{1,0:T(8,128)(2,1)S(1)}, bf16[16,512]{1,0:T(8,128)(2,1)S(1)}, bf16[16,512]{1,0:T(8,128)(2,1)S(1)}, bf16[16,512]{1,0:T(8,128)(2,1)S(1)}, bf16[16,128]{1,0:T(8,128)(2,1)S(1)}) custom-call(s32[2]{0:T(128)S(1)} %pad_add_fusion.scalars, f32[8,12288]{1,0:T(8,128)S(1)} %copy-done, s32[1,24]{1,0:T(1,128)S(1)} %copy-done.6, ...), custom_call_target="tpu_custom_call" | custom-call | tf_op jit(solution)/shard_map/whiten/pallas_call | solution.py:229
  9.4 0.5 %collective-permute-start = (bf16[16,512]{1,0:T(8,128)(2,1)S(1)}, bf16[16,512]{1,0:T(8,128)(2,1)S(1)}, u32[]{:S(2)}, u32[]{:S(2)}) collective-permute-start(bf16[16,512]{1,0:T(8,128)(2,1)S(1)} %get-tuple-element.11), channel_id=1, source_target_pairs={{0,1},{1,0},{2,3},{3,2},{4,5},{5,4},{6,7},{7,6},{8,9},{9,8},{10,11... | collective-permute-start | bytes 49160 | tf_op jit(solution)/shard_map/ppermute | solution.py:212
  9.9 2.6 %collective-permute-start.1 = (bf16[16,512]{1,0:T(8,128)(2,1)S(1)}, bf16[16,512]{1,0:T(8,128)(2,1)S(1)}, u32[]{:S(2)}, u32[]{:S(2)}) collective-permute-start(bf16[16,512]{1,0:T(8,128)(2,1)S(1)} %get-tuple-element.12), channel_id=1, source_target_pairs={{0,2},{1,3},{2,0},{3,1},{4,6},{5,7},{6,4},{7,5},{8,10},{9,11},{10,... | collective-permute-start | bytes 49160 | tf_op jit(solution)/shard_map/ppermute | solution.py:212
  12.5 1.6 %collective-permute-done.1 = bf16[16,512]{1,0:T(8,128)(2,1)S(1)} collective-permute-done((bf16[16,512]{1,0:T(8,128)(2,1)S(1)}, bf16[16,512]{1,0:T(8,128)(2,1)S(1)}, u32[]{:S(2)}, u32[]{:S(2)}) %collective-permute-start.1) | collective-permute-done | bytes 16416 | tf_op jit(solution)/shard_map/ppermute | solution.py:212
  14.2 1.4 %collective-permute-done.2 = bf16[16,512]{1,0:T(8,128)(2,1)S(1)} collective-permute-done((bf16[16,512]{1,0:T(8,128)(2,1)S(1)}, bf16[16,512]{1,0:T(8,128)(2,1)S(1)}, u32[]{:S(2)}, u32[]{:S(2)}) %collective-permute-start.2) | collective-permute-done | bytes 16416 | tf_op jit(solution)/shard_map/ppermute | solution.py:212
  15.6 3.6 %collective-permute-start.8 = (bf16[16,2176]{1,0:T(8,128)(2,1)S(1)}, bf16[16,2176]{1,0:T(8,128)(2,1)S(1)}, u32[]{:S(2)}, u32[]{:S(2)}) collective-permute-start(bf16[16,2176]{1,0:T(8,128)(2,1)S(1)} %constant_dynamic-update-slice_fusion.rest_0_), channel_id=1, source_target_pairs={{0,24},{4,28},{8,16},{12,20},{16,8},{20,12},{24,0},{28,4},{1,25},{... | collective-permute-start | bytes 208904 | tf_op jit(solution)/shard_map/ppermute | solution.py:212
  19.2 0.8 %collective-permute-start.4 = (bf16[16,2176]{1,0:T(8,128)(2,1)S(1)}, bf16[16,2176]{1,0:T(8,128)(2,1)S(1)}, u32[]{:S(2)}, u32[]{:S(2)}) collective-permute-start(bf16[16,2176]{1,0:T(8,128)(2,1)S(1)} %constant_dynamic-update-slice_fusion.rest_0_), channel_id=1, source_target_pairs={{0,8},{4,12},{8,0},{12,4},{16,24},{20,28},{24,16},{28,20},{1,9},{5... | collective-permute-start | bytes 208904 | tf_op jit(solution)/shard_map/ppermute | solution.py:212
  20.0 1.5 %collective-permute-start.3 = (bf16[16,2176]{1,0:T(8,128)(2,1)S(1)}, bf16[16,2176]{1,0:T(8,128)(2,1)S(1)}, u32[]{:S(2)}, u32[]{:S(2)}) collective-permute-start(bf16[16,2176]{1,0:T(8,128)(2,1)S(1)} %constant_dynamic-update-slice_fusion.rest_0_), channel_id=1, source_target_pairs={{0,4},{4,0},{8,12},{12,8},{16,20},{20,16},{24,28},{28,24},{1,5},{5... | collective-permute-start | bytes 208904 | tf_op jit(solution)/shard_map/ppermute | solution.py:212
  21.5 0.6 %collective-permute-done.8.rest_6_ = bf16[16,2176]{1,0:T(8,128)(2,1)S(1)} collective-permute-done((bf16[16,2176]{1,0:T(8,128)(2,1)S(1)}, bf16[16,2176]{1,0:T(8,128)(2,1)S(1)}, u32[]{:S(2)}, u32[]{:S(2)}) %collective-permute-start.8) | collective-permute-done | bytes 69664 | tf_op jit(solution)/shard_map/ppermute | solution.py:212
  22.1 1.5 %collective-permute-start.9 = (bf16[16,2176]{1,0:T(8,128)(2,1)S(1)}, bf16[16,2176]{1,0:T(8,128)(2,1)S(1)}, u32[]{:S(2)}, u32[]{:S(2)}) collective-permute-start(bf16[16,2176]{1,0:T(8,128)(2,1)S(1)} %collective-permute-done.8.rest_6_), channel_id=1, source_target_pairs={{0,4},{4,0},{8,12},{12,8},{16,20},{20,16},{24,28},{28,24},{1,5},{5... | collective-permute-start | bytes 208904 | tf_op jit(solution)/shard_map/ppermute | solution.py:212
  23.6 1.8 %collective-permute-done.6.rest_4_ = bf16[16,2176]{1,0:T(8,128)(2,1)S(1)} collective-permute-done((bf16[16,2176]{1,0:T(8,128)(2,1)S(1)}, bf16[16,2176]{1,0:T(8,128)(2,1)S(1)}, u32[]{:S(2)}, u32[]{:S(2)}) %collective-permute-start.6) | collective-permute-done | bytes 69664 | tf_op jit(solution)/shard_map/ppermute | solution.py:212
  25.4 1.5 %collective-permute-start.7 = (bf16[16,2176]{1,0:T(8,128)(2,1)S(1)}, bf16[16,2176]{1,0:T(8,128)(2,1)S(1)}, u32[]{:S(2)}, u32[]{:S(2)}) collective-permute-start(bf16[16,2176]{1,0:T(8,128)(2,1)S(1)} %collective-permute-done.6.rest_4_), channel_id=1, source_target_pairs={{0,4},{4,0},{8,12},{12,8},{16,20},{20,16},{24,28},{28,24},{1,5},{5... | collective-permute-start | bytes 208904 | tf_op jit(solution)/shard_map/ppermute | solution.py:212
  27.0 0.5 %collective-permute-start.5 = (bf16[16,2176]{1,0:T(8,128)(2,1)S(1)}, bf16[16,2176]{1,0:T(8,128)(2,1)S(1)}, u32[]{:S(2)}, u32[]{:S(2)}) collective-permute-start(bf16[16,2176]{1,0:T(8,128)(2,1)S(1)} %collective-permute-done.4.rest_2_), channel_id=1, source_target_pairs={{0,4},{4,0},{8,12},{12,8},{16,20},{20,16},{24,28},{28,24},{1,5},{5... | collective-permute-start | bytes 208904 | tf_op jit(solution)/shard_map/ppermute | solution.py:212
  27.5 2.8 %collective-permute-done.7.rest_5_ = bf16[16,2176]{1,0:T(8,128)(2,1)S(1)} collective-permute-done((bf16[16,2176]{1,0:T(8,128)(2,1)S(1)}, bf16[16,2176]{1,0:T(8,128)(2,1)S(1)}, u32[]{:S(2)}, u32[]{:S(2)}) %collective-permute-start.7) | collective-permute-done | bytes 69664 | tf_op jit(solution)/shard_map/ppermute | solution.py:212
  30.3 1.0 %collective-permute-done.5.rest_3_ = bf16[16,2176]{1,0:T(8,128)(2,1)S(1)} collective-permute-done((bf16[16,2176]{1,0:T(8,128)(2,1)S(1)}, bf16[16,2176]{1,0:T(8,128)(2,1)S(1)}, u32[]{:S(2)}, u32[]{:S(2)}) %collective-permute-start.5) | collective-permute-done | bytes 69664 | tf_op jit(solution)/shard_map/ppermute | solution.py:212
  31.3 1.4 %stack.9 = f32[384,128]{1,0:T(8,128)} custom-call(s32[1]{0:T(128)} %bitcast.scalars, bf16[16,2176]{1,0:T(8,128)(2,1)S(1)} %constant_dynamic-update-slice_fusion.rest_0_, bf16[16,2176]{1,0:T(8,128)(2,1)S(1)} %collective-permute-done.3.rest_1_, bf16[16,2176]{1,0:T(8,128)(2,1)S(1)} %collective-permute-done.4.rest_2_, ...), custom_call_target="tpu_custom_call" | custom-call | tf_op jit(solution)/shard_map/stack/pallas_call | solution.py:253
  (24 shorter events, 0.2 us)
Async XLA Ops:
  0.7 0.7 %copy-start.9 = (s32[24,1]{0,1:T(1,128)S(1)}, s32[24,1]{0,1:T(1,128)}, u32[]{:S(2)}) copy-start(s32[24,1]{0,1:T(1,128)} %param.16) | copy-start | bytes 292
  0.7 0.7 %copy-start.6 = (s32[1,24]{1,0:T(1,128)S(1)}, s32[1,24]{1,0:T(1,128)}, u32[]{:S(2)}) copy-start(s32[1,24]{1,0:T(1,128)} %source.1) | copy-start | bytes 292
  0.7 0.7 %copy-start.7 = (s32[1,24]{1,0:T(1,128)S(1)}, s32[1,24]{1,0:T(1,128)}, u32[]{:S(2)}) copy-start(s32[1,24]{1,0:T(1,128)} %receiver.1) | copy-start | bytes 292
  0.7 0.7 %copy-start.8 = (s32[1,24]{1,0:T(1,128)S(1)}, s32[1,24]{1,0:T(1,128)}, u32[]{:S(2)}) copy-start(s32[1,24]{1,0:T(1,128)} %hop.1) | copy-start | bytes 292
  1.4 1.0 %copy-start = (f32[8,12288]{1,0:T(8,128)S(1)}, f32[8,12288]{1,0:T(8,128)}, u32[]{:S(2)}) copy-start(f32[8,12288]{1,0:T(8,128)} %traces.1) | copy-start | bytes 1179652
  2.4 0.9 %copy-start.1 = (f32[2,128,128]{2,1,0:T(8,128)S(1)}, f32[2,128,128]{2,1,0:T(8,128)}, u32[]{:S(2)}) copy-start(f32[2,128,128]{2,1,0:T(8,128)} %constant.20.clone.twist) | copy-start | bytes 393220
  3.3 0.9 %copy-start.2 = (bf16[384,128]{1,0:T(8,128)(2,1)S(1)}, bf16[384,128]{1,0:T(8,128)(2,1)}, u32[]{:S(2)}) copy-start(bf16[384,128]{1,0:T(8,128)(2,1)} %constant.23.clone.band) | copy-start | bytes 294916
  4.2 0.8 %copy-start.3 = (f32[2,64,128]{2,1,0:T(8,128)S(1)}, f32[2,64,128]{2,1,0:T(8,128)}, u32[]{:S(2)}) copy-start(f32[2,64,128]{2,1,0:T(8,128)} %constant.22.clone.wave) | copy-start | bytes 196612
  5.1 0.8 %copy-start.4 = (f32[128,64]{1,0:T(8,128)S(1)}, f32[128,64]{1,0:T(8,128)}, u32[]{:S(2)}) copy-start(f32[128,64]{1,0:T(8,128)} %constant.19.clone.first) | copy-start | bytes 98308
  5.9 0.8 %copy-start.5 = (f32[48,256]{1,0:T(8,128)S(1)}, f32[48,256]{1,0:T(8,128)}, u32[]{:S(2)}) copy-start(f32[48,256]{1,0:T(8,128)} %constant.21.clone.second) | copy-start | bytes 147460
  9.4 3.2 %collective-permute-start = (bf16[16,512]{1,0:T(8,128)(2,1)S(1)}, bf16[16,512]{1,0:T(8,128)(2,1)S(1)}, u32[]{:S(2)}, u32[]{:S(2)}) collective-permute-start(bf16[16,512]{1,0:T(8,128)(2,1)S(1)} %get-tuple-element.11), channel_id=1, source_target_pairs={{0,1},{1,0},{2,3},{3,2},{4,5},{5,4},{6,7},{7,6},{8,9},{9,8},{10,11... | collective-permute-start | bytes 49160 | tf_op jit(solution)/shard_map/ppermute | solution.py:212
  9.9 4.3 %collective-permute-start.1 = (bf16[16,512]{1,0:T(8,128)(2,1)S(1)}, bf16[16,512]{1,0:T(8,128)(2,1)S(1)}, u32[]{:S(2)}, u32[]{:S(2)}) collective-permute-start(bf16[16,512]{1,0:T(8,128)(2,1)S(1)} %get-tuple-element.12), channel_id=1, source_target_pairs={{0,2},{1,3},{2,0},{3,1},{4,6},{5,7},{6,4},{7,5},{8,10},{9,11},{10,... | collective-permute-start | bytes 49160 | tf_op jit(solution)/shard_map/ppermute | solution.py:212
  12.5 3.2 %collective-permute-start.2 = (bf16[16,512]{1,0:T(8,128)(2,1)S(1)}, bf16[16,512]{1,0:T(8,128)(2,1)S(1)}, u32[]{:S(2)}, u32[]{:S(2)}) collective-permute-start(bf16[16,512]{1,0:T(8,128)(2,1)S(1)} %get-tuple-element.13), channel_id=1, source_target_pairs={{0,3},{1,2},{2,1},{3,0},{4,7},{5,6},{6,5},{7,4},{8,11},{9,10},{10,... | collective-permute-start | bytes 49160 | tf_op jit(solution)/shard_map/ppermute | solution.py:212
  15.6 6.5 %collective-permute-start.8 = (bf16[16,2176]{1,0:T(8,128)(2,1)S(1)}, bf16[16,2176]{1,0:T(8,128)(2,1)S(1)}, u32[]{:S(2)}, u32[]{:S(2)}) collective-permute-start(bf16[16,2176]{1,0:T(8,128)(2,1)S(1)} %constant_dynamic-update-slice_fusion.rest_0_), channel_id=1, source_target_pairs={{0,24},{4,28},{8,16},{12,20},{16,8},{20,12},{24,0},{28,4},{1,25},{... | collective-permute-start | bytes 208904 | tf_op jit(solution)/shard_map/ppermute | solution.py:212
  19.2 6.2 %collective-permute-start.6 = (bf16[16,2176]{1,0:T(8,128)(2,1)S(1)}, bf16[16,2176]{1,0:T(8,128)(2,1)S(1)}, u32[]{:S(2)}, u32[]{:S(2)}) collective-permute-start(bf16[16,2176]{1,0:T(8,128)(2,1)S(1)} %constant_dynamic-update-slice_fusion.rest_0_), channel_id=1, source_target_pairs={{0,16},{4,20},{8,24},{12,28},{16,0},{20,4},{24,8},{28,12},{1,17},{... | collective-permute-start | bytes 208904 | tf_op jit(solution)/shard_map/ppermute | solution.py:212
  19.2 7.7 %collective-permute-start.4 = (bf16[16,2176]{1,0:T(8,128)(2,1)S(1)}, bf16[16,2176]{1,0:T(8,128)(2,1)S(1)}, u32[]{:S(2)}, u32[]{:S(2)}) collective-permute-start(bf16[16,2176]{1,0:T(8,128)(2,1)S(1)} %constant_dynamic-update-slice_fusion.rest_0_), channel_id=1, source_target_pairs={{0,8},{4,12},{8,0},{12,4},{16,24},{20,28},{24,16},{28,20},{1,9},{5... | collective-permute-start | bytes 208904 | tf_op jit(solution)/shard_map/ppermute | solution.py:212
  20.0 7.4 %collective-permute-start.3 = (bf16[16,2176]{1,0:T(8,128)(2,1)S(1)}, bf16[16,2176]{1,0:T(8,128)(2,1)S(1)}, u32[]{:S(2)}, u32[]{:S(2)}) collective-permute-start(bf16[16,2176]{1,0:T(8,128)(2,1)S(1)} %constant_dynamic-update-slice_fusion.rest_0_), channel_id=1, source_target_pairs={{0,4},{4,0},{8,12},{12,8},{16,20},{20,16},{24,28},{28,24},{1,5},{5... | collective-permute-start | bytes 208904 | tf_op jit(solution)/shard_map/ppermute | solution.py:212
  22.1 5.4 %collective-permute-start.9 = (bf16[16,2176]{1,0:T(8,128)(2,1)S(1)}, bf16[16,2176]{1,0:T(8,128)(2,1)S(1)}, u32[]{:S(2)}, u32[]{:S(2)}) collective-permute-start(bf16[16,2176]{1,0:T(8,128)(2,1)S(1)} %collective-permute-done.8.rest_6_), channel_id=1, source_target_pairs={{0,4},{4,0},{8,12},{12,8},{16,20},{20,16},{24,28},{28,24},{1,5},{5... | collective-permute-start | bytes 208904 | tf_op jit(solution)/shard_map/ppermute | solution.py:212
  25.4 4.9 %collective-permute-start.7 = (bf16[16,2176]{1,0:T(8,128)(2,1)S(1)}, bf16[16,2176]{1,0:T(8,128)(2,1)S(1)}, u32[]{:S(2)}, u32[]{:S(2)}) collective-permute-start(bf16[16,2176]{1,0:T(8,128)(2,1)S(1)} %collective-permute-done.6.rest_4_), channel_id=1, source_target_pairs={{0,4},{4,0},{8,12},{12,8},{16,20},{20,16},{24,28},{28,24},{1,5},{5... | collective-permute-start | bytes 208904 | tf_op jit(solution)/shard_map/ppermute | solution.py:212
  27.0 4.3 %collective-permute-start.5 = (bf16[16,2176]{1,0:T(8,128)(2,1)S(1)}, bf16[16,2176]{1,0:T(8,128)(2,1)S(1)}, u32[]{:S(2)}, u32[]{:S(2)}) collective-permute-start(bf16[16,2176]{1,0:T(8,128)(2,1)S(1)} %collective-permute-done.4.rest_2_), channel_id=1, source_target_pairs={{0,4},{4,0},{8,12},{12,8},{16,20},{20,16},{24,28},{28,24},{1,5},{5... | collective-permute-start | bytes 208904 | tf_op jit(solution)/shard_map/ppermute | solution.py:212

commit v2 on v1

--- a/solution.py
+++ b/solution.py
@@ -18,7 +18,7 @@
 GRID_ROWS = 24
 F32 = jnp.float32
 BF16 = jnp.bfloat16
-HIGHEST = lax.Precision.HIGHEST
+LIMIT = 55000 << 10
 
 
 def tables():
@@ -26,27 +26,15 @@
     high = np.arange(HIGH)
     first = 2 * np.pi / HIGH * (np.outer(np.arange(HIGH) + SMOOTH_HALF, high) % HIGH)
     first = np.concatenate([np.cos(first), -np.sin(first)], axis=0)
+    first = np.concatenate([first, first], axis=1)
     twist = 2 * np.pi / NT * (np.outer(lane + SMOOTH_HALF, lane) % NT)
-    twist = np.stack([np.cos(twist), -np.sin(twist)])
     grid_row = np.arange(GRID_ROWS) - 1
     second = 2 * np.pi / HIGH * (np.outer(grid_row, lane) % HIGH)
-    cos, sin = np.cos(second), -np.sin(second)
     live = (np.arange(GRID_ROWS) < ROWS + 2)[:, None]
-    cos, sin = cos * live, sin * live
-    second = np.concatenate(
-        [np.concatenate([cos, -sin], axis=1), np.concatenate([sin, cos], axis=1)], axis=0
-    )
+    cos, sin = np.cos(second) * live, -np.sin(second) * live
     phase = 2 * np.pi / NT * np.arange(NT).reshape(HIGH, LANES)
-    wave = np.stack([np.cos(phase), np.sin(phase)])
-    source = np.arange(3 * LANES)[:, None] - LANES
-    band = np.abs(source - lane[None, :]) <= SMOOTH_HALF
-    return (
-        first.astype(np.float32),
-        twist.astype(np.float32),
-        second.astype(np.float32),
-        wave.astype(np.float32),
-        band.astype(jnp.bfloat16),
-    )
+    rows = [np.cos(phase), np.sin(phase), first, np.cos(twist), -np.sin(twist), cos, sin]
+    return np.concatenate(rows, axis=0).astype(np.float32)
 
 
 def split(value):
@@ -54,50 +42,89 @@
     return top, (value - top.astype(F32)).astype(BF16)
 
 
-def whiten_kernel(
-    scalars, traces, source, receiver, hop, owner, first, twist, second, wave, band, *rest
-):
-    outs, (centred, grid_real, grid_imag, white) = rest[:-4], rest[-4:]
-    windows = len(outs) - 1
+def whiten_kernel(place_ref, traces_far, offsets_far, table_far, *rest):
+    outs = rest[:-9]
+    traces, offsets, table, arrived, held, means, grid_real, grid_imag, white = rest[-9:]
+    copies = [
+        pltpu.make_async_copy(offsets_far, offsets, arrived.at[0]),
+        pltpu.make_async_copy(traces_far, traces, arrived.at[1]),
+        pltpu.make_async_copy(table_far, table, arrived.at[2]),
+    ]
+    for copy in copies:
+        copy.start()
+    windows = len(outs)
     channels = traces.shape[0]
-    offset, me = scalars[0], scalars[1]
-
+
+    spot = lax.broadcasted_iota(jnp.int32, (3 * LANES, LANES), 0) - LANES
+    spot = spot - lax.broadcasted_iota(jnp.int32, (3 * LANES, LANES), 1)
+    band = jnp.where(jnp.abs(spot) <= SMOOTH_HALF, 1.0, 0.0).astype(BF16)
+
+    copies[0].wait()
+    offset, me = offsets[0], place_ref[0]
+    copies[2].wait()
+    place = lax.broadcasted_iota(jnp.int32, (1, LANES), 1) == offset % LANES
+    turn = offset // LANES
+    cos_off = jnp.sum(
+        jnp.where(place, table[pl.ds(turn, 1), :], 0.0), axis=1, keepdims=True
+    )
+    sin_off = jnp.sum(
+        jnp.where(place, table[pl.ds(HIGH + turn, 1), :], 0.0), axis=1, keepdims=True
+    )
+    taper = 0.5 - 0.5 * (table[:HIGH, :] * cos_off + table[HIGH : 2 * HIGH, :] * sin_off)
+    at = 2 * HIGH
+    first = split(table[at : at + 2 * HIGH, :HIGH])
+    first = jnp.concatenate([first[0], first[0], first[1]], axis=1)
+    at += 2 * HIGH
+    twist_cos, twist_sin = table[at : at + LANES, :], table[at + LANES : at + 2 * LANES, :]
+    at += 2 * LANES
+    cos, sin = table[at : at + GRID_ROWS, :], table[at + GRID_ROWS : at + 2 * GRID_ROWS, :]
+    second = split(
+        jnp.concatenate(
+            [jnp.concatenate([cos, -sin], axis=1), jnp.concatenate([sin, cos], axis=1)], axis=0
+        )
+    )
+    second = jnp.concatenate([second[0], second[0], second[1]], axis=1)
+
+    copies[1].wait()
     lane = lax.broadcasted_iota(jnp.int32, (channels, LANES), 1)
-    total = jnp.zeros((channels, LANES), F32)
-    blocks = []
+    totals = [jnp.zeros((channels, LANES), F32) for _ in range(4)]
     spare = traces.shape[1] // LANES - HIGH
     for i in range(HIGH):
         piece = traces[:, i * LANES : (i + 1) * LANES]
         if i < spare:
             later = traces[:, (i + HIGH) * LANES : (i + HIGH + 1) * LANES]
             piece = jnp.where(lane + i * LANES >= offset, piece, later)
-        centred[i * channels : (i + 1) * channels, :] = piece
-        total = total + piece
+        held[i * channels : (i + 1) * channels, :] = piece
+        totals[i % 4] = totals[i % 4] + piece
+    total = (totals[0] + totals[1]) + (totals[2] + totals[3])
     mean = jnp.sum(total, axis=1, keepdims=True) * (1.0 / NT)
-    centred[...] = centred[...] - jnp.tile(mean, (HIGH, 1))
-
-    angle = jnp.full((8, LANES), offset, jnp.int32).astype(F32) * (2.0 * math.pi / NT)
-    cos_off = jnp.cos(angle)[0:1, :]
-    sin_off = jnp.sin(angle)[0:1, :]
-    taper = 0.5 - 0.5 * (wave[0] * cos_off + wave[1] * sin_off)
+    means[...] = jnp.broadcast_to(mean, (channels, LANES))
     segment = jnp.concatenate(
-        [centred[pl.ds(c, HIGH, stride=channels), :] * taper for c in range(channels)], axis=1
-    )
-    inner = jnp.dot(first[...], segment, precision=HIGHEST, preferred_element_type=F32)
-    twist_cos, twist_sin = twist[0], twist[1]
+        [
+            (held[pl.ds(c, HIGH, stride=channels), :] - means[c : c + 1, :]) * taper
+            for c in range(channels)
+        ],
+        axis=1,
+    )
+    top, low = split(segment)
+    inner = jnp.dot(
+        first, jnp.concatenate([top, low, top], axis=0), preferred_element_type=F32
+    )
     for c in range(channels):
         real = inner[:HIGH, c * LANES : (c + 1) * LANES]
         imag = inner[HIGH:, c * LANES : (c + 1) * LANES]
         real = jnp.concatenate([real, real], axis=0)
         imag = jnp.concatenate([imag, imag], axis=0)
-        mixed = jnp.concatenate(
-            [real * twist_cos - imag * twist_sin, real * twist_sin + imag * twist_cos], axis=1
+        top, low = split(
+            jnp.concatenate(
+                [real * twist_cos - imag * twist_sin, real * twist_sin + imag * twist_cos],
+                axis=1,
+            )
         )
         bins = lax.dot_general(
-            second[...],
-            mixed,
+            second,
+            jnp.concatenate([top, low, top], axis=1),
             (((1,), (1,)), ((), ())),
-            precision=HIGHEST,
             preferred_element_type=F32,
         )
         grid_real[pl.ds(c, GRID_ROWS, stride=channels), :] = bins[:GRID_ROWS]
@@ -106,17 +133,14 @@
     live = (ROWS + 2) * channels
     real, imag = grid_real[:live, :], grid_imag[:live, :]
     power = (real * real + imag * imag) * (1.0 / (2 * SMOOTH_HALF + 1))
-    place = lax.broadcasted_iota(jnp.int32, (channels, LANES), 1)
-    head = jnp.where(place >= LANES - SMOOTH_HALF, power[:channels], 0.0)
-    tail = jnp.where(place < SMOOTH_HALF, power[live - channels :], 0.0)
+    head = jnp.where(lane >= LANES - SMOOTH_HALF, power[:channels], 0.0)
+    tail = jnp.where(lane < SMOOTH_HALF, power[live - channels :], 0.0)
     power = jnp.concatenate([head, power[channels : live - channels], tail], axis=0)
-    top, low = split(power)
     count = ROWS * channels
-    around = [
-        piece[i * channels : i * channels + count] for piece in (top, low) for i in range(3)
-    ]
-    level = jnp.dot(jnp.concatenate(around[:3], axis=1), band[...], preferred_element_type=F32)
-    level += jnp.dot(jnp.concatenate(around[3:], axis=1), band[...], preferred_element_type=F32)
+    level = jnp.zeros((count, LANES), F32)
+    for part in split(power):
+        around = [part[i * channels : i * channels + count] for i in range(3)]
+        level += jnp.dot(jnp.concatenate(around, axis=1), band, preferred_element_type=F32)
     scale = lax.rsqrt(level + 1e-06)
     kept_real = real[channels : channels + count] * scale
     kept_imag = imag[channels : channels + count] * scale
@@ -127,13 +151,6 @@
         white[i // part, :, (i % part) * LANES : (i % part + 1) * LANES] = tile
     for k in range(windows):
         outs[k][...] = white[me ^ k]
-    fields = [f[...].astype(F32) for f in (source, receiver, hop, owner)]
-    fields.append(jnp.zeros((2 * channels - 4, fields[0].shape[1]), F32))
-    fields = jnp.concatenate(fields, axis=0)
-    fields = jnp.concatenate(
-        [fields, jnp.zeros((2 * channels, LANES - fields.shape[1]), F32)], axis=1
-    )
-    outs[windows][...] = fields.astype(BF16)
 
 
 def stack_kernel(blocks, windows, capacity, reach, pair_slots, scalars, *rest):
@@ -224,30 +241,39 @@
     smem = pl.BlockSpec(memory_space=pltpu.SMEM)
     height = 2 * channels
 
-    scalars = jnp.stack([offsets[0], lax.axis_index("win").astype(jnp.int32)])
-    constants = [jnp.asarray(t) for t in tables()]
+    table = jnp.asarray(tables())
     pieces = pl.pallas_call(
         whiten_kernel,
-        out_shape=[jax.ShapeDtypeStruct((height, width), BF16)] * windows
-        + [jax.ShapeDtypeStruct((height, LANES), BF16)],
-        in_specs=[smem] + [vmem] * 10,
-        out_specs=[vmem] * (windows + 1),
+        out_shape=[jax.ShapeDtypeStruct((height, width), BF16)] * windows,
+        in_specs=[smem] + [pl.BlockSpec(memory_space=pltpu.HBM)] * 3,
+        out_specs=[vmem] * windows,
         scratch_shapes=[
+            pltpu.VMEM(traces.shape, F32),
+            pltpu.SMEM(offsets.shape, jnp.int32),
+            pltpu.VMEM(table.shape, F32),
+            pltpu.SemaphoreType.DMA((3,)),
             pltpu.VMEM((HIGH * channels, LANES), F32),
+            pltpu.VMEM((channels, LANES), F32),
             pltpu.VMEM((GRID_ROWS * channels, LANES), F32),
             pltpu.VMEM((GRID_ROWS * channels, LANES), F32),
             pltpu.VMEM((windows, height, width), BF16),
         ],
-        compiler_params=pltpu.CompilerParams(vmem_limit_bytes=32 << 20),
+        compiler_params=pltpu.CompilerParams(vmem_limit_bytes=LIMIT),
         name="whiten",
-    )(scalars, traces, pair_source, pair_recv, pair_hop, pair_owner.reshape(1, -1), *constants)
+    )(lax.axis_index("win").astype(jnp.int32).reshape(1), traces, offsets, table)
+    fields = [pair_source, pair_recv, pair_hop, pair_owner.reshape(1, -1)]
+    fields = jnp.concatenate(fields, axis=0).astype(BF16)
+    fields = jnp.pad(fields, ((0, height - 4), (0, LANES - pair_slots)))
     moved = [pieces[0]] + [swapped(pieces[k], "win", k) for k in range(1, windows)]
-    packed = jnp.concatenate(moved + [pieces[windows]], axis=1)
+    packed = jnp.concatenate(moved + [fields], axis=1)
 
     gathered = {0: packed}
-    for k in range(2, blocks, 2):
+    half = blocks // 2
+    for k in range(blocks - 2, half - 1, -2):
         gathered[k] = swapped(packed, "chan", k)
-    for k in range(0, blocks, 2):
+    for k in range(1, half):
+        gathered[k] = swapped(packed, "chan", k)
+    for k in range(blocks - 2, half - 1, -2):
         gathered[k + 1] = swapped(gathered[k], "chan", 1)
 
     stacked = pl.pallas_call(

time: 33 us -> 25.2 us (0.76)
  waiting for transfers between devices: 9.26 us -> 5.17 us
  local copies, waits for them, and re-layouts: 5.97 us -> 1.96 us
  starting transfers between devices: 12.6 us -> 13.3 us
    ppermute x10, waiting for transfers between devices: 9.26 us -> 5.17 us  [swapped(): return lax.ppermute(value, axis, [(i, i ^ bits) for i in range(peers)])]
    unnamed x24 -> x12, local copies, waits for them, and re-layouts: 5.96 us -> 1.96 us
    ppermute x10, starting transfers between devices: 12.6 us -> 13.3 us  [swapped(): return lax.ppermute(value, axis, [(i, i ^ bits) for i in range(peers)])]
  transfers between devices with their start and end apart: 10 -> 10, of which waited for: 6 -> 5; matrix products, arithmetic and copies ran while one was open for 0% -> 0% of each run, Pallas kernels for 0% -> 0%
where the time goes in v2:
time: 25.2 us; the launch traced here: 25 us
  starting transfers between devices  13.3 us (53%)
  waiting for transfers between devices  5.17 us (21%)
  Pallas kernels  3.83 us (15%)
  local copies, waits for them, and re-layouts  1.96 us (8%)
  between operations  0.7 us (3%)
    ppermute x10, starting transfers between devices, swapped(): return lax.ppermute(value, axis, [(i, i ^ bits) for i in range(peers)])  13.3 us
    ppermute x10, waiting for transfers between devices, swapped(): return lax.ppermute(value, axis, [(i, i ^ bits) for i in range(peers)])  5.17 us
    pallas_call x1, Pallas kernels, local(): pl.pallas_call(whiten_kernel, out_shape=[jax.ShapeDtypeStruct((height, wi...  2.44 us
    unnamed x12, local copies, waits for them, and re-layouts  1.96 us
    pallas_call x1, Pallas kernels, local(): pl.pallas_call(functools.partial(stack_kernel, blocks, windows, capacity,...  1.4 us
  transfers between devices with their start and end apart: 10, of which 5 were waited for; matrix products, arithmetic and copies ran while one was open for 0% of the time, Pallas kernels for 0%

profile of v2, /device:TPU:0, one launch (start us, length us, event | category | flops | bytes accessed | tf_op | source)
XLA Modules:
  0.0 25.0 jit_solution(10206906744410192947)
XLA Ops:
  0.7 2.4 %whiten.1 = (bf16[16,512]{1,0:T(8,128)(2,1)S(1)}, bf16[16,512]{1,0:T(8,128)(2,1)S(1)}, bf16[16,512]{1,0:T(8,128)(2,1)S(1)}, bf16[16,512]{1,0:T(8,128)(2,1)S(1)}) custom-call(s32[1]{0:T(128)} %bitcast.1.place_ref, f32[8,12288]{1,0:T(8,128)} %traces_far.1, s32[1]{0:T(128)S(6)} %copy.13.offsets_far, f32[560,128]{1,0:T(8,128)} %constant.14.clone.table_far), custom_call_target="tpu_custom_call" | custom-call | tf_op jit(solution)/shard_map/whiten/pallas_call | solution.py:245
  3.1 0.5 %collective-permute-start = (bf16[16,512]{1,0:T(8,128)(2,1)S(1)}, bf16[16,512]{1,0:T(8,128)(2,1)S(1)}, u32[]{:S(2)}, u32[]{:S(2)}) collective-permute-start(bf16[16,512]{1,0:T(8,128)(2,1)S(1)} %get-tuple-element.10), channel_id=1, source_target_pairs={{0,1},{1,0},{2,3},{3,2},{4,5},{5,4},{6,7},{7,6},{8,9},{9,8},{10,11... | collective-permute-start | bytes 49160 | tf_op jit(solution)/shard_map/ppermute | solution.py:229
  3.6 2.6 %collective-permute-start.1 = (bf16[16,512]{1,0:T(8,128)(2,1)S(1)}, bf16[16,512]{1,0:T(8,128)(2,1)S(1)}, u32[]{:S(2)}, u32[]{:S(2)}) collective-permute-start(bf16[16,512]{1,0:T(8,128)(2,1)S(1)} %get-tuple-element.11), channel_id=1, source_target_pairs={{0,2},{1,3},{2,0},{3,1},{4,6},{5,7},{6,4},{7,5},{8,10},{9,11},{10,... | collective-permute-start | bytes 49160 | tf_op jit(solution)/shard_map/ppermute | solution.py:229
  6.2 0.1 collective-permute-start.2
  6.3 0.6 %copy-done.1 = s32[1,24]{1,0:T(1,128)S(1)} copy-done((s32[1,24]{1,0:T(1,128)S(1)}, s32[1,24]{1,0:T(1,128)}, u32[]{:S(2)}) %copy-start.1) | copy-done | bytes 120
  6.9 0.6 %copy-done.2 = s32[1,24]{1,0:T(1,128)S(1)} copy-done((s32[1,24]{1,0:T(1,128)S(1)}, s32[1,24]{1,0:T(1,128)}, u32[]{:S(2)}) %copy-start.2) | copy-done | bytes 120
  7.6 0.6 %copy-done.3 = s32[1,24]{1,0:T(1,128)S(1)} copy-done((s32[1,24]{1,0:T(1,128)S(1)}, s32[1,24]{1,0:T(1,128)}, u32[]{:S(2)}) %copy-start.3) | copy-done | bytes 120
  8.2 0.0 collective-permute-done
  8.2 0.0 collective-permute-done.1
  8.3 1.1 %collective-permute-done.2 = bf16[16,512]{1,0:T(8,128)(2,1)S(1)} collective-permute-done((bf16[16,512]{1,0:T(8,128)(2,1)S(1)}, bf16[16,512]{1,0:T(8,128)(2,1)S(1)}, u32[]{:S(2)}, u32[]{:S(2)}) %collective-permute-start.2) | collective-permute-done | bytes 16416 | tf_op jit(solution)/shard_map/ppermute | solution.py:229
  9.4 3.7 %collective-permute-start.8 = (bf16[16,2176]{1,0:T(8,128)(2,1)S(1)}, bf16[16,2176]{1,0:T(8,128)(2,1)S(1)}, u32[]{:S(2)}, u32[]{:S(2)}) collective-permute-start(bf16[16,2176]{1,0:T(8,128)(2,1)S(1)} %constant_dynamic-update-slice_fusion.rest_0_), channel_id=1, source_target_pairs={{0,24},{4,28},{8,16},{12,20},{16,8},{20,12},{24,0},{28,4},{1,25},{... | collective-permute-start | bytes 208904 | tf_op jit(solution)/shard_map/ppermute | solution.py:229
  13.0 0.0 collective-permute-start.6
  13.0 1.7 %collective-permute-start.5 = (bf16[16,2176]{1,0:T(8,128)(2,1)S(1)}, bf16[16,2176]{1,0:T(8,128)(2,1)S(1)}, u32[]{:S(2)}, u32[]{:S(2)}) collective-permute-start(bf16[16,2176]{1,0:T(8,128)(2,1)S(1)} %constant_dynamic-update-slice_fusion.rest_0_), channel_id=1, source_target_pairs={{0,12},{4,8},{8,4},{12,0},{16,28},{20,24},{24,20},{28,16},{1,13},{... | collective-permute-start | bytes 208904 | tf_op jit(solution)/shard_map/ppermute | solution.py:229
  14.8 1.2 %collective-permute-start.4 = (bf16[16,2176]{1,0:T(8,128)(2,1)S(1)}, bf16[16,2176]{1,0:T(8,128)(2,1)S(1)}, u32[]{:S(2)}, u32[]{:S(2)}) collective-permute-start(bf16[16,2176]{1,0:T(8,128)(2,1)S(1)} %constant_dynamic-update-slice_fusion.rest_0_), channel_id=1, source_target_pairs={{0,8},{4,12},{8,0},{12,4},{16,24},{20,28},{24,16},{28,20},{1,9},{5... | collective-permute-start | bytes 208904 | tf_op jit(solution)/shard_map/ppermute | solution.py:229
  16.0 0.5 %collective-permute-start.3 = (bf16[16,2176]{1,0:T(8,128)(2,1)S(1)}, bf16[16,2176]{1,0:T(8,128)(2,1)S(1)}, u32[]{:S(2)}, u32[]{:S(2)}) collective-permute-start(bf16[16,2176]{1,0:T(8,128)(2,1)S(1)} %constant_dynamic-update-slice_fusion.rest_0_), channel_id=1, source_target_pairs={{0,4},{4,0},{8,12},{12,8},{16,20},{20,16},{24,28},{28,24},{1,5},{5... | collective-permute-start | bytes 208904 | tf_op jit(solution)/shard_map/ppermute | solution.py:229
  16.5 0.0 collective-permute-done.8.rest_6_
  16.5 1.5 %collective-permute-start.9 = (bf16[16,2176]{1,0:T(8,128)(2,1)S(1)}, bf16[16,2176]{1,0:T(8,128)(2,1)S(1)}, u32[]{:S(2)}, u32[]{:S(2)}) collective-permute-start(bf16[16,2176]{1,0:T(8,128)(2,1)S(1)} %collective-permute-done.8.rest_6_), channel_id=1, source_target_pairs={{0,4},{4,0},{8,12},{12,8},{16,20},{20,16},{24,28},{28,24},{1,5},{5... | collective-permute-start | bytes 208904 | tf_op jit(solution)/shard_map/ppermute | solution.py:229
  18.1 1.3 %collective-permute-done.6.rest_4_ = bf16[16,2176]{1,0:T(8,128)(2,1)S(1)} collective-permute-done((bf16[16,2176]{1,0:T(8,128)(2,1)S(1)}, bf16[16,2176]{1,0:T(8,128)(2,1)S(1)}, u32[]{:S(2)}, u32[]{:S(2)}) %collective-permute-start.6) | collective-permute-done | bytes 69664 | tf_op jit(solution)/shard_map/ppermute | solution.py:229
  19.3 1.5 %collective-permute-start.7 = (bf16[16,2176]{1,0:T(8,128)(2,1)S(1)}, bf16[16,2176]{1,0:T(8,128)(2,1)S(1)}, u32[]{:S(2)}, u32[]{:S(2)}) collective-permute-start(bf16[16,2176]{1,0:T(8,128)(2,1)S(1)} %collective-permute-done.6.rest_4_), channel_id=1, source_target_pairs={{0,4},{4,0},{8,12},{12,8},{16,20},{20,16},{24,28},{28,24},{1,5},{5... | collective-permute-start | bytes 208904 | tf_op jit(solution)/shard_map/ppermute | solution.py:229
  20.9 0.1 collective-permute-done.4.rest_2_
  20.9 0.0 collective-permute-done.3.rest_1_
  20.9 0.6 %collective-permute-done.9.rest_7_ = bf16[16,2176]{1,0:T(8,128)(2,1)S(1)} collective-permute-done((bf16[16,2176]{1,0:T(8,128)(2,1)S(1)}, bf16[16,2176]{1,0:T(8,128)(2,1)S(1)}, u32[]{:S(2)}, u32[]{:S(2)}) %collective-permute-start.9) | collective-permute-done | bytes 69664 | tf_op jit(solution)/shard_map/ppermute | solution.py:229
  21.5 2.2 %collective-permute-done.7.rest_5_ = bf16[16,2176]{1,0:T(8,128)(2,1)S(1)} collective-permute-done((bf16[16,2176]{1,0:T(8,128)(2,1)S(1)}, bf16[16,2176]{1,0:T(8,128)(2,1)S(1)}, u32[]{:S(2)}, u32[]{:S(2)}) %collective-permute-start.7) | collective-permute-done | bytes 69664 | tf_op jit(solution)/shard_map/ppermute | solution.py:229
  23.6 1.4 %stack.1 = f32[384,128]{1,0:T(8,128)} custom-call(s32[1]{0:T(128)} %bitcast.scalars, bf16[16,2176]{1,0:T(8,128)(2,1)S(1)} %constant_dynamic-update-slice_fusion.rest_0_, bf16[16,2176]{1,0:T(8,128)(2,1)S(1)} %collective-permute-done.3.rest_1_, bf16[16,2176]{1,0:T(8,128)(2,1)S(1)} %collective-permute-done.4.rest_2_, ...), custom_call_target="tpu_custom_call" | custom-call | tf_op jit(solution)/shard_map/stack/pallas_call | solution.py:279
  (15 shorter events, 0.1 us)
Async XLA Ops:
  3.1 5.1 %collective-permute-start = (bf16[16,512]{1,0:T(8,128)(2,1)S(1)}, bf16[16,512]{1,0:T(8,128)(2,1)S(1)}, u32[]{:S(2)}, u32[]{:S(2)}) collective-permute-start(bf16[16,512]{1,0:T(8,128)(2,1)S(1)} %get-tuple-element.10), channel_id=1, source_target_pairs={{0,1},{1,0},{2,3},{3,2},{4,5},{5,4},{6,7},{7,6},{8,9},{9,8},{10,11... | collective-permute-start | bytes 49160 | tf_op jit(solution)/shard_map/ppermute | solution.py:229
  3.6 2.6 %copy-start = (s32[24,1]{0,1:T(1,128)S(1)}, s32[24,1]{0,1:T(1,128)}, u32[]{:S(2)}) copy-start(s32[24,1]{0,1:T(1,128)} %param.12) | copy-start | bytes 292
  3.6 4.6 %collective-permute-start.1 = (bf16[16,512]{1,0:T(8,128)(2,1)S(1)}, bf16[16,512]{1,0:T(8,128)(2,1)S(1)}, u32[]{:S(2)}, u32[]{:S(2)}) collective-permute-start(bf16[16,512]{1,0:T(8,128)(2,1)S(1)} %get-tuple-element.11), channel_id=1, source_target_pairs={{0,2},{1,3},{2,0},{3,1},{4,6},{5,7},{6,4},{7,5},{8,10},{9,11},{10,... | collective-permute-start | bytes 49160 | tf_op jit(solution)/shard_map/ppermute | solution.py:229
  6.2 3.2 %collective-permute-start.2 = (bf16[16,512]{1,0:T(8,128)(2,1)S(1)}, bf16[16,512]{1,0:T(8,128)(2,1)S(1)}, u32[]{:S(2)}, u32[]{:S(2)}) collective-permute-start(bf16[16,512]{1,0:T(8,128)(2,1)S(1)} %get-tuple-element.12), channel_id=1, source_target_pairs={{0,3},{1,2},{2,1},{3,0},{4,7},{5,6},{6,5},{7,4},{8,11},{9,10},{10,... | collective-permute-start | bytes 49160 | tf_op jit(solution)/shard_map/ppermute | solution.py:229
  6.3 0.7 %copy-start.1 = (s32[1,24]{1,0:T(1,128)S(1)}, s32[1,24]{1,0:T(1,128)}, u32[]{:S(2)}) copy-start(s32[1,24]{1,0:T(1,128)} %param.9) | copy-start | bytes 292
  6.9 0.7 %copy-start.2 = (s32[1,24]{1,0:T(1,128)S(1)}, s32[1,24]{1,0:T(1,128)}, u32[]{:S(2)}) copy-start(s32[1,24]{1,0:T(1,128)} %param.10) | copy-start | bytes 292
  7.6 0.7 %copy-start.3 = (s32[1,24]{1,0:T(1,128)S(1)}, s32[1,24]{1,0:T(1,128)}, u32[]{:S(2)}) copy-start(s32[1,24]{1,0:T(1,128)} %param.11) | copy-start | bytes 292
  9.4 7.2 %collective-permute-start.8 = (bf16[16,2176]{1,0:T(8,128)(2,1)S(1)}, bf16[16,2176]{1,0:T(8,128)(2,1)S(1)}, u32[]{:S(2)}, u32[]{:S(2)}) collective-permute-start(bf16[16,2176]{1,0:T(8,128)(2,1)S(1)} %constant_dynamic-update-slice_fusion.rest_0_), channel_id=1, source_target_pairs={{0,24},{4,28},{8,16},{12,20},{16,8},{20,12},{24,0},{28,4},{1,25},{... | collective-permute-start | bytes 208904 | tf_op jit(solution)/shard_map/ppermute | solution.py:229
  13.0 6.3 %collective-permute-start.6 = (bf16[16,2176]{1,0:T(8,128)(2,1)S(1)}, bf16[16,2176]{1,0:T(8,128)(2,1)S(1)}, u32[]{:S(2)}, u32[]{:S(2)}) collective-permute-start(bf16[16,2176]{1,0:T(8,128)(2,1)S(1)} %constant_dynamic-update-slice_fusion.rest_0_), channel_id=1, source_target_pairs={{0,16},{4,20},{8,24},{12,28},{16,0},{20,4},{24,8},{28,12},{1,17},{... | collective-permute-start | bytes 208904 | tf_op jit(solution)/shard_map/ppermute | solution.py:229
  13.0 7.8 %collective-permute-start.5 = (bf16[16,2176]{1,0:T(8,128)(2,1)S(1)}, bf16[16,2176]{1,0:T(8,128)(2,1)S(1)}, u32[]{:S(2)}, u32[]{:S(2)}) collective-permute-start(bf16[16,2176]{1,0:T(8,128)(2,1)S(1)} %constant_dynamic-update-slice_fusion.rest_0_), channel_id=1, source_target_pairs={{0,12},{4,8},{8,4},{12,0},{16,28},{20,24},{24,20},{28,16},{1,13},{... | collective-permute-start | bytes 208904 | tf_op jit(solution)/shard_map/ppermute | solution.py:229
  14.8 6.1 %collective-permute-start.4 = (bf16[16,2176]{1,0:T(8,128)(2,1)S(1)}, bf16[16,2176]{1,0:T(8,128)(2,1)S(1)}, u32[]{:S(2)}, u32[]{:S(2)}) collective-permute-start(bf16[16,2176]{1,0:T(8,128)(2,1)S(1)} %constant_dynamic-update-slice_fusion.rest_0_), channel_id=1, source_target_pairs={{0,8},{4,12},{8,0},{12,4},{16,24},{20,28},{24,16},{28,20},{1,9},{5... | collective-permute-start | bytes 208904 | tf_op jit(solution)/shard_map/ppermute | solution.py:229
  16.0 4.9 %collective-permute-start.3 = (bf16[16,2176]{1,0:T(8,128)(2,1)S(1)}, bf16[16,2176]{1,0:T(8,128)(2,1)S(1)}, u32[]{:S(2)}, u32[]{:S(2)}) collective-permute-start(bf16[16,2176]{1,0:T(8,128)(2,1)S(1)} %constant_dynamic-update-slice_fusion.rest_0_), channel_id=1, source_target_pairs={{0,4},{4,0},{8,12},{12,8},{16,20},{20,16},{24,28},{28,24},{1,5},{5... | collective-permute-start | bytes 208904 | tf_op jit(solution)/shard_map/ppermute | solution.py:229
  16.5 5.0 %collective-permute-start.9 = (bf16[16,2176]{1,0:T(8,128)(2,1)S(1)}, bf16[16,2176]{1,0:T(8,128)(2,1)S(1)}, u32[]{:S(2)}, u32[]{:S(2)}) collective-permute-start(bf16[16,2176]{1,0:T(8,128)(2,1)S(1)} %collective-permute-done.8.rest_6_), channel_id=1, source_target_pairs={{0,4},{4,0},{8,12},{12,8},{16,20},{20,16},{24,28},{28,24},{1,5},{5... | collective-permute-start | bytes 208904 | tf_op jit(solution)/shard_map/ppermute | solution.py:229
  19.3 4.3 %collective-permute-start.7 = (bf16[16,2176]{1,0:T(8,128)(2,1)S(1)}, bf16[16,2176]{1,0:T(8,128)(2,1)S(1)}, u32[]{:S(2)}, u32[]{:S(2)}) collective-permute-start(bf16[16,2176]{1,0:T(8,128)(2,1)S(1)} %collective-permute-done.6.rest_4_), channel_id=1, source_target_pairs={{0,4},{4,0},{8,12},{12,8},{16,20},{20,16},{24,28},{28,24},{1,5},{5... | collective-permute-start | bytes 208904 | tf_op jit(solution)/shard_map/ppermute | solution.py:229

commit v3 on v2

--- a/solution.py
+++ b/solution.py
@@ -27,10 +27,11 @@
     first = 2 * np.pi / HIGH * (np.outer(np.arange(HIGH) + SMOOTH_HALF, high) % HIGH)
     first = np.concatenate([np.cos(first), -np.sin(first)], axis=0)
     first = np.concatenate([first, first], axis=1)
-    twist = 2 * np.pi / NT * (np.outer(lane + SMOOTH_HALF, lane) % NT)
-    grid_row = np.arange(GRID_ROWS) - 1
-    second = 2 * np.pi / HIGH * (np.outer(grid_row, lane) % HIGH)
-    live = (np.arange(GRID_ROWS) < ROWS + 2)[:, None]
+    twist = 2 * np.pi / NT * (np.outer(high + SMOOTH_HALF, lane) % NT)
+    half_row = 2 * (np.arange(GRID_ROWS) - 1)
+    half_row = np.concatenate([half_row, half_row + 1])
+    second = 2 * np.pi / LANES * (np.outer(half_row, lane) % LANES)
+    live = np.tile(np.arange(GRID_ROWS) < ROWS + 2, 2)[:, None]
     cos, sin = np.cos(second) * live, -np.sin(second) * live
     phase = 2 * np.pi / NT * np.arange(NT).reshape(HIGH, LANES)
     rows = [np.cos(phase), np.sin(phase), first, np.cos(twist), -np.sin(twist), cos, sin]
@@ -75,9 +76,10 @@
     first = split(table[at : at + 2 * HIGH, :HIGH])
     first = jnp.concatenate([first[0], first[0], first[1]], axis=1)
     at += 2 * HIGH
-    twist_cos, twist_sin = table[at : at + LANES, :], table[at + LANES : at + 2 * LANES, :]
-    at += 2 * LANES
-    cos, sin = table[at : at + GRID_ROWS, :], table[at + GRID_ROWS : at + 2 * GRID_ROWS, :]
+    twist_cos = jnp.concatenate([table[at : at + HIGH, :]] * 2, axis=0)
+    twist_sin = jnp.concatenate([table[at + HIGH : at + 2 * HIGH, :]] * 2, axis=0)
+    at += 2 * HIGH
+    cos, sin = table[at : at + 2 * GRID_ROWS, :], table[at + 2 * GRID_ROWS :, :]
     second = split(
         jnp.concatenate(
             [jnp.concatenate([cos, -sin], axis=1), jnp.concatenate([sin, cos], axis=1)], axis=0
@@ -110,25 +112,34 @@
     inner = jnp.dot(
         first, jnp.concatenate([top, low, top], axis=0), preferred_element_type=F32
     )
-    for c in range(channels):
-        real = inner[:HIGH, c * LANES : (c + 1) * LANES]
-        imag = inner[HIGH:, c * LANES : (c + 1) * LANES]
-        real = jnp.concatenate([real, real], axis=0)
-        imag = jnp.concatenate([imag, imag], axis=0)
+    lower = lax.broadcasted_iota(jnp.int32, (GRID_ROWS, LANES), 1) < HIGH
+    mixed = []
+    for c in range(0, channels, 2):
+        pair = [slice((c + i) * LANES, (c + i + 1) * LANES) for i in range(2)]
+        real = jnp.concatenate([inner[:HIGH, lanes] for lanes in pair], axis=0)
+        imag = jnp.concatenate([inner[HIGH:, lanes] for lanes in pair], axis=0)
         top, low = split(
             jnp.concatenate(
                 [real * twist_cos - imag * twist_sin, real * twist_sin + imag * twist_cos],
                 axis=1,
             )
         )
-        bins = lax.dot_general(
-            second,
-            jnp.concatenate([top, low, top], axis=1),
-            (((1,), (1,)), ((), ())),
-            preferred_element_type=F32,
-        )
-        grid_real[pl.ds(c, GRID_ROWS, stride=channels), :] = bins[:GRID_ROWS]
-        grid_imag[pl.ds(c, GRID_ROWS, stride=channels), :] = bins[GRID_ROWS:]
+        mixed.append(jnp.concatenate([top, low, top], axis=1))
+    bins_of_all = lax.dot_general(
+        second,
+        jnp.concatenate(mixed, axis=0),
+        (((1,), (1,)), ((), ())),
+        preferred_element_type=F32,
+    )
+    for c in range(0, channels, 2):
+        bins = bins_of_all[:, c // 2 * LANES : (c // 2 + 1) * LANES]
+        for grid, start in ((grid_real, 0), (grid_imag, 2 * GRID_ROWS)):
+            under = bins[start : start + GRID_ROWS]
+            over = bins[start + GRID_ROWS : start + 2 * GRID_ROWS]
+            rows = jnp.where(lower, under, pltpu.roll(over, HIGH, 1))
+            grid[pl.ds(c, GRID_ROWS, stride=channels), :] = rows
+            rows = jnp.where(lower, pltpu.roll(under, HIGH, 1), over)
+            grid[pl.ds(c + 1, GRID_ROWS, stride=channels), :] = rows
 
     live = (ROWS + 2) * channels
     real, imag = grid_real[:live, :], grid_imag[:live, :]
@@ -153,14 +164,22 @@
         outs[k][...] = white[me ^ k]
 
 
-def stack_kernel(blocks, windows, capacity, reach, pair_slots, scalars, *rest):
-    gathered, out = rest[:-1], rest[-1]
+def stack_kernel(blocks, windows, capacity, reach, pair_slots, width, places, scalars, *rest):
+    pieces, out = rest[:-1], rest[-1]
     me = scalars[0]
-    height = gathered[0].shape[0]
+    height = pieces[0].shape[0]
     channels = height // 2
-    width = (gathered[0].shape[1] - LANES) // windows
     slots = blocks * capacity
-    meta = jnp.concatenate([g[:, windows * width :] for g in gathered], axis=0)
+
+    def lanes_of(start, size):
+        found = []
+        for b in range(blocks):
+            for index, offset in places[b]:
+                if offset <= start < offset + pieces[index].shape[1]:
+                    found.append(pieces[index][:, start - offset : start - offset + size])
+        return jnp.concatenate(found, axis=0)
+
+    meta = lanes_of(0, LANES)
 
     row = lax.broadcasted_iota(jnp.int32, (slots, LANES), 0)
     lane = lax.broadcasted_iota(jnp.int32, (slots, LANES), 1)
@@ -212,7 +231,7 @@
     real = jnp.zeros((slots, width), F32)
     imag = jnp.zeros((slots, width), F32)
     for w in range(windows):
-        white = jnp.concatenate([g[:, w * width : (w + 1) * width] for g in gathered], axis=0)
+        white = lanes_of(LANES + w * width, width)
         rows = jnp.dot(choice, white, preferred_element_type=F32)
         sr, si, rr, ri = [rows[i * slots : (i + 1) * slots] for i in range(4)]
         real += sr * rr + si * ri
@@ -262,31 +281,42 @@
         name="whiten",
     )(lax.axis_index("win").astype(jnp.int32).reshape(1), traces, offsets, table)
     fields = [pair_source, pair_recv, pair_hop, pair_owner.reshape(1, -1)]
-    fields = jnp.concatenate(fields, axis=0).astype(BF16)
-    fields = jnp.pad(fields, ((0, height - 4), (0, LANES - pair_slots)))
-    moved = [pieces[0]] + [swapped(pieces[k], "win", k) for k in range(1, windows)]
-    packed = jnp.concatenate(moved + [fields], axis=1)
-
-    gathered = {0: packed}
+    fields = sum(
+        jnp.pad(field, ((i, height - 1 - i), (0, LANES - pair_slots)))
+        for i, field in enumerate(fields)
+    ).astype(BF16)
+    moved = [pieces[0]] + [swapped(pieces[k], "win", k) for k in range(windows - 1, 0, -1)]
+    packed = jnp.concatenate([fields] + moved, axis=1)
+
+    gathered = {0: [packed]}
     half = blocks // 2
     for k in range(blocks - 2, half - 1, -2):
-        gathered[k] = swapped(packed, "chan", k)
+        gathered[k] = [swapped(packed, "chan", k)]
     for k in range(1, half):
-        gathered[k] = swapped(packed, "chan", k)
+        gathered[k] = [swapped(packed, "chan", k)]
     for k in range(blocks - 2, half - 1, -2):
-        gathered[k + 1] = swapped(gathered[k], "chan", 1)
+        gathered[k + 1] = [swapped(piece, "chan", 1) for piece in gathered[k]]
+
+    order = [k for k in range(blocks - 2, half - 1, -2)]
+    order = [k + i for k in order for i in range(2)] + list(range(half - 1, -1, -1))
+    operands, places = [], {}
+    for k in order:
+        offset, places[k] = 0, []
+        for piece in gathered[k]:
+            places[k].append((len(operands), offset))
+            operands.append(piece)
+            offset += piece.shape[1]
 
     stacked = pl.pallas_call(
-        functools.partial(stack_kernel, blocks, windows, capacity, reach, pair_slots),
+        functools.partial(
+            stack_kernel, blocks, windows, capacity, reach, pair_slots, width, places
+        ),
         out_shape=jax.ShapeDtypeStruct((blocks * capacity * 2 * width // LANES, LANES), F32),
-        in_specs=[smem] + [vmem] * blocks,
+        in_specs=[smem] + [vmem] * len(operands),
         out_specs=vmem,
         compiler_params=pltpu.CompilerParams(vmem_limit_bytes=32 << 20),
         name="stack",
-    )(
-        lax.axis_index("chan").astype(jnp.int32).reshape(1),
-        *[gathered[k] for k in range(blocks)],
-    )
+    )(lax.axis_index("chan").astype(jnp.int32).reshape(1), *operands)
     stacked = stacked.reshape(blocks * capacity, width // LANES, 2, LANES)
     return stacked.transpose(0, 2, 1, 3).reshape(blocks * capacity, 2, width)
 

time: 25.2 us -> 24.4 us (0.968)
  local copies, waits for them, and re-layouts: 1.96 us -> 0.59 us
  waiting for transfers between devices: 5.17 us -> 6.23 us
  Pallas kernels: 3.83 us -> 3.56 us
    unnamed x12 -> x11, local copies, waits for them, and re-layouts: 1.96 us -> 0.59 us
    ppermute x10, waiting for transfers between devices: 5.17 us -> 6.23 us  [swapped(): return lax.ppermute(value, axis, [(i, i ^ bits) for i in range(peers)])]
    pallas_call x1, Pallas kernels: 2.44 us -> 2.16 us  [local(): pl.pallas_call(whiten_kernel, out_shape=[jax.ShapeDtypeStruct((height, wi...]
  transfers between devices with their start and end apart: 10 -> 10, of which waited for: 5 -> 6; matrix products, arithmetic and copies ran while one was open for 0% -> 0% of each run, Pallas kernels for 0% -> 0%
where the time goes in v3:
time: 24.4 us; the launch traced here: 24.2 us
  starting transfers between devices  13.1 us (54%)
  waiting for transfers between devices  6.23 us (26%)
  Pallas kernels  3.56 us (15%)
  between operations  0.69 us (3%)
  local copies, waits for them, and re-layouts  0.59 us (2%)
    ppermute x10, starting transfers between devices, swapped(): return lax.ppermute(value, axis, [(i, i ^ bits) for i in range(peers)])  13.1 us
    ppermute x10, waiting for transfers between devices, swapped(): return lax.ppermute(value, axis, [(i, i ^ bits) for i in range(peers)])  6.23 us
    pallas_call x1, Pallas kernels, local(): pl.pallas_call(whiten_kernel, out_shape=[jax.ShapeDtypeStruct((height, wi...  2.16 us
    pallas_call x1, Pallas kernels, local(): pl.pallas_call(functools.partial(stack_kernel, blocks, windows, capacity,...  1.4 us
    unnamed x11, local copies, waits for them, and re-layouts  0.59 us
  transfers between devices with their start and end apart: 10, of which 6 were waited for; matrix products, arithmetic and copies ran while one was open for 0% of the time, Pallas kernels for 0%

profile of v3, /device:TPU:0, one launch (start us, length us, event | category | flops | bytes accessed | tf_op | source)
XLA Modules:
  0.0 24.2 jit_solution(9619549707288156739)
XLA Ops:
  0.7 2.2 %whiten.1 = (bf16[16,512]{1,0:T(8,128)(2,1)S(1)}, bf16[16,512]{1,0:T(8,128)(2,1)S(1)}, bf16[16,512]{1,0:T(8,128)(2,1)S(1)}, bf16[16,512]{1,0:T(8,128)(2,1)S(1)}) custom-call(s32[1]{0:T(128)} %bitcast.2.place_ref, f32[8,12288]{1,0:T(8,128)} %traces_far.1, s32[1]{0:T(128)S(6)} %copy.13.offsets_far, f32[480,128]{1,0:T(8,128)} %constant.13.clone.table_far), custom_call_target="tpu_custom_call" | custom-call | tf_op jit(solution)/shard_map/whiten/pallas_call | solution.py:264
  2.8 2.4 %collective-permute-start = (bf16[16,512]{1,0:T(8,128)(2,1)S(1)}, bf16[16,512]{1,0:T(8,128)(2,1)S(1)}, u32[]{:S(2)}, u32[]{:S(2)}) collective-permute-start(bf16[16,512]{1,0:T(8,128)(2,1)S(1)} %get-tuple-element.10), channel_id=1, source_target_pairs={{0,3},{1,2},{2,1},{3,0},{4,7},{5,6},{6,5},{7,4},{8,11},{9,10},{10,... | collective-permute-start | bytes 49160 | tf_op jit(solution)/shard_map/ppermute | solution.py:248
  5.3 0.6 %collective-permute-start.1 = (bf16[16,512]{1,0:T(8,128)(2,1)S(1)}, bf16[16,512]{1,0:T(8,128)(2,1)S(1)}, u32[]{:S(2)}, u32[]{:S(2)}) collective-permute-start(bf16[16,512]{1,0:T(8,128)(2,1)S(1)} %get-tuple-element.11), channel_id=1, source_target_pairs={{0,2},{1,3},{2,0},{3,1},{4,6},{5,7},{6,4},{7,5},{8,10},{9,11},{10,... | collective-permute-start | bytes 49160 | tf_op jit(solution)/shard_map/ppermute | solution.py:248
  5.9 0.1 collective-permute-start.2
  6.0 0.5 %copy-done.3 = s32[1,24]{1,0:T(1,128)S(1)} copy-done((s32[1,24]{1,0:T(1,128)S(1)}, s32[1,24]{1,0:T(1,128)}, u32[]{:S(2)}) %copy-start.3) | copy-done | bytes 120
  6.6 0.0 copy-done
  6.6 0.0 copy-done.1
  6.6 0.0 copy-done.2
  6.6 0.1 collective-permute-done
  6.7 2.3 %collective-permute-done.1 = bf16[16,512]{1,0:T(8,128)(2,1)S(1)} collective-permute-done((bf16[16,512]{1,0:T(8,128)(2,1)S(1)}, bf16[16,512]{1,0:T(8,128)(2,1)S(1)}, u32[]{:S(2)}, u32[]{:S(2)}) %collective-permute-start.1) | collective-permute-done | bytes 16416 | tf_op jit(solution)/shard_map/ppermute | solution.py:248
  9.0 0.0 collective-permute-done.2
  9.0 2.7 %collective-permute-start.5 = (bf16[16,2176]{1,0:T(8,128)(2,1)S(1)}, bf16[16,2176]{1,0:T(8,128)(2,1)S(1)}, u32[]{:S(2)}, u32[]{:S(2)}) collective-permute-start(bf16[16,2176]{1,0:T(8,128)(2,1)S(1)} %constant_dynamic-update-slice_fusion.rest_7_), channel_id=1, source_target_pairs={{0,16},{4,20},{8,24},{12,28},{16,0},{20,4},{24,8},{28,12},{1,17},{... | collective-permute-start | bytes 208904 | tf_op jit(solution)/shard_map/ppermute | solution.py:248
  11.7 1.3 %collective-permute-start.3 = (bf16[16,2176]{1,0:T(8,128)(2,1)S(1)}, bf16[16,2176]{1,0:T(8,128)(2,1)S(1)}, u32[]{:S(2)}, u32[]{:S(2)}) collective-permute-start(bf16[16,2176]{1,0:T(8,128)(2,1)S(1)} %constant_dynamic-update-slice_fusion.rest_7_), channel_id=1, source_target_pairs={{0,24},{4,28},{8,16},{12,20},{16,8},{20,12},{24,0},{28,4},{1,25},{... | collective-permute-start | bytes 208904 | tf_op jit(solution)/shard_map/ppermute | solution.py:248
  13.0 1.5 %collective-permute-start.9 = (bf16[16,2176]{1,0:T(8,128)(2,1)S(1)}, bf16[16,2176]{1,0:T(8,128)(2,1)S(1)}, u32[]{:S(2)}, u32[]{:S(2)}) collective-permute-start(bf16[16,2176]{1,0:T(8,128)(2,1)S(1)} %constant_dynamic-update-slice_fusion.rest_7_), channel_id=1, source_target_pairs={{0,4},{4,0},{8,12},{12,8},{16,20},{20,16},{24,28},{28,24},{1,5},{5... | collective-permute-start | bytes 208904 | tf_op jit(solution)/shard_map/ppermute | solution.py:248
  14.5 0.2 collective-permute-start.8
  14.8 1.7 %collective-permute-start.7 = (bf16[16,2176]{1,0:T(8,128)(2,1)S(1)}, bf16[16,2176]{1,0:T(8,128)(2,1)S(1)}, u32[]{:S(2)}, u32[]{:S(2)}) collective-permute-start(bf16[16,2176]{1,0:T(8,128)(2,1)S(1)} %constant_dynamic-update-slice_fusion.rest_7_), channel_id=1, source_target_pairs={{0,12},{4,8},{8,4},{12,0},{16,28},{20,24},{24,20},{28,16},{1,13},{... | collective-permute-start | bytes 208904 | tf_op jit(solution)/shard_map/ppermute | solution.py:248
  16.5 0.0 collective-permute-done.5.rest_2_
  16.5 1.5 %collective-permute-start.6 = (bf16[16,2176]{1,0:T(8,128)(2,1)S(1)}, bf16[16,2176]{1,0:T(8,128)(2,1)S(1)}, u32[]{:S(2)}, u32[]{:S(2)}) collective-permute-start(bf16[16,2176]{1,0:T(8,128)(2,1)S(1)} %collective-permute-done.5.rest_2_), channel_id=1, source_target_pairs={{0,4},{4,0},{8,12},{12,8},{16,20},{20,16},{24,28},{28,24},{1,5},{5... | collective-permute-start | bytes 208904 | tf_op jit(solution)/shard_map/ppermute | solution.py:248
  18.0 0.5 %collective-permute-done.3.rest_0_ = bf16[16,2176]{1,0:T(8,128)(2,1)S(1)} collective-permute-done((bf16[16,2176]{1,0:T(8,128)(2,1)S(1)}, bf16[16,2176]{1,0:T(8,128)(2,1)S(1)}, u32[]{:S(2)}, u32[]{:S(2)}) %collective-permute-start.3) | collective-permute-done | bytes 69664 | tf_op jit(solution)/shard_map/ppermute | solution.py:248
  18.5 0.9 %collective-permute-start.4 = (bf16[16,2176]{1,0:T(8,128)(2,1)S(1)}, bf16[16,2176]{1,0:T(8,128)(2,1)S(1)}, u32[]{:S(2)}, u32[]{:S(2)}) collective-permute-start(bf16[16,2176]{1,0:T(8,128)(2,1)S(1)} %collective-permute-done.3.rest_0_), channel_id=1, source_target_pairs={{0,4},{4,0},{8,12},{12,8},{16,20},{20,16},{24,28},{28,24},{1,5},{5... | collective-permute-start | bytes 208904 | tf_op jit(solution)/shard_map/ppermute | solution.py:248
  19.5 0.9 %collective-permute-done.7.rest_4_ = bf16[16,2176]{1,0:T(8,128)(2,1)S(1)} collective-permute-done((bf16[16,2176]{1,0:T(8,128)(2,1)S(1)}, bf16[16,2176]{1,0:T(8,128)(2,1)S(1)}, u32[]{:S(2)}, u32[]{:S(2)}) %collective-permute-start.7) | collective-permute-done | bytes 69664 | tf_op jit(solution)/shard_map/ppermute | solution.py:248
  20.3 0.7 %collective-permute-done.6.rest_3_ = bf16[16,2176]{1,0:T(8,128)(2,1)S(1)} collective-permute-done((bf16[16,2176]{1,0:T(8,128)(2,1)S(1)}, bf16[16,2176]{1,0:T(8,128)(2,1)S(1)}, u32[]{:S(2)}, u32[]{:S(2)}) %collective-permute-start.6) | collective-permute-done | bytes 69664 | tf_op jit(solution)/shard_map/ppermute | solution.py:248
  21.1 1.8 %collective-permute-done.4.rest_1_ = bf16[16,2176]{1,0:T(8,128)(2,1)S(1)} collective-permute-done((bf16[16,2176]{1,0:T(8,128)(2,1)S(1)}, bf16[16,2176]{1,0:T(8,128)(2,1)S(1)}, u32[]{:S(2)}, u32[]{:S(2)}) %collective-permute-start.4) | collective-permute-done | bytes 69664 | tf_op jit(solution)/shard_map/ppermute | solution.py:248
  22.8 1.4 %stack.1 = f32[384,128]{1,0:T(8,128)} custom-call(s32[1]{0:T(128)} %bitcast.scalars, bf16[16,2176]{1,0:T(8,128)(2,1)S(1)} %collective-permute-done.3.rest_0_, bf16[16,2176]{1,0:T(8,128)(2,1)S(1)} %collective-permute-done.4.rest_1_, bf16[16,2176]{1,0:T(8,128)(2,1)S(1)} %collective-permute-done.5.rest_2_, bf16[16,2176]{1,0:T(8,128)(2,1)S(1)} %collective-permute-done.6.rest_3_, ...), custom_call_target="tpu_custom_call" | custom-call | tf_op jit(solution)/shard_map/stack/pallas_call | solution.py:310
  (11 shorter events, 0.0 us)
Async XLA Ops:
  2.8 3.9 %collective-permute-start = (bf16[16,512]{1,0:T(8,128)(2,1)S(1)}, bf16[16,512]{1,0:T(8,128)(2,1)S(1)}, u32[]{:S(2)}, u32[]{:S(2)}) collective-permute-start(bf16[16,512]{1,0:T(8,128)(2,1)S(1)} %get-tuple-element.10), channel_id=1, source_target_pairs={{0,3},{1,2},{2,1},{3,0},{4,7},{5,6},{6,5},{7,4},{8,11},{9,10},{10,... | collective-permute-start | bytes 49160 | tf_op jit(solution)/shard_map/ppermute | solution.py:248
  5.3 3.7 %collective-permute-start.1 = (bf16[16,512]{1,0:T(8,128)(2,1)S(1)}, bf16[16,512]{1,0:T(8,128)(2,1)S(1)}, u32[]{:S(2)}, u32[]{:S(2)}) collective-permute-start(bf16[16,512]{1,0:T(8,128)(2,1)S(1)} %get-tuple-element.11), channel_id=1, source_target_pairs={{0,2},{1,3},{2,0},{3,1},{4,6},{5,7},{6,4},{7,5},{8,10},{9,11},{10,... | collective-permute-start | bytes 49160 | tf_op jit(solution)/shard_map/ppermute | solution.py:248
  5.9 0.7 %copy-start.3 = (s32[1,24]{1,0:T(1,128)S(1)}, s32[1,24]{1,0:T(1,128)}, u32[]{:S(2)}) copy-start(s32[1,24]{1,0:T(1,128)} %param.9) | copy-start | bytes 292
  5.9 0.7 %copy-start = (s32[24,1]{0,1:T(1,128)S(1)}, s32[24,1]{0,1:T(1,128)}, u32[]{:S(2)}) copy-start(s32[24,1]{0,1:T(1,128)} %param.12) | copy-start | bytes 292
  5.9 0.7 %copy-start.1 = (s32[1,24]{1,0:T(1,128)S(1)}, s32[1,24]{1,0:T(1,128)}, u32[]{:S(2)}) copy-start(s32[1,24]{1,0:T(1,128)} %param.11) | copy-start | bytes 292
  5.9 0.7 %copy-start.2 = (s32[1,24]{1,0:T(1,128)S(1)}, s32[1,24]{1,0:T(1,128)}, u32[]{:S(2)}) copy-start(s32[1,24]{1,0:T(1,128)} %param.10) | copy-start | bytes 292
  5.9 3.1 %collective-permute-start.2 = (bf16[16,512]{1,0:T(8,128)(2,1)S(1)}, bf16[16,512]{1,0:T(8,128)(2,1)S(1)}, u32[]{:S(2)}, u32[]{:S(2)}) collective-permute-start(bf16[16,512]{1,0:T(8,128)(2,1)S(1)} %get-tuple-element.12), channel_id=1, source_target_pairs={{0,1},{1,0},{2,3},{3,2},{4,5},{5,4},{6,7},{7,6},{8,9},{9,8},{10,11... | collective-permute-start | bytes 49160 | tf_op jit(solution)/shard_map/ppermute | solution.py:248
  9.0 7.5 %collective-permute-start.5 = (bf16[16,2176]{1,0:T(8,128)(2,1)S(1)}, bf16[16,2176]{1,0:T(8,128)(2,1)S(1)}, u32[]{:S(2)}, u32[]{:S(2)}) collective-permute-start(bf16[16,2176]{1,0:T(8,128)(2,1)S(1)} %constant_dynamic-update-slice_fusion.rest_7_), channel_id=1, source_target_pairs={{0,16},{4,20},{8,24},{12,28},{16,0},{20,4},{24,8},{28,12},{1,17},{... | collective-permute-start | bytes 208904 | tf_op jit(solution)/shard_map/ppermute | solution.py:248
  11.7 6.8 %collective-permute-start.3 = (bf16[16,2176]{1,0:T(8,128)(2,1)S(1)}, bf16[16,2176]{1,0:T(8,128)(2,1)S(1)}, u32[]{:S(2)}, u32[]{:S(2)}) collective-permute-start(bf16[16,2176]{1,0:T(8,128)(2,1)S(1)} %constant_dynamic-update-slice_fusion.rest_7_), channel_id=1, source_target_pairs={{0,24},{4,28},{8,16},{12,20},{16,8},{20,12},{24,0},{28,4},{1,25},{... | collective-permute-start | bytes 208904 | tf_op jit(solution)/shard_map/ppermute | solution.py:248
  13.0 6.4 %collective-permute-start.9 = (bf16[16,2176]{1,0:T(8,128)(2,1)S(1)}, bf16[16,2176]{1,0:T(8,128)(2,1)S(1)}, u32[]{:S(2)}, u32[]{:S(2)}) collective-permute-start(bf16[16,2176]{1,0:T(8,128)(2,1)S(1)} %constant_dynamic-update-slice_fusion.rest_7_), channel_id=1, source_target_pairs={{0,4},{4,0},{8,12},{12,8},{16,20},{20,16},{24,28},{28,24},{1,5},{5... | collective-permute-start | bytes 208904 | tf_op jit(solution)/shard_map/ppermute | solution.py:248
  14.5 4.9 %collective-permute-start.8 = (bf16[16,2176]{1,0:T(8,128)(2,1)S(1)}, bf16[16,2176]{1,0:T(8,128)(2,1)S(1)}, u32[]{:S(2)}, u32[]{:S(2)}) collective-permute-start(bf16[16,2176]{1,0:T(8,128)(2,1)S(1)} %constant_dynamic-update-slice_fusion.rest_7_), channel_id=1, source_target_pairs={{0,8},{4,12},{8,0},{12,4},{16,24},{20,28},{24,16},{28,20},{1,9},{5... | collective-permute-start | bytes 208904 | tf_op jit(solution)/shard_map/ppermute | solution.py:248
  14.8 5.6 %collective-permute-start.7 = (bf16[16,2176]{1,0:T(8,128)(2,1)S(1)}, bf16[16,2176]{1,0:T(8,128)(2,1)S(1)}, u32[]{:S(2)}, u32[]{:S(2)}) collective-permute-start(bf16[16,2176]{1,0:T(8,128)(2,1)S(1)} %constant_dynamic-update-slice_fusion.rest_7_), channel_id=1, source_target_pairs={{0,12},{4,8},{8,4},{12,0},{16,28},{20,24},{24,20},{28,16},{1,13},{... | collective-permute-start | bytes 208904 | tf_op jit(solution)/shard_map/ppermute | solution.py:248
  16.5 4.5 %collective-permute-start.6 = (bf16[16,2176]{1,0:T(8,128)(2,1)S(1)}, bf16[16,2176]{1,0:T(8,128)(2,1)S(1)}, u32[]{:S(2)}, u32[]{:S(2)}) collective-permute-start(bf16[16,2176]{1,0:T(8,128)(2,1)S(1)} %collective-permute-done.5.rest_2_), channel_id=1, source_target_pairs={{0,4},{4,0},{8,12},{12,8},{16,20},{20,16},{24,28},{28,24},{1,5},{5... | collective-permute-start | bytes 208904 | tf_op jit(solution)/shard_map/ppermute | solution.py:248
  18.5 4.3 %collective-permute-start.4 = (bf16[16,2176]{1,0:T(8,128)(2,1)S(1)}, bf16[16,2176]{1,0:T(8,128)(2,1)S(1)}, u32[]{:S(2)}, u32[]{:S(2)}) collective-permute-start(bf16[16,2176]{1,0:T(8,128)(2,1)S(1)} %collective-permute-done.3.rest_0_), channel_id=1, source_target_pairs={{0,4},{4,0},{8,12},{12,8},{16,20},{20,16},{24,28},{28,24},{1,5},{5... | collective-permute-start | bytes 208904 | tf_op jit(solution)/shard_map/ppermute | solution.py:248

commit v4 on v3

--- a/solution.py
+++ b/solution.py
@@ -164,7 +164,7 @@
         outs[k][...] = white[me ^ k]
 
 
-def stack_kernel(blocks, windows, capacity, reach, pair_slots, width, places, scalars, *rest):
+def stack_kernel(blocks, windows, capacity, reach, pair_slots, width, order, scalars, *rest):
     pieces, out = rest[:-1], rest[-1]
     me = scalars[0]
     height = pieces[0].shape[0]
@@ -172,12 +172,9 @@
     slots = blocks * capacity
 
     def lanes_of(start, size):
-        found = []
-        for b in range(blocks):
-            for index, offset in places[b]:
-                if offset <= start < offset + pieces[index].shape[1]:
-                    found.append(pieces[index][:, start - offset : start - offset + size])
-        return jnp.concatenate(found, axis=0)
+        return jnp.concatenate(
+            [pieces[order.index(b)][:, start : start + size] for b in range(blocks)], axis=0
+        )
 
     meta = lanes_of(0, LANES)
 
@@ -288,35 +285,27 @@
     moved = [pieces[0]] + [swapped(pieces[k], "win", k) for k in range(windows - 1, 0, -1)]
     packed = jnp.concatenate([fields] + moved, axis=1)
 
-    gathered = {0: [packed]}
-    half = blocks // 2
-    for k in range(blocks - 2, half - 1, -2):
-        gathered[k] = [swapped(packed, "chan", k)]
-    for k in range(1, half):
-        gathered[k] = [swapped(packed, "chan", k)]
-    for k in range(blocks - 2, half - 1, -2):
-        gathered[k + 1] = [swapped(piece, "chan", 1) for piece in gathered[k]]
-
-    order = [k for k in range(blocks - 2, half - 1, -2)]
-    order = [k + i for k in order for i in range(2)] + list(range(half - 1, -1, -1))
-    operands, places = [], {}
-    for k in order:
-        offset, places[k] = 0, []
-        for piece in gathered[k]:
-            places[k].append((len(operands), offset))
-            operands.append(piece)
-            offset += piece.shape[1]
+    gathered = {0: packed}
+    roots = [k + 2 for k in range(4, blocks, 4)]
+    for root in roots:
+        gathered[root] = swapped(packed, "chan", root)
+    for k in range(1, 4):
+        gathered[k] = swapped(packed, "chan", k)
+    for root in roots:
+        for k in range(1, 4):
+            gathered[root ^ k] = swapped(gathered[root], "chan", k)
+    order = [root ^ k for root in roots for k in (2, 1, 3, 0)] + [3, 2, 1, 0]
 
     stacked = pl.pallas_call(
         functools.partial(
-            stack_kernel, blocks, windows, capacity, reach, pair_slots, width, places
+            stack_kernel, blocks, windows, capacity, reach, pair_slots, width, order
         ),
         out_shape=jax.ShapeDtypeStruct((blocks * capacity * 2 * width // LANES, LANES), F32),
-        in_specs=[smem] + [vmem] * len(operands),
+        in_specs=[smem] + [vmem] * blocks,
         out_specs=vmem,
         compiler_params=pltpu.CompilerParams(vmem_limit_bytes=32 << 20),
         name="stack",
-    )(lax.axis_index("chan").astype(jnp.int32).reshape(1), *operands)
+    )(lax.axis_index("chan").astype(jnp.int32).reshape(1), *[gathered[k] for k in order])
     stacked = stacked.reshape(blocks * capacity, width // LANES, 2, LANES)
     return stacked.transpose(0, 2, 1, 3).reshape(blocks * capacity, 2, width)
 

time: 24.4 us -> 23.8 us (0.975)
  waiting for transfers between devices: 6.23 us -> 4.95 us
  starting transfers between devices: 13.1 us -> 13.8 us
    ppermute x10, waiting for transfers between devices: 6.23 us -> 4.95 us  [swapped(): return lax.ppermute(value, axis, [(i, i ^ bits) for i in range(peers)])]
    ppermute x10, starting transfers between devices: 13.1 us -> 13.8 us  [swapped(): return lax.ppermute(value, axis, [(i, i ^ bits) for i in range(peers)])]
  transfers between devices with their start and end apart: 10 -> 10, of which waited for: 6 -> 5; matrix products, arithmetic and copies ran while one was open for 0% -> 0% of each run, Pallas kernels for 0% -> 0%
where the time goes in v4:
time: 23.8 us; the launch traced here: 23.6 us
  starting transfers between devices  13.8 us (58%)
  waiting for transfers between devices  4.95 us (21%)
  Pallas kernels  3.55 us (15%)
  between operations  0.69 us (3%)
  local copies, waits for them, and re-layouts  0.59 us (2%)
    ppermute x10, starting transfers between devices, swapped(): return lax.ppermute(value, axis, [(i, i ^ bits) for i in range(peers)])  13.8 us
    ppermute x10, waiting for transfers between devices, swapped(): return lax.ppermute(value, axis, [(i, i ^ bits) for i in range(peers)])  4.95 us
    pallas_call x1, Pallas kernels, local(): pl.pallas_call(whiten_kernel, out_shape=[jax.ShapeDtypeStruct((height, wi...  2.16 us
    pallas_call x1, Pallas kernels, local(): pl.pallas_call(functools.partial(stack_kernel, blocks, windows, capacity,...  1.39 us
    unnamed x11, local copies, waits for them, and re-layouts  0.59 us
  transfers between devices with their start and end apart: 10, of which 5 were waited for; matrix products, arithmetic and copies ran while one was open for 0% of the time, Pallas kernels for 0%

profile of v4, /device:TPU:0, one launch (start us, length us, event | category | flops | bytes accessed | tf_op | source)
XLA Modules:
  0.0 23.6 jit_solution(3234614691361094521)
XLA Ops:
  0.7 2.2 %whiten.1 = (bf16[16,512]{1,0:T(8,128)(2,1)S(1)}, bf16[16,512]{1,0:T(8,128)(2,1)S(1)}, bf16[16,512]{1,0:T(8,128)(2,1)S(1)}, bf16[16,512]{1,0:T(8,128)(2,1)S(1)}) custom-call(s32[1]{0:T(128)} %bitcast.2.place_ref, f32[8,12288]{1,0:T(8,128)} %traces_far.1, s32[1]{0:T(128)S(6)} %copy.13.offsets_far, f32[480,128]{1,0:T(8,128)} %constant.13.clone.table_far), custom_call_target="tpu_custom_call" | custom-call | tf_op jit(solution)/shard_map/whiten/pallas_call | solution.py:261
  2.8 2.4 %collective-permute-start = (bf16[16,512]{1,0:T(8,128)(2,1)S(1)}, bf16[16,512]{1,0:T(8,128)(2,1)S(1)}, u32[]{:S(2)}, u32[]{:S(2)}) collective-permute-start(bf16[16,512]{1,0:T(8,128)(2,1)S(1)} %get-tuple-element.10), channel_id=1, source_target_pairs={{0,3},{1,2},{2,1},{3,0},{4,7},{5,6},{6,5},{7,4},{8,11},{9,10},{10,... | collective-permute-start | bytes 49160 | tf_op jit(solution)/shard_map/ppermute | solution.py:245
  5.3 0.6 %collective-permute-start.1 = (bf16[16,512]{1,0:T(8,128)(2,1)S(1)}, bf16[16,512]{1,0:T(8,128)(2,1)S(1)}, u32[]{:S(2)}, u32[]{:S(2)}) collective-permute-start(bf16[16,512]{1,0:T(8,128)(2,1)S(1)} %get-tuple-element.11), channel_id=1, source_target_pairs={{0,2},{1,3},{2,0},{3,1},{4,6},{5,7},{6,4},{7,5},{8,10},{9,11},{10,... | collective-permute-start | bytes 49160 | tf_op jit(solution)/shard_map/ppermute | solution.py:245
  5.9 0.1 collective-permute-start.2
  6.0 0.5 %copy-done.3 = s32[1,24]{1,0:T(1,128)S(1)} copy-done((s32[1,24]{1,0:T(1,128)S(1)}, s32[1,24]{1,0:T(1,128)}, u32[]{:S(2)}) %copy-start.3) | copy-done | bytes 120
  6.6 0.0 copy-done
  6.6 0.0 copy-done.1
  6.6 0.0 copy-done.2
  6.6 0.1 collective-permute-done
  6.7 2.3 %collective-permute-done.1 = bf16[16,512]{1,0:T(8,128)(2,1)S(1)} collective-permute-done((bf16[16,512]{1,0:T(8,128)(2,1)S(1)}, bf16[16,512]{1,0:T(8,128)(2,1)S(1)}, u32[]{:S(2)}, u32[]{:S(2)}) %collective-permute-start.1) | collective-permute-done | bytes 16416 | tf_op jit(solution)/shard_map/ppermute | solution.py:245
  9.0 0.0 collective-permute-done.2
  9.0 3.7 %collective-permute-start.3 = (bf16[16,2176]{1,0:T(8,128)(2,1)S(1)}, bf16[16,2176]{1,0:T(8,128)(2,1)S(1)}, u32[]{:S(2)}, u32[]{:S(2)}) collective-permute-start(bf16[16,2176]{1,0:T(8,128)(2,1)S(1)} %constant_dynamic-update-slice_fusion.rest_7_), channel_id=1, source_target_pairs={{0,24},{4,28},{8,16},{12,20},{16,8},{20,12},{24,0},{28,4},{1,25},{... | collective-permute-start | bytes 208904 | tf_op jit(solution)/shard_map/ppermute | solution.py:245
  12.7 1.5 %collective-permute-start.9 = (bf16[16,2176]{1,0:T(8,128)(2,1)S(1)}, bf16[16,2176]{1,0:T(8,128)(2,1)S(1)}, u32[]{:S(2)}, u32[]{:S(2)}) collective-permute-start(bf16[16,2176]{1,0:T(8,128)(2,1)S(1)} %constant_dynamic-update-slice_fusion.rest_7_), channel_id=1, source_target_pairs={{0,4},{4,0},{8,12},{12,8},{16,20},{20,16},{24,28},{28,24},{1,5},{5... | collective-permute-start | bytes 208904 | tf_op jit(solution)/shard_map/ppermute | solution.py:245
  14.2 2.0 %collective-permute-start.7 = (bf16[16,2176]{1,0:T(8,128)(2,1)S(1)}, bf16[16,2176]{1,0:T(8,128)(2,1)S(1)}, u32[]{:S(2)}, u32[]{:S(2)}) collective-permute-start(bf16[16,2176]{1,0:T(8,128)(2,1)S(1)} %constant_dynamic-update-slice_fusion.rest_7_), channel_id=1, source_target_pairs={{0,12},{4,8},{8,4},{12,0},{16,28},{20,24},{24,20},{28,16},{1,13},{... | collective-permute-start | bytes 208904 | tf_op jit(solution)/shard_map/ppermute | solution.py:245
  16.2 1.0 %collective-permute-start.6 = (bf16[16,2176]{1,0:T(8,128)(2,1)S(1)}, bf16[16,2176]{1,0:T(8,128)(2,1)S(1)}, u32[]{:S(2)}, u32[]{:S(2)}) collective-permute-start(bf16[16,2176]{1,0:T(8,128)(2,1)S(1)} %collective-permute-done.3.rest_3_), channel_id=1, source_target_pairs={{0,12},{4,8},{8,4},{12,0},{16,28},{20,24},{24,20},{28,16},{1,13},{... | collective-permute-start | bytes 208904 | tf_op jit(solution)/shard_map/ppermute | solution.py:245
  17.1 0.6 %collective-permute-start.5 = (bf16[16,2176]{1,0:T(8,128)(2,1)S(1)}, bf16[16,2176]{1,0:T(8,128)(2,1)S(1)}, u32[]{:S(2)}, u32[]{:S(2)}) collective-permute-start(bf16[16,2176]{1,0:T(8,128)(2,1)S(1)} %collective-permute-done.3.rest_3_), channel_id=1, source_target_pairs={{0,4},{4,0},{8,12},{12,8},{16,20},{20,16},{24,28},{28,24},{1,5},{5... | collective-permute-start | bytes 208904 | tf_op jit(solution)/shard_map/ppermute | solution.py:245
  17.7 0.0 collective-permute-done.9.rest_6_
  17.7 1.9 %collective-permute-start.4 = (bf16[16,2176]{1,0:T(8,128)(2,1)S(1)}, bf16[16,2176]{1,0:T(8,128)(2,1)S(1)}, u32[]{:S(2)}, u32[]{:S(2)}) collective-permute-start(bf16[16,2176]{1,0:T(8,128)(2,1)S(1)} %collective-permute-done.3.rest_3_), channel_id=1, source_target_pairs={{0,8},{4,12},{8,0},{12,4},{16,24},{20,28},{24,16},{28,20},{1,9},{5... | collective-permute-start | bytes 208904 | tf_op jit(solution)/shard_map/ppermute | solution.py:245
  19.7 0.0 collective-permute-done.8.rest_5_
  19.7 0.7 %collective-permute-done.7.rest_4_ = bf16[16,2176]{1,0:T(8,128)(2,1)S(1)} collective-permute-done((bf16[16,2176]{1,0:T(8,128)(2,1)S(1)}, bf16[16,2176]{1,0:T(8,128)(2,1)S(1)}, u32[]{:S(2)}, u32[]{:S(2)}) %collective-permute-start.7) | collective-permute-done | bytes 69664 | tf_op jit(solution)/shard_map/ppermute | solution.py:245
  20.4 1.1 %collective-permute-done.6.rest_2_ = bf16[16,2176]{1,0:T(8,128)(2,1)S(1)} collective-permute-done((bf16[16,2176]{1,0:T(8,128)(2,1)S(1)}, bf16[16,2176]{1,0:T(8,128)(2,1)S(1)}, u32[]{:S(2)}, u32[]{:S(2)}) %collective-permute-start.6) | collective-permute-done | bytes 69664 | tf_op jit(solution)/shard_map/ppermute | solution.py:245
  21.5 0.7 %collective-permute-done.5.rest_1_ = bf16[16,2176]{1,0:T(8,128)(2,1)S(1)} collective-permute-done((bf16[16,2176]{1,0:T(8,128)(2,1)S(1)}, bf16[16,2176]{1,0:T(8,128)(2,1)S(1)}, u32[]{:S(2)}, u32[]{:S(2)}) %collective-permute-start.5) | collective-permute-done | bytes 69664 | tf_op jit(solution)/shard_map/ppermute | solution.py:245
  22.2 0.0 collective-permute-done.4.rest_0_
  22.2 1.4 %stack.1 = f32[384,128]{1,0:T(8,128)} custom-call(s32[1]{0:T(128)} %bitcast.scalars, bf16[16,2176]{1,0:T(8,128)(2,1)S(1)} %collective-permute-done.4.rest_0_, bf16[16,2176]{1,0:T(8,128)(2,1)S(1)} %collective-permute-done.5.rest_1_, bf16[16,2176]{1,0:T(8,128)(2,1)S(1)} %collective-permute-done.6.rest_2_, bf16[16,2176]{1,0:T(8,128)(2,1)S(1)} %collective-permute-done.3.rest_3_, ...), custom_call_target="tpu_custom_call" | custom-call | tf_op jit(solution)/shard_map/stack/pallas_call | solution.py:299
  (11 shorter events, 0.0 us)
Async XLA Ops:
  2.8 3.9 %collective-permute-start = (bf16[16,512]{1,0:T(8,128)(2,1)S(1)}, bf16[16,512]{1,0:T(8,128)(2,1)S(1)}, u32[]{:S(2)}, u32[]{:S(2)}) collective-permute-start(bf16[16,512]{1,0:T(8,128)(2,1)S(1)} %get-tuple-element.10), channel_id=1, source_target_pairs={{0,3},{1,2},{2,1},{3,0},{4,7},{5,6},{6,5},{7,4},{8,11},{9,10},{10,... | collective-permute-start | bytes 49160 | tf_op jit(solution)/shard_map/ppermute | solution.py:245
  5.3 3.7 %collective-permute-start.1 = (bf16[16,512]{1,0:T(8,128)(2,1)S(1)}, bf16[16,512]{1,0:T(8,128)(2,1)S(1)}, u32[]{:S(2)}, u32[]{:S(2)}) collective-permute-start(bf16[16,512]{1,0:T(8,128)(2,1)S(1)} %get-tuple-element.11), channel_id=1, source_target_pairs={{0,2},{1,3},{2,0},{3,1},{4,6},{5,7},{6,4},{7,5},{8,10},{9,11},{10,... | collective-permute-start | bytes 49160 | tf_op jit(solution)/shard_map/ppermute | solution.py:245
  5.9 0.7 %copy-start.3 = (s32[1,24]{1,0:T(1,128)S(1)}, s32[1,24]{1,0:T(1,128)}, u32[]{:S(2)}) copy-start(s32[1,24]{1,0:T(1,128)} %param.9) | copy-start | bytes 292
  5.9 0.7 %copy-start = (s32[24,1]{0,1:T(1,128)S(1)}, s32[24,1]{0,1:T(1,128)}, u32[]{:S(2)}) copy-start(s32[24,1]{0,1:T(1,128)} %param.12) | copy-start | bytes 292
  5.9 0.7 %copy-start.1 = (s32[1,24]{1,0:T(1,128)S(1)}, s32[1,24]{1,0:T(1,128)}, u32[]{:S(2)}) copy-start(s32[1,24]{1,0:T(1,128)} %param.11) | copy-start | bytes 292
  5.9 0.7 %copy-start.2 = (s32[1,24]{1,0:T(1,128)S(1)}, s32[1,24]{1,0:T(1,128)}, u32[]{:S(2)}) copy-start(s32[1,24]{1,0:T(1,128)} %param.10) | copy-start | bytes 292
  5.9 3.1 %collective-permute-start.2 = (bf16[16,512]{1,0:T(8,128)(2,1)S(1)}, bf16[16,512]{1,0:T(8,128)(2,1)S(1)}, u32[]{:S(2)}, u32[]{:S(2)}) collective-permute-start(bf16[16,512]{1,0:T(8,128)(2,1)S(1)} %get-tuple-element.12), channel_id=1, source_target_pairs={{0,1},{1,0},{2,3},{3,2},{4,5},{5,4},{6,7},{7,6},{8,9},{9,8},{10,11... | collective-permute-start | bytes 49160 | tf_op jit(solution)/shard_map/ppermute | solution.py:245
  9.0 7.2 %collective-permute-start.3 = (bf16[16,2176]{1,0:T(8,128)(2,1)S(1)}, bf16[16,2176]{1,0:T(8,128)(2,1)S(1)}, u32[]{:S(2)}, u32[]{:S(2)}) collective-permute-start(bf16[16,2176]{1,0:T(8,128)(2,1)S(1)} %constant_dynamic-update-slice_fusion.rest_7_), channel_id=1, source_target_pairs={{0,24},{4,28},{8,16},{12,20},{16,8},{20,12},{24,0},{28,4},{1,25},{... | collective-permute-start | bytes 208904 | tf_op jit(solution)/shard_map/ppermute | solution.py:245
  12.7 5.0 %collective-permute-start.9 = (bf16[16,2176]{1,0:T(8,128)(2,1)S(1)}, bf16[16,2176]{1,0:T(8,128)(2,1)S(1)}, u32[]{:S(2)}, u32[]{:S(2)}) collective-permute-start(bf16[16,2176]{1,0:T(8,128)(2,1)S(1)} %constant_dynamic-update-slice_fusion.rest_7_), channel_id=1, source_target_pairs={{0,4},{4,0},{8,12},{12,8},{16,20},{20,16},{24,28},{28,24},{1,5},{5... | collective-permute-start | bytes 208904 | tf_op jit(solution)/shard_map/ppermute | solution.py:245
  14.2 5.5 %collective-permute-start.8 = (bf16[16,2176]{1,0:T(8,128)(2,1)S(1)}, bf16[16,2176]{1,0:T(8,128)(2,1)S(1)}, u32[]{:S(2)}, u32[]{:S(2)}) collective-permute-start(bf16[16,2176]{1,0:T(8,128)(2,1)S(1)} %constant_dynamic-update-slice_fusion.rest_7_), channel_id=1, source_target_pairs={{0,8},{4,12},{8,0},{12,4},{16,24},{20,28},{24,16},{28,20},{1,9},{5... | collective-permute-start | bytes 208904 | tf_op jit(solution)/shard_map/ppermute | solution.py:245
  14.2 6.2 %collective-permute-start.7 = (bf16[16,2176]{1,0:T(8,128)(2,1)S(1)}, bf16[16,2176]{1,0:T(8,128)(2,1)S(1)}, u32[]{:S(2)}, u32[]{:S(2)}) collective-permute-start(bf16[16,2176]{1,0:T(8,128)(2,1)S(1)} %constant_dynamic-update-slice_fusion.rest_7_), channel_id=1, source_target_pairs={{0,12},{4,8},{8,4},{12,0},{16,28},{20,24},{24,20},{28,16},{1,13},{... | collective-permute-start | bytes 208904 | tf_op jit(solution)/shard_map/ppermute | solution.py:245
  16.2 5.4 %collective-permute-start.6 = (bf16[16,2176]{1,0:T(8,128)(2,1)S(1)}, bf16[16,2176]{1,0:T(8,128)(2,1)S(1)}, u32[]{:S(2)}, u32[]{:S(2)}) collective-permute-start(bf16[16,2176]{1,0:T(8,128)(2,1)S(1)} %collective-permute-done.3.rest_3_), channel_id=1, source_target_pairs={{0,12},{4,8},{8,4},{12,0},{16,28},{20,24},{24,20},{28,16},{1,13},{... | collective-permute-start | bytes 208904 | tf_op jit(solution)/shard_map/ppermute | solution.py:245
  17.1 5.0 %collective-permute-start.5 = (bf16[16,2176]{1,0:T(8,128)(2,1)S(1)}, bf16[16,2176]{1,0:T(8,128)(2,1)S(1)}, u32[]{:S(2)}, u32[]{:S(2)}) collective-permute-start(bf16[16,2176]{1,0:T(8,128)(2,1)S(1)} %collective-permute-done.3.rest_3_), channel_id=1, source_target_pairs={{0,4},{4,0},{8,12},{12,8},{16,20},{20,16},{24,28},{28,24},{1,5},{5... | collective-permute-start | bytes 208904 | tf_op jit(solution)/shard_map/ppermute | solution.py:245
  17.7 4.5 %collective-permute-start.4 = (bf16[16,2176]{1,0:T(8,128)(2,1)S(1)}, bf16[16,2176]{1,0:T(8,128)(2,1)S(1)}, u32[]{:S(2)}, u32[]{:S(2)}) collective-permute-start(bf16[16,2176]{1,0:T(8,128)(2,1)S(1)} %collective-permute-done.3.rest_3_), channel_id=1, source_target_pairs={{0,8},{4,12},{8,0},{12,4},{16,24},{20,28},{24,16},{28,20},{1,9},{5... | collective-permute-start | bytes 208904 | tf_op jit(solution)/shard_map/ppermute | solution.py:245

commit v5 on v4

--- a/solution.py
+++ b/solution.py
@@ -101,17 +101,16 @@
     total = (totals[0] + totals[1]) + (totals[2] + totals[3])
     mean = jnp.sum(total, axis=1, keepdims=True) * (1.0 / NT)
     means[...] = jnp.broadcast_to(mean, (channels, LANES))
-    segment = jnp.concatenate(
-        [
-            (held[pl.ds(c, HIGH, stride=channels), :] - means[c : c + 1, :]) * taper
-            for c in range(channels)
-        ],
-        axis=1,
-    )
-    top, low = split(segment)
-    inner = jnp.dot(
-        first, jnp.concatenate([top, low, top], axis=0), preferred_element_type=F32
-    )
+    inner = []
+    for c in range(0, channels, 2):
+        segment = [
+            (held[pl.ds(c + i, HIGH, stride=channels), :] - means[c + i : c + i + 1, :]) * taper
+            for i in range(2)
+        ]
+        top, low = split(jnp.concatenate(segment, axis=1))
+        stacked = jnp.concatenate([top, low, top], axis=0)
+        inner.append(jnp.dot(first, stacked, preferred_element_type=F32))
+    inner = jnp.concatenate(inner, axis=1)
     lower = lax.broadcasted_iota(jnp.int32, (GRID_ROWS, LANES), 1) < HIGH
     mixed = []
     for c in range(0, channels, 2):
@@ -197,13 +196,9 @@
         meta,
         preferred_element_type=F32,
     )
-    source, receiver, hop, owner = [table[i * slots : (i + 1) * slots] for i in range(4)]
-    mine = jnp.where((owner == me.astype(F32)) & (lane < pair_slots), 1.0, 0.0)
-    above = lax.broadcasted_iota(jnp.int32, (LANES, LANES), 0)
-    below = lax.broadcasted_iota(jnp.int32, (LANES, LANES), 1)
-    earlier = jnp.where(above < below, 1.0, 0.0).astype(BF16)
-    rank = jnp.dot(mine.astype(BF16), earlier, preferred_element_type=F32)
-    chosen = jnp.where(rank == slot.astype(F32), mine, 0.0)
+    source, receiver, hop, target_row = [table[i * slots : (i + 1) * slots] for i in range(4)]
+    wanted = (me * capacity + slot).astype(F32)
+    chosen = jnp.where((target_row == wanted) & (lane < pair_slots), 1.0, 0.0)
 
     def value_of(field):
         return jnp.sum(chosen * field, axis=1, keepdims=True).astype(jnp.int32)
@@ -277,12 +272,16 @@
         compiler_params=pltpu.CompilerParams(vmem_limit_bytes=LIMIT),
         name="whiten",
     )(lax.axis_index("win").astype(jnp.int32).reshape(1), traces, offsets, table)
-    fields = [pair_source, pair_recv, pair_hop, pair_owner.reshape(1, -1)]
+    owner = pair_owner.reshape(1, -1)
+    spot = jnp.arange(pair_slots)
+    same = (pair_owner == owner) & (spot[:, None] < spot[None, :])
+    row = owner * capacity + jnp.sum(same.astype(jnp.int32), axis=0, keepdims=True)
+    fields = [pair_source, pair_recv, pair_hop, row]
     fields = sum(
         jnp.pad(field, ((i, height - 1 - i), (0, LANES - pair_slots)))
         for i, field in enumerate(fields)
     ).astype(BF16)
-    moved = [pieces[0]] + [swapped(pieces[k], "win", k) for k in range(windows - 1, 0, -1)]
+    moved = [pieces[0]] + [swapped(pieces[k], "win", k) for k in [*range(2, windows), 1]]
     packed = jnp.concatenate([fields] + moved, axis=1)
 
     gathered = {0: packed}

time: 23.8 us -> 23.7 us (level)
  waiting for transfers between devices: 4.95 us -> 4.28 us
  local copies, waits for them, and re-layouts: 0.59 us -> 1.13 us
    ppermute x10, waiting for transfers between devices: 4.95 us -> 4.28 us  [swapped(): return lax.ppermute(value, axis, [(i, i ^ bits) for i in range(peers)])]
    unnamed x11, local copies, waits for them, and re-layouts: 0.59 us -> 1.13 us
  transfers between devices with their start and end apart: 10 -> 10, of which waited for: 5 -> 6; matrix products, arithmetic and copies ran while one was open for 0% -> 0% of each run, Pallas kernels for 0% -> 0%
where the time goes in v5:
time: 23.7 us; the launch traced here: 23.5 us
  starting transfers between devices  13.8 us (58%)
  waiting for transfers between devices  4.28 us (18%)
  Pallas kernels  3.46 us (15%)
  local copies, waits for them, and re-layouts  1.13 us (5%)
  between operations  0.72 us (3%)
    ppermute x10, starting transfers between devices, swapped(): return lax.ppermute(value, axis, [(i, i ^ bits) for i in range(peers)])  13.8 us
    ppermute x10, waiting for transfers between devices, swapped(): return lax.ppermute(value, axis, [(i, i ^ bits) for i in range(peers)])  4.28 us
    pallas_call x1, Pallas kernels, local(): pl.pallas_call(whiten_kernel, out_shape=[jax.ShapeDtypeStruct((height, wi...  2.16 us
    pallas_call x1, Pallas kernels, local(): pl.pallas_call(functools.partial(stack_kernel, blocks, windows, capacity,...  1.3 us
    unnamed x11, local copies, waits for them, and re-layouts  1.13 us
  transfers between devices with their start and end apart: 10, of which 6 were waited for; matrix products, arithmetic and copies ran while one was open for 0% of the time, Pallas kernels for 0%

profile of v5, /device:TPU:0, one launch (start us, length us, event | category | flops | bytes accessed | tf_op | source)
XLA Modules:
  0.0 23.5 jit_solution(11947052338881963375)
XLA Ops:
  0.7 2.2 %whiten.1 = (bf16[16,512]{1,0:T(8,128)(2,1)S(1)}, bf16[16,512]{1,0:T(8,128)(2,1)S(1)}, bf16[16,512]{1,0:T(8,128)(2,1)S(1)}, bf16[16,512]{1,0:T(8,128)(2,1)S(1)}) custom-call(s32[1]{0:T(128)} %bitcast.4.place_ref, f32[8,12288]{1,0:T(8,128)} %traces_far.1, s32[1]{0:T(128)S(6)} %copy.14.offsets_far, f32[480,128]{1,0:T(8,128)} %constant.15.clone.table_far), custom_call_target="tpu_custom_call" | custom-call | tf_op jit(solution)/shard_map/whiten/pallas_call | solution.py:256
  2.8 3.0 %collective-permute-start = (bf16[16,512]{1,0:T(8,128)(2,1)S(1)}, bf16[16,512]{1,0:T(8,128)(2,1)S(1)}, u32[]{:S(2)}, u32[]{:S(2)}) collective-permute-start(bf16[16,512]{1,0:T(8,128)(2,1)S(1)} %get-tuple-element.10), channel_id=1, source_target_pairs={{0,2},{1,3},{2,0},{3,1},{4,6},{5,7},{6,4},{7,5},{8,10},{9,11},{10,... | collective-permute-start | bytes 49160 | tf_op jit(solution)/shard_map/ppermute | solution.py:240
  5.8 0.0 collective-permute-start.1
  5.8 0.2 collective-permute-start.2
  6.0 0.5 %copy-done.3 = s32[24,1]{0,1:T(1,128)S(1)} copy-done((s32[24,1]{0,1:T(1,128)S(1)}, s32[24,1]{0,1:T(1,128)}, u32[]{:S(2)}) %copy-start.3) | copy-done | bytes 120
  6.5 0.1 convert_reduce_fusion
  6.6 0.0 copy-start.1
  6.6 0.0 copy-start.2
  6.6 0.6 %copy-done = s32[1,24]{1,0:T(1,128)S(1)} copy-done((s32[1,24]{1,0:T(1,128)S(1)}, s32[1,24]{1,0:T(1,128)}, u32[]{:S(2)}) %copy-start) | copy-done | bytes 120
  7.2 0.0 copy-done.1
  7.2 0.0 copy-done.2
  7.3 0.3 %collective-permute-done = bf16[16,512]{1,0:T(8,128)(2,1)S(1)} collective-permute-done((bf16[16,512]{1,0:T(8,128)(2,1)S(1)}, bf16[16,512]{1,0:T(8,128)(2,1)S(1)}, u32[]{:S(2)}, u32[]{:S(2)}) %collective-permute-start) | collective-permute-done | bytes 16416 | tf_op jit(solution)/shard_map/ppermute | solution.py:240
  7.5 1.4 %collective-permute-done.1 = bf16[16,512]{1,0:T(8,128)(2,1)S(1)} collective-permute-done((bf16[16,512]{1,0:T(8,128)(2,1)S(1)}, bf16[16,512]{1,0:T(8,128)(2,1)S(1)}, u32[]{:S(2)}, u32[]{:S(2)}) %collective-permute-start.1) | collective-permute-done | bytes 16416 | tf_op jit(solution)/shard_map/ppermute | solution.py:240
  9.0 3.7 %collective-permute-start.3 = (bf16[16,2176]{1,0:T(8,128)(2,1)S(1)}, bf16[16,2176]{1,0:T(8,128)(2,1)S(1)}, u32[]{:S(2)}, u32[]{:S(2)}) collective-permute-start(bf16[16,2176]{1,0:T(8,128)(2,1)S(1)} %constant_dynamic-update-slice_fusion.rest_7_), channel_id=1, source_target_pairs={{0,24},{4,28},{8,16},{12,20},{16,8},{20,12},{24,0},{28,4},{1,25},{... | collective-permute-start | bytes 208904 | tf_op jit(solution)/shard_map/ppermute | solution.py:240
  12.7 1.5 %collective-permute-start.9 = (bf16[16,2176]{1,0:T(8,128)(2,1)S(1)}, bf16[16,2176]{1,0:T(8,128)(2,1)S(1)}, u32[]{:S(2)}, u32[]{:S(2)}) collective-permute-start(bf16[16,2176]{1,0:T(8,128)(2,1)S(1)} %constant_dynamic-update-slice_fusion.rest_7_), channel_id=1, source_target_pairs={{0,4},{4,0},{8,12},{12,8},{16,20},{20,16},{24,28},{28,24},{1,5},{5... | collective-permute-start | bytes 208904 | tf_op jit(solution)/shard_map/ppermute | solution.py:240
  14.2 2.0 %collective-permute-start.7 = (bf16[16,2176]{1,0:T(8,128)(2,1)S(1)}, bf16[16,2176]{1,0:T(8,128)(2,1)S(1)}, u32[]{:S(2)}, u32[]{:S(2)}) collective-permute-start(bf16[16,2176]{1,0:T(8,128)(2,1)S(1)} %constant_dynamic-update-slice_fusion.rest_7_), channel_id=1, source_target_pairs={{0,12},{4,8},{8,4},{12,0},{16,28},{20,24},{24,20},{28,16},{1,13},{... | collective-permute-start | bytes 208904 | tf_op jit(solution)/shard_map/ppermute | solution.py:240
  16.2 1.0 %collective-permute-start.6 = (bf16[16,2176]{1,0:T(8,128)(2,1)S(1)}, bf16[16,2176]{1,0:T(8,128)(2,1)S(1)}, u32[]{:S(2)}, u32[]{:S(2)}) collective-permute-start(bf16[16,2176]{1,0:T(8,128)(2,1)S(1)} %collective-permute-done.3.rest_3_), channel_id=1, source_target_pairs={{0,12},{4,8},{8,4},{12,0},{16,28},{20,24},{24,20},{28,16},{1,13},{... | collective-permute-start | bytes 208904 | tf_op jit(solution)/shard_map/ppermute | solution.py:240
  17.1 0.6 %collective-permute-start.5 = (bf16[16,2176]{1,0:T(8,128)(2,1)S(1)}, bf16[16,2176]{1,0:T(8,128)(2,1)S(1)}, u32[]{:S(2)}, u32[]{:S(2)}) collective-permute-start(bf16[16,2176]{1,0:T(8,128)(2,1)S(1)} %collective-permute-done.3.rest_3_), channel_id=1, source_target_pairs={{0,4},{4,0},{8,12},{12,8},{16,20},{20,16},{24,28},{28,24},{1,5},{5... | collective-permute-start | bytes 208904 | tf_op jit(solution)/shard_map/ppermute | solution.py:240
  17.7 1.9 %collective-permute-start.4 = (bf16[16,2176]{1,0:T(8,128)(2,1)S(1)}, bf16[16,2176]{1,0:T(8,128)(2,1)S(1)}, u32[]{:S(2)}, u32[]{:S(2)}) collective-permute-start(bf16[16,2176]{1,0:T(8,128)(2,1)S(1)} %collective-permute-done.3.rest_3_), channel_id=1, source_target_pairs={{0,8},{4,12},{8,0},{12,4},{16,24},{20,28},{24,16},{28,20},{1,9},{5... | collective-permute-start | bytes 208904 | tf_op jit(solution)/shard_map/ppermute | solution.py:240
  19.7 0.8 %collective-permute-done.7.rest_4_ = bf16[16,2176]{1,0:T(8,128)(2,1)S(1)} collective-permute-done((bf16[16,2176]{1,0:T(8,128)(2,1)S(1)}, bf16[16,2176]{1,0:T(8,128)(2,1)S(1)}, u32[]{:S(2)}, u32[]{:S(2)}) %collective-permute-start.7) | collective-permute-done | bytes 69664 | tf_op jit(solution)/shard_map/ppermute | solution.py:240
  20.5 1.1 %collective-permute-done.6.rest_2_ = bf16[16,2176]{1,0:T(8,128)(2,1)S(1)} collective-permute-done((bf16[16,2176]{1,0:T(8,128)(2,1)S(1)}, bf16[16,2176]{1,0:T(8,128)(2,1)S(1)}, u32[]{:S(2)}, u32[]{:S(2)}) %collective-permute-start.6) | collective-permute-done | bytes 69664 | tf_op jit(solution)/shard_map/ppermute | solution.py:240
  21.5 0.6 %collective-permute-done.5.rest_1_ = bf16[16,2176]{1,0:T(8,128)(2,1)S(1)} collective-permute-done((bf16[16,2176]{1,0:T(8,128)(2,1)S(1)}, bf16[16,2176]{1,0:T(8,128)(2,1)S(1)}, u32[]{:S(2)}, u32[]{:S(2)}) %collective-permute-start.5) | collective-permute-done | bytes 69664 | tf_op jit(solution)/shard_map/ppermute | solution.py:240
  22.2 0.1 collective-permute-done.4.rest_0_
  22.2 1.3 %stack.1 = f32[384,128]{1,0:T(8,128)} custom-call(s32[1]{0:T(128)} %bitcast.scalars, bf16[16,2176]{1,0:T(8,128)(2,1)S(1)} %collective-permute-done.4.rest_0_, bf16[16,2176]{1,0:T(8,128)(2,1)S(1)} %collective-permute-done.5.rest_1_, bf16[16,2176]{1,0:T(8,128)(2,1)S(1)} %collective-permute-done.6.rest_2_, bf16[16,2176]{1,0:T(8,128)(2,1)S(1)} %collective-permute-done.3.rest_3_, ...), custom_call_target="tpu_custom_call" | custom-call | tf_op jit(solution)/shard_map/stack/pallas_call | solution.py:298
  (13 shorter events, 0.0 us)
Async XLA Ops:
  2.8 4.7 %collective-permute-start = (bf16[16,512]{1,0:T(8,128)(2,1)S(1)}, bf16[16,512]{1,0:T(8,128)(2,1)S(1)}, u32[]{:S(2)}, u32[]{:S(2)}) collective-permute-start(bf16[16,512]{1,0:T(8,128)(2,1)S(1)} %get-tuple-element.10), channel_id=1, source_target_pairs={{0,2},{1,3},{2,0},{3,1},{4,6},{5,7},{6,4},{7,5},{8,10},{9,11},{10,... | collective-permute-start | bytes 49160 | tf_op jit(solution)/shard_map/ppermute | solution.py:240
  5.8 3.2 %collective-permute-start.1 = (bf16[16,512]{1,0:T(8,128)(2,1)S(1)}, bf16[16,512]{1,0:T(8,128)(2,1)S(1)}, u32[]{:S(2)}, u32[]{:S(2)}) collective-permute-start(bf16[16,512]{1,0:T(8,128)(2,1)S(1)} %get-tuple-element.11), channel_id=1, source_target_pairs={{0,3},{1,2},{2,1},{3,0},{4,7},{5,6},{6,5},{7,4},{8,11},{9,10},{10,... | collective-permute-start | bytes 49160 | tf_op jit(solution)/shard_map/ppermute | solution.py:240
  5.8 0.7 %copy-start.3 = (s32[24,1]{0,1:T(1,128)S(1)}, s32[24,1]{0,1:T(1,128)}, u32[]{:S(2)}) copy-start(s32[24,1]{0,1:T(1,128)} %param.12) | copy-start | bytes 292
  5.8 3.2 %collective-permute-start.2 = (bf16[16,512]{1,0:T(8,128)(2,1)S(1)}, bf16[16,512]{1,0:T(8,128)(2,1)S(1)}, u32[]{:S(2)}, u32[]{:S(2)}) collective-permute-start(bf16[16,512]{1,0:T(8,128)(2,1)S(1)} %get-tuple-element.12), channel_id=1, source_target_pairs={{0,1},{1,0},{2,3},{3,2},{4,5},{5,4},{6,7},{7,6},{8,9},{9,8},{10,11... | collective-permute-start | bytes 49160 | tf_op jit(solution)/shard_map/ppermute | solution.py:240
  6.6 0.7 %copy-start = (s32[1,24]{1,0:T(1,128)S(1)}, s32[1,24]{1,0:T(1,128)}, u32[]{:S(2)}) copy-start(s32[1,24]{1,0:T(1,128)} %param.11) | copy-start | bytes 292
  6.6 0.7 %copy-start.1 = (s32[1,24]{1,0:T(1,128)S(1)}, s32[1,24]{1,0:T(1,128)}, u32[]{:S(2)}) copy-start(s32[1,24]{1,0:T(1,128)} %param.10) | copy-start | bytes 292
  6.6 0.7 %copy-start.2 = (s32[1,24]{1,0:T(1,128)S(1)}, s32[1,24]{1,0:T(1,128)}, u32[]{:S(2)}) copy-start(s32[1,24]{1,0:T(1,128)} %param.9) | copy-start | bytes 292
  9.0 7.2 %collective-permute-start.3 = (bf16[16,2176]{1,0:T(8,128)(2,1)S(1)}, bf16[16,2176]{1,0:T(8,128)(2,1)S(1)}, u32[]{:S(2)}, u32[]{:S(2)}) collective-permute-start(bf16[16,2176]{1,0:T(8,128)(2,1)S(1)} %constant_dynamic-update-slice_fusion.rest_7_), channel_id=1, source_target_pairs={{0,24},{4,28},{8,16},{12,20},{16,8},{20,12},{24,0},{28,4},{1,25},{... | collective-permute-start | bytes 208904 | tf_op jit(solution)/shard_map/ppermute | solution.py:240
  12.7 5.0 %collective-permute-start.9 = (bf16[16,2176]{1,0:T(8,128)(2,1)S(1)}, bf16[16,2176]{1,0:T(8,128)(2,1)S(1)}, u32[]{:S(2)}, u32[]{:S(2)}) collective-permute-start(bf16[16,2176]{1,0:T(8,128)(2,1)S(1)} %constant_dynamic-update-slice_fusion.rest_7_), channel_id=1, source_target_pairs={{0,4},{4,0},{8,12},{12,8},{16,20},{20,16},{24,28},{28,24},{1,5},{5... | collective-permute-start | bytes 208904 | tf_op jit(solution)/shard_map/ppermute | solution.py:240
  14.2 5.5 %collective-permute-start.8 = (bf16[16,2176]{1,0:T(8,128)(2,1)S(1)}, bf16[16,2176]{1,0:T(8,128)(2,1)S(1)}, u32[]{:S(2)}, u32[]{:S(2)}) collective-permute-start(bf16[16,2176]{1,0:T(8,128)(2,1)S(1)} %constant_dynamic-update-slice_fusion.rest_7_), channel_id=1, source_target_pairs={{0,8},{4,12},{8,0},{12,4},{16,24},{20,28},{24,16},{28,20},{1,9},{5... | collective-permute-start | bytes 208904 | tf_op jit(solution)/shard_map/ppermute | solution.py:240
  14.2 6.3 %collective-permute-start.7 = (bf16[16,2176]{1,0:T(8,128)(2,1)S(1)}, bf16[16,2176]{1,0:T(8,128)(2,1)S(1)}, u32[]{:S(2)}, u32[]{:S(2)}) collective-permute-start(bf16[16,2176]{1,0:T(8,128)(2,1)S(1)} %constant_dynamic-update-slice_fusion.rest_7_), channel_id=1, source_target_pairs={{0,12},{4,8},{8,4},{12,0},{16,28},{20,24},{24,20},{28,16},{1,13},{... | collective-permute-start | bytes 208904 | tf_op jit(solution)/shard_map/ppermute | solution.py:240
  16.2 5.4 %collective-permute-start.6 = (bf16[16,2176]{1,0:T(8,128)(2,1)S(1)}, bf16[16,2176]{1,0:T(8,128)(2,1)S(1)}, u32[]{:S(2)}, u32[]{:S(2)}) collective-permute-start(bf16[16,2176]{1,0:T(8,128)(2,1)S(1)} %collective-permute-done.3.rest_3_), channel_id=1, source_target_pairs={{0,12},{4,8},{8,4},{12,0},{16,28},{20,24},{24,20},{28,16},{1,13},{... | collective-permute-start | bytes 208904 | tf_op jit(solution)/shard_map/ppermute | solution.py:240
  17.1 5.1 %collective-permute-start.5 = (bf16[16,2176]{1,0:T(8,128)(2,1)S(1)}, bf16[16,2176]{1,0:T(8,128)(2,1)S(1)}, u32[]{:S(2)}, u32[]{:S(2)}) collective-permute-start(bf16[16,2176]{1,0:T(8,128)(2,1)S(1)} %collective-permute-done.3.rest_3_), channel_id=1, source_target_pairs={{0,4},{4,0},{8,12},{12,8},{16,20},{20,16},{24,28},{28,24},{1,5},{5... | collective-permute-start | bytes 208904 | tf_op jit(solution)/shard_map/ppermute | solution.py:240
  17.7 4.5 %collective-permute-start.4 = (bf16[16,2176]{1,0:T(8,128)(2,1)S(1)}, bf16[16,2176]{1,0:T(8,128)(2,1)S(1)}, u32[]{:S(2)}, u32[]{:S(2)}) collective-permute-start(bf16[16,2176]{1,0:T(8,128)(2,1)S(1)} %collective-permute-done.3.rest_3_), channel_id=1, source_target_pairs={{0,8},{4,12},{8,0},{12,4},{16,24},{20,28},{24,16},{28,20},{1,9},{5... | collective-permute-start | bytes 208904 | tf_op jit(solution)/shard_map/ppermute | solution.py:240

commit v6 on v5

--- a/solution.py
+++ b/solution.py
@@ -164,7 +164,7 @@
 
 
 def stack_kernel(blocks, windows, capacity, reach, pair_slots, width, order, scalars, *rest):
-    pieces, out = rest[:-1], rest[-1]
+    pieces, (far_out, out, sent) = rest[:-3], rest[-3:]
     me = scalars[0]
     height = pieces[0].shape[0]
     channels = height // 2
@@ -185,14 +185,15 @@
     slot = row - block * capacity
 
     def pick(index, size):
-        spot = lax.broadcasted_iota(jnp.int32, (slots, size), 1)
-        index = jnp.concatenate([index] * (size // LANES), axis=1)
-        return jnp.where(spot == index, 1.0, 0.0).astype(BF16)
+        spot = lax.broadcasted_iota(jnp.int32, (index.shape[0], size), 1)
+        if index.shape[1] > 1:
+            index = jnp.concatenate([index] * (size // LANES), axis=1)
+        return jnp.where(spot == index, 1.0, 0.0)
 
     base = (block ^ me) * height
     depth = blocks * height
     table = jnp.dot(
-        jnp.concatenate([pick(base + i, depth) for i in range(4)], axis=0),
+        jnp.concatenate([pick(base + i, depth) for i in range(4)], axis=0).astype(BF16),
         meta,
         preferred_element_type=F32,
     )
@@ -211,28 +212,35 @@
     receiver_row = (target ^ me) * height + value_of(receiver)
     source_row = jnp.where(filled, source_row, -depth)
     receiver_row = jnp.where(filled, receiver_row, -depth)
-    choice = jnp.concatenate(
-        [
-            pick(source_row, depth),
-            pick(source_row + channels, depth),
-            pick(receiver_row, depth),
-            pick(receiver_row + channels, depth),
-        ],
-        axis=0,
-    )
-    real = jnp.zeros((slots, width), F32)
-    imag = jnp.zeros((slots, width), F32)
-    for w in range(windows):
-        white = lanes_of(LANES + w * width, width)
-        rows = jnp.dot(choice, white, preferred_element_type=F32)
-        sr, si, rr, ri = [rows[i * slots : (i + 1) * slots] for i in range(4)]
-        real += sr * rr + si * ri
-        imag += sr * ri - si * rr
+    rows_of = [source_row, source_row + channels, receiver_row, receiver_row + channels]
     parts = width // LANES
-    for i in range(parts):
-        lanes = slice(i * LANES, (i + 1) * LANES)
-        out[pl.ds(2 * i, slots, stride=2 * parts), :] = real[:, lanes]
-        out[pl.ds(2 * i + 1, slots, stride=2 * parts), :] = imag[:, lanes]
+    half = slots // 2
+    copies = []
+    for first in (0, half):
+        choice = [pick(index[first : first + half, :1], depth) for index in rows_of]
+        choice = jnp.concatenate(choice, axis=0).astype(BF16)
+        real = jnp.zeros((half, width), F32)
+        imag = jnp.zeros((half, width), F32)
+        for w in range(windows):
+            white = lanes_of(LANES + w * width, width)
+            rows = jnp.dot(choice, white, preferred_element_type=F32)
+            sr, si, rr, ri = [rows[i * half : (i + 1) * half] for i in range(4)]
+            real += sr * rr + si * ri
+            imag += sr * ri - si * rr
+        at = 2 * parts * first
+        for i in range(parts):
+            lanes = slice(i * LANES, (i + 1) * LANES)
+            out[pl.ds(at + 2 * i, half, stride=2 * parts), :] = real[:, lanes]
+            out[pl.ds(at + 2 * i + 1, half, stride=2 * parts), :] = imag[:, lanes]
+        size = 2 * parts * half
+        copies.append(
+            pltpu.make_async_copy(
+                out.at[pl.ds(at, size)], far_out.at[pl.ds(at, size)], sent.at[len(copies)]
+            )
+        )
+        copies[-1].start()
+    for copy in copies:
+        copy.wait()
 
 
 def swapped(value, axis, bits):
@@ -301,7 +309,11 @@
         ),
         out_shape=jax.ShapeDtypeStruct((blocks * capacity * 2 * width // LANES, LANES), F32),
         in_specs=[smem] + [vmem] * blocks,
-        out_specs=vmem,
+        out_specs=pl.BlockSpec(memory_space=pltpu.HBM),
+        scratch_shapes=[
+            pltpu.VMEM((blocks * capacity * 2 * width // LANES, LANES), F32),
+            pltpu.SemaphoreType.DMA((2,)),
+        ],
         compiler_params=pltpu.CompilerParams(vmem_limit_bytes=32 << 20),
         name="stack",
     )(lax.axis_index("chan").astype(jnp.int32).reshape(1), *[gathered[k] for k in order])

time: 23.7 us -> 23.7 us (level)
  no operation moved by 1% of the time
where the time goes in v6:
time: 23.7 us; the launch traced here: 23.5 us
  starting transfers between devices  13.8 us (58%)
  waiting for transfers between devices  4.28 us (18%)
  Pallas kernels  3.42 us (14%)
  local copies, waits for them, and re-layouts  1.13 us (5%)
  between operations  0.72 us (3%)
    ppermute x10, starting transfers between devices, swapped(): return lax.ppermute(value, axis, [(i, i ^ bits) for i in range(peers)])  13.8 us
    ppermute x10, waiting for transfers between devices, swapped(): return lax.ppermute(value, axis, [(i, i ^ bits) for i in range(peers)])  4.28 us
    pallas_call x1, Pallas kernels, local(): pl.pallas_call(whiten_kernel, out_shape=[jax.ShapeDtypeStruct((height, wi...  2.16 us
    pallas_call x1, Pallas kernels, local(): pl.pallas_call(functools.partial(stack_kernel, blocks, windows, capacity,...  1.27 us
    unnamed x11, local copies, waits for them, and re-layouts  1.13 us
  transfers between devices with their start and end apart: 10, of which 6 were waited for; matrix products, arithmetic and copies ran while one was open for 0% of the time, Pallas kernels for 0%

profile of v6, /device:TPU:0, one launch (start us, length us, event | category | flops | bytes accessed | tf_op | source)
XLA Modules:
  0.0 23.5 jit_solution(11931063250767068342)
XLA Ops:
  0.7 2.2 %whiten.1 = (bf16[16,512]{1,0:T(8,128)(2,1)S(1)}, bf16[16,512]{1,0:T(8,128)(2,1)S(1)}, bf16[16,512]{1,0:T(8,128)(2,1)S(1)}, bf16[16,512]{1,0:T(8,128)(2,1)S(1)}) custom-call(s32[1]{0:T(128)} %bitcast.4.place_ref, f32[8,12288]{1,0:T(8,128)} %traces_far.1, s32[1]{0:T(128)S(6)} %copy.14.offsets_far, f32[480,128]{1,0:T(8,128)} %constant.15.clone.table_far), custom_call_target="tpu_custom_call" | custom-call | tf_op jit(solution)/shard_map/whiten/pallas_call | solution.py:264
  2.8 3.0 %collective-permute-start = (bf16[16,512]{1,0:T(8,128)(2,1)S(1)}, bf16[16,512]{1,0:T(8,128)(2,1)S(1)}, u32[]{:S(2)}, u32[]{:S(2)}) collective-permute-start(bf16[16,512]{1,0:T(8,128)(2,1)S(1)} %get-tuple-element.10), channel_id=1, source_target_pairs={{0,2},{1,3},{2,0},{3,1},{4,6},{5,7},{6,4},{7,5},{8,10},{9,11},{10,... | collective-permute-start | bytes 49160 | tf_op jit(solution)/shard_map/ppermute | solution.py:248
  5.8 0.0 collective-permute-start.1
  5.8 0.2 collective-permute-start.2
  6.0 0.5 %copy-done.3 = s32[24,1]{0,1:T(1,128)S(1)} copy-done((s32[24,1]{0,1:T(1,128)S(1)}, s32[24,1]{0,1:T(1,128)}, u32[]{:S(2)}) %copy-start.3) | copy-done | bytes 120
  6.5 0.1 convert_reduce_fusion
  6.6 0.0 copy-start.1
  6.6 0.0 copy-start.2
  6.6 0.6 %copy-done = s32[1,24]{1,0:T(1,128)S(1)} copy-done((s32[1,24]{1,0:T(1,128)S(1)}, s32[1,24]{1,0:T(1,128)}, u32[]{:S(2)}) %copy-start) | copy-done | bytes 120
  7.2 0.0 copy-done.1
  7.2 0.0 copy-done.2
  7.3 0.3 %collective-permute-done = bf16[16,512]{1,0:T(8,128)(2,1)S(1)} collective-permute-done((bf16[16,512]{1,0:T(8,128)(2,1)S(1)}, bf16[16,512]{1,0:T(8,128)(2,1)S(1)}, u32[]{:S(2)}, u32[]{:S(2)}) %collective-permute-start) | collective-permute-done | bytes 16416 | tf_op jit(solution)/shard_map/ppermute | solution.py:248
  7.5 1.4 %collective-permute-done.1 = bf16[16,512]{1,0:T(8,128)(2,1)S(1)} collective-permute-done((bf16[16,512]{1,0:T(8,128)(2,1)S(1)}, bf16[16,512]{1,0:T(8,128)(2,1)S(1)}, u32[]{:S(2)}, u32[]{:S(2)}) %collective-permute-start.1) | collective-permute-done | bytes 16416 | tf_op jit(solution)/shard_map/ppermute | solution.py:248
  9.0 3.7 %collective-permute-start.3 = (bf16[16,2176]{1,0:T(8,128)(2,1)S(1)}, bf16[16,2176]{1,0:T(8,128)(2,1)S(1)}, u32[]{:S(2)}, u32[]{:S(2)}) collective-permute-start(bf16[16,2176]{1,0:T(8,128)(2,1)S(1)} %constant_dynamic-update-slice_fusion.rest_7_), channel_id=1, source_target_pairs={{0,24},{4,28},{8,16},{12,20},{16,8},{20,12},{24,0},{28,4},{1,25},{... | collective-permute-start | bytes 208904 | tf_op jit(solution)/shard_map/ppermute | solution.py:248
  12.7 1.5 %collective-permute-start.9 = (bf16[16,2176]{1,0:T(8,128)(2,1)S(1)}, bf16[16,2176]{1,0:T(8,128)(2,1)S(1)}, u32[]{:S(2)}, u32[]{:S(2)}) collective-permute-start(bf16[16,2176]{1,0:T(8,128)(2,1)S(1)} %constant_dynamic-update-slice_fusion.rest_7_), channel_id=1, source_target_pairs={{0,4},{4,0},{8,12},{12,8},{16,20},{20,16},{24,28},{28,24},{1,5},{5... | collective-permute-start | bytes 208904 | tf_op jit(solution)/shard_map/ppermute | solution.py:248
  14.2 2.0 %collective-permute-start.7 = (bf16[16,2176]{1,0:T(8,128)(2,1)S(1)}, bf16[16,2176]{1,0:T(8,128)(2,1)S(1)}, u32[]{:S(2)}, u32[]{:S(2)}) collective-permute-start(bf16[16,2176]{1,0:T(8,128)(2,1)S(1)} %constant_dynamic-update-slice_fusion.rest_7_), channel_id=1, source_target_pairs={{0,12},{4,8},{8,4},{12,0},{16,28},{20,24},{24,20},{28,16},{1,13},{... | collective-permute-start | bytes 208904 | tf_op jit(solution)/shard_map/ppermute | solution.py:248
  16.2 1.0 %collective-permute-start.6 = (bf16[16,2176]{1,0:T(8,128)(2,1)S(1)}, bf16[16,2176]{1,0:T(8,128)(2,1)S(1)}, u32[]{:S(2)}, u32[]{:S(2)}) collective-permute-start(bf16[16,2176]{1,0:T(8,128)(2,1)S(1)} %collective-permute-done.3.rest_3_), channel_id=1, source_target_pairs={{0,12},{4,8},{8,4},{12,0},{16,28},{20,24},{24,20},{28,16},{1,13},{... | collective-permute-start | bytes 208904 | tf_op jit(solution)/shard_map/ppermute | solution.py:248
  17.1 0.6 %collective-permute-start.5 = (bf16[16,2176]{1,0:T(8,128)(2,1)S(1)}, bf16[16,2176]{1,0:T(8,128)(2,1)S(1)}, u32[]{:S(2)}, u32[]{:S(2)}) collective-permute-start(bf16[16,2176]{1,0:T(8,128)(2,1)S(1)} %collective-permute-done.3.rest_3_), channel_id=1, source_target_pairs={{0,4},{4,0},{8,12},{12,8},{16,20},{20,16},{24,28},{28,24},{1,5},{5... | collective-permute-start | bytes 208904 | tf_op jit(solution)/shard_map/ppermute | solution.py:248
  17.7 1.9 %collective-permute-start.4 = (bf16[16,2176]{1,0:T(8,128)(2,1)S(1)}, bf16[16,2176]{1,0:T(8,128)(2,1)S(1)}, u32[]{:S(2)}, u32[]{:S(2)}) collective-permute-start(bf16[16,2176]{1,0:T(8,128)(2,1)S(1)} %collective-permute-done.3.rest_3_), channel_id=1, source_target_pairs={{0,8},{4,12},{8,0},{12,4},{16,24},{20,28},{24,16},{28,20},{1,9},{5... | collective-permute-start | bytes 208904 | tf_op jit(solution)/shard_map/ppermute | solution.py:248
  19.7 0.8 %collective-permute-done.7.rest_4_ = bf16[16,2176]{1,0:T(8,128)(2,1)S(1)} collective-permute-done((bf16[16,2176]{1,0:T(8,128)(2,1)S(1)}, bf16[16,2176]{1,0:T(8,128)(2,1)S(1)}, u32[]{:S(2)}, u32[]{:S(2)}) %collective-permute-start.7) | collective-permute-done | bytes 69664 | tf_op jit(solution)/shard_map/ppermute | solution.py:248
  20.5 1.1 %collective-permute-done.6.rest_2_ = bf16[16,2176]{1,0:T(8,128)(2,1)S(1)} collective-permute-done((bf16[16,2176]{1,0:T(8,128)(2,1)S(1)}, bf16[16,2176]{1,0:T(8,128)(2,1)S(1)}, u32[]{:S(2)}, u32[]{:S(2)}) %collective-permute-start.6) | collective-permute-done | bytes 69664 | tf_op jit(solution)/shard_map/ppermute | solution.py:248
  21.5 0.6 %collective-permute-done.5.rest_1_ = bf16[16,2176]{1,0:T(8,128)(2,1)S(1)} collective-permute-done((bf16[16,2176]{1,0:T(8,128)(2,1)S(1)}, bf16[16,2176]{1,0:T(8,128)(2,1)S(1)}, u32[]{:S(2)}, u32[]{:S(2)}) %collective-permute-start.5) | collective-permute-done | bytes 69664 | tf_op jit(solution)/shard_map/ppermute | solution.py:248
  22.2 0.1 collective-permute-done.4.rest_0_
  22.2 1.3 %stack.1 = f32[384,128]{1,0:T(8,128)} custom-call(s32[1]{0:T(128)} %bitcast.scalars, bf16[16,2176]{1,0:T(8,128)(2,1)S(1)} %collective-permute-done.4.rest_0_, bf16[16,2176]{1,0:T(8,128)(2,1)S(1)} %collective-permute-done.5.rest_1_, bf16[16,2176]{1,0:T(8,128)(2,1)S(1)} %collective-permute-done.6.rest_2_, bf16[16,2176]{1,0:T(8,128)(2,1)S(1)} %collective-permute-done.3.rest_3_, ...), custom_call_target="tpu_custom_call" | custom-call | tf_op jit(solution)/shard_map/stack/pallas_call | solution.py:306
  (13 shorter events, 0.0 us)
Async XLA Ops:
  2.8 4.7 %collective-permute-start = (bf16[16,512]{1,0:T(8,128)(2,1)S(1)}, bf16[16,512]{1,0:T(8,128)(2,1)S(1)}, u32[]{:S(2)}, u32[]{:S(2)}) collective-permute-start(bf16[16,512]{1,0:T(8,128)(2,1)S(1)} %get-tuple-element.10), channel_id=1, source_target_pairs={{0,2},{1,3},{2,0},{3,1},{4,6},{5,7},{6,4},{7,5},{8,10},{9,11},{10,... | collective-permute-start | bytes 49160 | tf_op jit(solution)/shard_map/ppermute | solution.py:248
  5.8 3.2 %collective-permute-start.1 = (bf16[16,512]{1,0:T(8,128)(2,1)S(1)}, bf16[16,512]{1,0:T(8,128)(2,1)S(1)}, u32[]{:S(2)}, u32[]{:S(2)}) collective-permute-start(bf16[16,512]{1,0:T(8,128)(2,1)S(1)} %get-tuple-element.11), channel_id=1, source_target_pairs={{0,3},{1,2},{2,1},{3,0},{4,7},{5,6},{6,5},{7,4},{8,11},{9,10},{10,... | collective-permute-start | bytes 49160 | tf_op jit(solution)/shard_map/ppermute | solution.py:248
  5.8 0.7 %copy-start.3 = (s32[24,1]{0,1:T(1,128)S(1)}, s32[24,1]{0,1:T(1,128)}, u32[]{:S(2)}) copy-start(s32[24,1]{0,1:T(1,128)} %param.12) | copy-start | bytes 292
  5.8 3.2 %collective-permute-start.2 = (bf16[16,512]{1,0:T(8,128)(2,1)S(1)}, bf16[16,512]{1,0:T(8,128)(2,1)S(1)}, u32[]{:S(2)}, u32[]{:S(2)}) collective-permute-start(bf16[16,512]{1,0:T(8,128)(2,1)S(1)} %get-tuple-element.12), channel_id=1, source_target_pairs={{0,1},{1,0},{2,3},{3,2},{4,5},{5,4},{6,7},{7,6},{8,9},{9,8},{10,11... | collective-permute-start | bytes 49160 | tf_op jit(solution)/shard_map/ppermute | solution.py:248
  6.6 0.7 %copy-start = (s32[1,24]{1,0:T(1,128)S(1)}, s32[1,24]{1,0:T(1,128)}, u32[]{:S(2)}) copy-start(s32[1,24]{1,0:T(1,128)} %param.11) | copy-start | bytes 292
  6.6 0.7 %copy-start.1 = (s32[1,24]{1,0:T(1,128)S(1)}, s32[1,24]{1,0:T(1,128)}, u32[]{:S(2)}) copy-start(s32[1,24]{1,0:T(1,128)} %param.10) | copy-start | bytes 292
  6.6 0.7 %copy-start.2 = (s32[1,24]{1,0:T(1,128)S(1)}, s32[1,24]{1,0:T(1,128)}, u32[]{:S(2)}) copy-start(s32[1,24]{1,0:T(1,128)} %param.9) | copy-start | bytes 292
  9.0 7.2 %collective-permute-start.3 = (bf16[16,2176]{1,0:T(8,128)(2,1)S(1)}, bf16[16,2176]{1,0:T(8,128)(2,1)S(1)}, u32[]{:S(2)}, u32[]{:S(2)}) collective-permute-start(bf16[16,2176]{1,0:T(8,128)(2,1)S(1)} %constant_dynamic-update-slice_fusion.rest_7_), channel_id=1, source_target_pairs={{0,24},{4,28},{8,16},{12,20},{16,8},{20,12},{24,0},{28,4},{1,25},{... | collective-permute-start | bytes 208904 | tf_op jit(solution)/shard_map/ppermute | solution.py:248
  12.7 5.0 %collective-permute-start.9 = (bf16[16,2176]{1,0:T(8,128)(2,1)S(1)}, bf16[16,2176]{1,0:T(8,128)(2,1)S(1)}, u32[]{:S(2)}, u32[]{:S(2)}) collective-permute-start(bf16[16,2176]{1,0:T(8,128)(2,1)S(1)} %constant_dynamic-update-slice_fusion.rest_7_), channel_id=1, source_target_pairs={{0,4},{4,0},{8,12},{12,8},{16,20},{20,16},{24,28},{28,24},{1,5},{5... | collective-permute-start | bytes 208904 | tf_op jit(solution)/shard_map/ppermute | solution.py:248
  14.2 5.5 %collective-permute-start.8 = (bf16[16,2176]{1,0:T(8,128)(2,1)S(1)}, bf16[16,2176]{1,0:T(8,128)(2,1)S(1)}, u32[]{:S(2)}, u32[]{:S(2)}) collective-permute-start(bf16[16,2176]{1,0:T(8,128)(2,1)S(1)} %constant_dynamic-update-slice_fusion.rest_7_), channel_id=1, source_target_pairs={{0,8},{4,12},{8,0},{12,4},{16,24},{20,28},{24,16},{28,20},{1,9},{5... | collective-permute-start | bytes 208904 | tf_op jit(solution)/shard_map/ppermute | solution.py:248
  14.2 6.3 %collective-permute-start.7 = (bf16[16,2176]{1,0:T(8,128)(2,1)S(1)}, bf16[16,2176]{1,0:T(8,128)(2,1)S(1)}, u32[]{:S(2)}, u32[]{:S(2)}) collective-permute-start(bf16[16,2176]{1,0:T(8,128)(2,1)S(1)} %constant_dynamic-update-slice_fusion.rest_7_), channel_id=1, source_target_pairs={{0,12},{4,8},{8,4},{12,0},{16,28},{20,24},{24,20},{28,16},{1,13},{... | collective-permute-start | bytes 208904 | tf_op jit(solution)/shard_map/ppermute | solution.py:248
  16.2 5.4 %collective-permute-start.6 = (bf16[16,2176]{1,0:T(8,128)(2,1)S(1)}, bf16[16,2176]{1,0:T(8,128)(2,1)S(1)}, u32[]{:S(2)}, u32[]{:S(2)}) collective-permute-start(bf16[16,2176]{1,0:T(8,128)(2,1)S(1)} %collective-permute-done.3.rest_3_), channel_id=1, source_target_pairs={{0,12},{4,8},{8,4},{12,0},{16,28},{20,24},{24,20},{28,16},{1,13},{... | collective-permute-start | bytes 208904 | tf_op jit(solution)/shard_map/ppermute | solution.py:248
  17.1 5.1 %collective-permute-start.5 = (bf16[16,2176]{1,0:T(8,128)(2,1)S(1)}, bf16[16,2176]{1,0:T(8,128)(2,1)S(1)}, u32[]{:S(2)}, u32[]{:S(2)}) collective-permute-start(bf16[16,2176]{1,0:T(8,128)(2,1)S(1)} %collective-permute-done.3.rest_3_), channel_id=1, source_target_pairs={{0,4},{4,0},{8,12},{12,8},{16,20},{20,16},{24,28},{28,24},{1,5},{5... | collective-permute-start | bytes 208904 | tf_op jit(solution)/shard_map/ppermute | solution.py:248
  17.7 4.5 %collective-permute-start.4 = (bf16[16,2176]{1,0:T(8,128)(2,1)S(1)}, bf16[16,2176]{1,0:T(8,128)(2,1)S(1)}, u32[]{:S(2)}, u32[]{:S(2)}) collective-permute-start(bf16[16,2176]{1,0:T(8,128)(2,1)S(1)} %collective-permute-done.3.rest_3_), channel_id=1, source_target_pairs={{0,8},{4,12},{8,0},{12,4},{16,24},{20,28},{24,16},{28,20},{1,9},{5... | collective-permute-start | bytes 208904 | tf_op jit(solution)/shard_map/ppermute | solution.py:248

commit v7 on v6

--- a/solution.py
+++ b/solution.py
@@ -147,10 +147,14 @@
     tail = jnp.where(lane < SMOOTH_HALF, power[live - channels :], 0.0)
     power = jnp.concatenate([head, power[channels : live - channels], tail], axis=0)
     count = ROWS * channels
-    level = jnp.zeros((count, LANES), F32)
-    for part in split(power):
-        around = [part[i * channels : i * channels + count] for i in range(3)]
-        level += jnp.dot(jnp.concatenate(around, axis=1), band, preferred_element_type=F32)
+    around = [
+        part[i * channels : i * channels + count] for part in split(power) for i in range(3)
+    ]
+    level = jnp.dot(
+        jnp.concatenate(around, axis=1),
+        jnp.concatenate([band, band], axis=0),
+        preferred_element_type=F32,
+    )
     scale = lax.rsqrt(level + 1e-06)
     kept_real = real[channels : channels + count] * scale
     kept_imag = imag[channels : channels + count] * scale

time: 23.7 us -> 23.7 us (level)
  no operation moved by 1% of the time
where the time goes in v7:
time: 23.7 us; the launch traced here: 23.5 us
  starting transfers between devices  13.8 us (58%)
  waiting for transfers between devices  4.28 us (18%)
  Pallas kernels  3.42 us (14%)
  local copies, waits for them, and re-layouts  1.13 us (5%)
  between operations  0.72 us (3%)
    ppermute x10, starting transfers between devices, swapped(): return lax.ppermute(value, axis, [(i, i ^ bits) for i in range(peers)])  13.8 us
    ppermute x10, waiting for transfers between devices, swapped(): return lax.ppermute(value, axis, [(i, i ^ bits) for i in range(peers)])  4.28 us
    pallas_call x1, Pallas kernels, local(): pl.pallas_call(whiten_kernel, out_shape=[jax.ShapeDtypeStruct((height, wi...  2.15 us
    pallas_call x1, Pallas kernels, local(): pl.pallas_call(functools.partial(stack_kernel, blocks, windows, capacity,...  1.27 us
    unnamed x11, local copies, waits for them, and re-layouts  1.13 us
  transfers between devices with their start and end apart: 10, of which 6 were waited for; matrix products, arithmetic and copies ran while one was open for 0% of the time, Pallas kernels for 0%

profile of v7, /device:TPU:0, one launch (start us, length us, event | category | flops | bytes accessed | tf_op | source)
XLA Modules:
  0.0 23.5 jit_solution(1802211114237865788)
XLA Ops:
  0.7 2.2 %whiten.1 = (bf16[16,512]{1,0:T(8,128)(2,1)S(1)}, bf16[16,512]{1,0:T(8,128)(2,1)S(1)}, bf16[16,512]{1,0:T(8,128)(2,1)S(1)}, bf16[16,512]{1,0:T(8,128)(2,1)S(1)}) custom-call(s32[1]{0:T(128)} %bitcast.4.place_ref, f32[8,12288]{1,0:T(8,128)} %traces_far.1, s32[1]{0:T(128)S(6)} %copy.14.offsets_far, f32[480,128]{1,0:T(8,128)} %constant.15.clone.table_far), custom_call_target="tpu_custom_call" | custom-call | tf_op jit(solution)/shard_map/whiten/pallas_call | solution.py:268
  2.8 3.0 %collective-permute-start = (bf16[16,512]{1,0:T(8,128)(2,1)S(1)}, bf16[16,512]{1,0:T(8,128)(2,1)S(1)}, u32[]{:S(2)}, u32[]{:S(2)}) collective-permute-start(bf16[16,512]{1,0:T(8,128)(2,1)S(1)} %get-tuple-element.10), channel_id=1, source_target_pairs={{0,2},{1,3},{2,0},{3,1},{4,6},{5,7},{6,4},{7,5},{8,10},{9,11},{10,... | collective-permute-start | bytes 49160 | tf_op jit(solution)/shard_map/ppermute | solution.py:252
  5.8 0.2 collective-permute-start.2
  6.0 0.5 %copy-done.3 = s32[24,1]{0,1:T(1,128)S(1)} copy-done((s32[24,1]{0,1:T(1,128)S(1)}, s32[24,1]{0,1:T(1,128)}, u32[]{:S(2)}) %copy-start.3) | copy-done | bytes 120
  6.5 0.1 convert_reduce_fusion
  6.6 0.0 copy-start.1
  6.6 0.0 copy-start.2
  6.6 0.6 %copy-done = s32[1,24]{1,0:T(1,128)S(1)} copy-done((s32[1,24]{1,0:T(1,128)S(1)}, s32[1,24]{1,0:T(1,128)}, u32[]{:S(2)}) %copy-start) | copy-done | bytes 120
  7.2 0.0 copy-done.1
  7.2 0.0 copy-done.2
  7.3 0.3 %collective-permute-done = bf16[16,512]{1,0:T(8,128)(2,1)S(1)} collective-permute-done((bf16[16,512]{1,0:T(8,128)(2,1)S(1)}, bf16[16,512]{1,0:T(8,128)(2,1)S(1)}, u32[]{:S(2)}, u32[]{:S(2)}) %collective-permute-start) | collective-permute-done | bytes 16416 | tf_op jit(solution)/shard_map/ppermute | solution.py:252
  7.5 1.4 %collective-permute-done.1 = bf16[16,512]{1,0:T(8,128)(2,1)S(1)} collective-permute-done((bf16[16,512]{1,0:T(8,128)(2,1)S(1)}, bf16[16,512]{1,0:T(8,128)(2,1)S(1)}, u32[]{:S(2)}, u32[]{:S(2)}) %collective-permute-start.1) | collective-permute-done | bytes 16416 | tf_op jit(solution)/shard_map/ppermute | solution.py:252
  9.0 0.0 collective-permute-done.2
  9.0 3.7 %collective-permute-start.3 = (bf16[16,2176]{1,0:T(8,128)(2,1)S(1)}, bf16[16,2176]{1,0:T(8,128)(2,1)S(1)}, u32[]{:S(2)}, u32[]{:S(2)}) collective-permute-start(bf16[16,2176]{1,0:T(8,128)(2,1)S(1)} %constant_dynamic-update-slice_fusion.rest_7_), channel_id=1, source_target_pairs={{0,24},{4,28},{8,16},{12,20},{16,8},{20,12},{24,0},{28,4},{1,25},{... | collective-permute-start | bytes 208904 | tf_op jit(solution)/shard_map/ppermute | solution.py:252
  12.7 1.5 %collective-permute-start.9 = (bf16[16,2176]{1,0:T(8,128)(2,1)S(1)}, bf16[16,2176]{1,0:T(8,128)(2,1)S(1)}, u32[]{:S(2)}, u32[]{:S(2)}) collective-permute-start(bf16[16,2176]{1,0:T(8,128)(2,1)S(1)} %constant_dynamic-update-slice_fusion.rest_7_), channel_id=1, source_target_pairs={{0,4},{4,0},{8,12},{12,8},{16,20},{20,16},{24,28},{28,24},{1,5},{5... | collective-permute-start | bytes 208904 | tf_op jit(solution)/shard_map/ppermute | solution.py:252
  14.2 2.0 %collective-permute-start.7 = (bf16[16,2176]{1,0:T(8,128)(2,1)S(1)}, bf16[16,2176]{1,0:T(8,128)(2,1)S(1)}, u32[]{:S(2)}, u32[]{:S(2)}) collective-permute-start(bf16[16,2176]{1,0:T(8,128)(2,1)S(1)} %constant_dynamic-update-slice_fusion.rest_7_), channel_id=1, source_target_pairs={{0,12},{4,8},{8,4},{12,0},{16,28},{20,24},{24,20},{28,16},{1,13},{... | collective-permute-start | bytes 208904 | tf_op jit(solution)/shard_map/ppermute | solution.py:252
  16.1 1.0 %collective-permute-start.6 = (bf16[16,2176]{1,0:T(8,128)(2,1)S(1)}, bf16[16,2176]{1,0:T(8,128)(2,1)S(1)}, u32[]{:S(2)}, u32[]{:S(2)}) collective-permute-start(bf16[16,2176]{1,0:T(8,128)(2,1)S(1)} %collective-permute-done.3.rest_3_), channel_id=1, source_target_pairs={{0,12},{4,8},{8,4},{12,0},{16,28},{20,24},{24,20},{28,16},{1,13},{... | collective-permute-start | bytes 208904 | tf_op jit(solution)/shard_map/ppermute | solution.py:252
  17.1 0.6 %collective-permute-start.5 = (bf16[16,2176]{1,0:T(8,128)(2,1)S(1)}, bf16[16,2176]{1,0:T(8,128)(2,1)S(1)}, u32[]{:S(2)}, u32[]{:S(2)}) collective-permute-start(bf16[16,2176]{1,0:T(8,128)(2,1)S(1)} %collective-permute-done.3.rest_3_), channel_id=1, source_target_pairs={{0,4},{4,0},{8,12},{12,8},{16,20},{20,16},{24,28},{28,24},{1,5},{5... | collective-permute-start | bytes 208904 | tf_op jit(solution)/shard_map/ppermute | solution.py:252
  17.7 1.9 %collective-permute-start.4 = (bf16[16,2176]{1,0:T(8,128)(2,1)S(1)}, bf16[16,2176]{1,0:T(8,128)(2,1)S(1)}, u32[]{:S(2)}, u32[]{:S(2)}) collective-permute-start(bf16[16,2176]{1,0:T(8,128)(2,1)S(1)} %collective-permute-done.3.rest_3_), channel_id=1, source_target_pairs={{0,8},{4,12},{8,0},{12,4},{16,24},{20,28},{24,16},{28,20},{1,9},{5... | collective-permute-start | bytes 208904 | tf_op jit(solution)/shard_map/ppermute | solution.py:252
  19.6 0.8 %collective-permute-done.7.rest_4_ = bf16[16,2176]{1,0:T(8,128)(2,1)S(1)} collective-permute-done((bf16[16,2176]{1,0:T(8,128)(2,1)S(1)}, bf16[16,2176]{1,0:T(8,128)(2,1)S(1)}, u32[]{:S(2)}, u32[]{:S(2)}) %collective-permute-start.7) | collective-permute-done | bytes 69664 | tf_op jit(solution)/shard_map/ppermute | solution.py:252
  20.5 1.1 %collective-permute-done.6.rest_2_ = bf16[16,2176]{1,0:T(8,128)(2,1)S(1)} collective-permute-done((bf16[16,2176]{1,0:T(8,128)(2,1)S(1)}, bf16[16,2176]{1,0:T(8,128)(2,1)S(1)}, u32[]{:S(2)}, u32[]{:S(2)}) %collective-permute-start.6) | collective-permute-done | bytes 69664 | tf_op jit(solution)/shard_map/ppermute | solution.py:252
  21.5 0.6 %collective-permute-done.5.rest_1_ = bf16[16,2176]{1,0:T(8,128)(2,1)S(1)} collective-permute-done((bf16[16,2176]{1,0:T(8,128)(2,1)S(1)}, bf16[16,2176]{1,0:T(8,128)(2,1)S(1)}, u32[]{:S(2)}, u32[]{:S(2)}) %collective-permute-start.5) | collective-permute-done | bytes 69664 | tf_op jit(solution)/shard_map/ppermute | solution.py:252
  22.2 0.1 collective-permute-done.4.rest_0_
  22.2 1.3 %stack.1 = f32[384,128]{1,0:T(8,128)} custom-call(s32[1]{0:T(128)} %bitcast.scalars, bf16[16,2176]{1,0:T(8,128)(2,1)S(1)} %collective-permute-done.4.rest_0_, bf16[16,2176]{1,0:T(8,128)(2,1)S(1)} %collective-permute-done.5.rest_1_, bf16[16,2176]{1,0:T(8,128)(2,1)S(1)} %collective-permute-done.6.rest_2_, bf16[16,2176]{1,0:T(8,128)(2,1)S(1)} %collective-permute-done.3.rest_3_, ...), custom_call_target="tpu_custom_call" | custom-call | tf_op jit(solution)/shard_map/stack/pallas_call | solution.py:310
  (13 shorter events, 0.0 us)
Async XLA Ops:
  2.8 4.7 %collective-permute-start = (bf16[16,512]{1,0:T(8,128)(2,1)S(1)}, bf16[16,512]{1,0:T(8,128)(2,1)S(1)}, u32[]{:S(2)}, u32[]{:S(2)}) collective-permute-start(bf16[16,512]{1,0:T(8,128)(2,1)S(1)} %get-tuple-element.10), channel_id=1, source_target_pairs={{0,2},{1,3},{2,0},{3,1},{4,6},{5,7},{6,4},{7,5},{8,10},{9,11},{10,... | collective-permute-start | bytes 49160 | tf_op jit(solution)/shard_map/ppermute | solution.py:252
  5.8 3.2 %collective-permute-start.1 = (bf16[16,512]{1,0:T(8,128)(2,1)S(1)}, bf16[16,512]{1,0:T(8,128)(2,1)S(1)}, u32[]{:S(2)}, u32[]{:S(2)}) collective-permute-start(bf16[16,512]{1,0:T(8,128)(2,1)S(1)} %get-tuple-element.11), channel_id=1, source_target_pairs={{0,3},{1,2},{2,1},{3,0},{4,7},{5,6},{6,5},{7,4},{8,11},{9,10},{10,... | collective-permute-start | bytes 49160 | tf_op jit(solution)/shard_map/ppermute | solution.py:252
  5.8 0.7 %copy-start.3 = (s32[24,1]{0,1:T(1,128)S(1)}, s32[24,1]{0,1:T(1,128)}, u32[]{:S(2)}) copy-start(s32[24,1]{0,1:T(1,128)} %param.12) | copy-start | bytes 292
  5.8 3.2 %collective-permute-start.2 = (bf16[16,512]{1,0:T(8,128)(2,1)S(1)}, bf16[16,512]{1,0:T(8,128)(2,1)S(1)}, u32[]{:S(2)}, u32[]{:S(2)}) collective-permute-start(bf16[16,512]{1,0:T(8,128)(2,1)S(1)} %get-tuple-element.12), channel_id=1, source_target_pairs={{0,1},{1,0},{2,3},{3,2},{4,5},{5,4},{6,7},{7,6},{8,9},{9,8},{10,11... | collective-permute-start | bytes 49160 | tf_op jit(solution)/shard_map/ppermute | solution.py:252
  6.6 0.7 %copy-start = (s32[1,24]{1,0:T(1,128)S(1)}, s32[1,24]{1,0:T(1,128)}, u32[]{:S(2)}) copy-start(s32[1,24]{1,0:T(1,128)} %param.11) | copy-start | bytes 292
  6.6 0.7 %copy-start.1 = (s32[1,24]{1,0:T(1,128)S(1)}, s32[1,24]{1,0:T(1,128)}, u32[]{:S(2)}) copy-start(s32[1,24]{1,0:T(1,128)} %param.10) | copy-start | bytes 292
  6.6 0.7 %copy-start.2 = (s32[1,24]{1,0:T(1,128)S(1)}, s32[1,24]{1,0:T(1,128)}, u32[]{:S(2)}) copy-start(s32[1,24]{1,0:T(1,128)} %param.9) | copy-start | bytes 292
  9.0 7.2 %collective-permute-start.3 = (bf16[16,2176]{1,0:T(8,128)(2,1)S(1)}, bf16[16,2176]{1,0:T(8,128)(2,1)S(1)}, u32[]{:S(2)}, u32[]{:S(2)}) collective-permute-start(bf16[16,2176]{1,0:T(8,128)(2,1)S(1)} %constant_dynamic-update-slice_fusion.rest_7_), channel_id=1, source_target_pairs={{0,24},{4,28},{8,16},{12,20},{16,8},{20,12},{24,0},{28,4},{1,25},{... | collective-permute-start | bytes 208904 | tf_op jit(solution)/shard_map/ppermute | solution.py:252
  12.7 5.1 %collective-permute-start.9 = (bf16[16,2176]{1,0:T(8,128)(2,1)S(1)}, bf16[16,2176]{1,0:T(8,128)(2,1)S(1)}, u32[]{:S(2)}, u32[]{:S(2)}) collective-permute-start(bf16[16,2176]{1,0:T(8,128)(2,1)S(1)} %constant_dynamic-update-slice_fusion.rest_7_), channel_id=1, source_target_pairs={{0,4},{4,0},{8,12},{12,8},{16,20},{20,16},{24,28},{28,24},{1,5},{5... | collective-permute-start | bytes 208904 | tf_op jit(solution)/shard_map/ppermute | solution.py:252
  14.2 5.5 %collective-permute-start.8 = (bf16[16,2176]{1,0:T(8,128)(2,1)S(1)}, bf16[16,2176]{1,0:T(8,128)(2,1)S(1)}, u32[]{:S(2)}, u32[]{:S(2)}) collective-permute-start(bf16[16,2176]{1,0:T(8,128)(2,1)S(1)} %constant_dynamic-update-slice_fusion.rest_7_), channel_id=1, source_target_pairs={{0,8},{4,12},{8,0},{12,4},{16,24},{20,28},{24,16},{28,20},{1,9},{5... | collective-permute-start | bytes 208904 | tf_op jit(solution)/shard_map/ppermute | solution.py:252
  14.2 6.3 %collective-permute-start.7 = (bf16[16,2176]{1,0:T(8,128)(2,1)S(1)}, bf16[16,2176]{1,0:T(8,128)(2,1)S(1)}, u32[]{:S(2)}, u32[]{:S(2)}) collective-permute-start(bf16[16,2176]{1,0:T(8,128)(2,1)S(1)} %constant_dynamic-update-slice_fusion.rest_7_), channel_id=1, source_target_pairs={{0,12},{4,8},{8,4},{12,0},{16,28},{20,24},{24,20},{28,16},{1,13},{... | collective-permute-start | bytes 208904 | tf_op jit(solution)/shard_map/ppermute | solution.py:252
  16.1 5.4 %collective-permute-start.6 = (bf16[16,2176]{1,0:T(8,128)(2,1)S(1)}, bf16[16,2176]{1,0:T(8,128)(2,1)S(1)}, u32[]{:S(2)}, u32[]{:S(2)}) collective-permute-start(bf16[16,2176]{1,0:T(8,128)(2,1)S(1)} %collective-permute-done.3.rest_3_), channel_id=1, source_target_pairs={{0,12},{4,8},{8,4},{12,0},{16,28},{20,24},{24,20},{28,16},{1,13},{... | collective-permute-start | bytes 208904 | tf_op jit(solution)/shard_map/ppermute | solution.py:252
  17.1 5.1 %collective-permute-start.5 = (bf16[16,2176]{1,0:T(8,128)(2,1)S(1)}, bf16[16,2176]{1,0:T(8,128)(2,1)S(1)}, u32[]{:S(2)}, u32[]{:S(2)}) collective-permute-start(bf16[16,2176]{1,0:T(8,128)(2,1)S(1)} %collective-permute-done.3.rest_3_), channel_id=1, source_target_pairs={{0,4},{4,0},{8,12},{12,8},{16,20},{20,16},{24,28},{28,24},{1,5},{5... | collective-permute-start | bytes 208904 | tf_op jit(solution)/shard_map/ppermute | solution.py:252
  17.7 4.5 %collective-permute-start.4 = (bf16[16,2176]{1,0:T(8,128)(2,1)S(1)}, bf16[16,2176]{1,0:T(8,128)(2,1)S(1)}, u32[]{:S(2)}, u32[]{:S(2)}) collective-permute-start(bf16[16,2176]{1,0:T(8,128)(2,1)S(1)} %collective-permute-done.3.rest_3_), channel_id=1, source_target_pairs={{0,8},{4,12},{8,0},{12,4},{16,24},{20,28},{24,16},{28,20},{1,9},{5... | collective-permute-start | bytes 208904 | tf_op jit(solution)/shard_map/ppermute | solution.py:252

commit v8 on v7

--- a/solution.py
+++ b/solution.py
@@ -218,9 +218,9 @@
     receiver_row = jnp.where(filled, receiver_row, -depth)
     rows_of = [source_row, source_row + channels, receiver_row, receiver_row + channels]
     parts = width // LANES
-    half = slots // 2
+    cut = slots - 16
     copies = []
-    for first in (0, half):
+    for first, half in ((0, cut), (cut, slots - cut)):
         choice = [pick(index[first : first + half, :1], depth) for index in rows_of]
         choice = jnp.concatenate(choice, axis=0).astype(BF16)
         real = jnp.zeros((half, width), F32)

time: 23.7 us -> 23.6 us (level)
  no operation moved by 1% of the time
where the time goes in v8:
time: 23.6 us; the launch traced here: 23.5 us
  starting transfers between devices  13.8 us (58%)
  waiting for transfers between devices  4.28 us (18%)
  Pallas kernels  3.4 us (14%)
  local copies, waits for them, and re-layouts  1.13 us (5%)
  between operations  0.72 us (3%)
    ppermute x10, starting transfers between devices, swapped(): return lax.ppermute(value, axis, [(i, i ^ bits) for i in range(peers)])  13.8 us
    ppermute x10, waiting for transfers between devices, swapped(): return lax.ppermute(value, axis, [(i, i ^ bits) for i in range(peers)])  4.28 us
    pallas_call x1, Pallas kernels, local(): pl.pallas_call(whiten_kernel, out_shape=[jax.ShapeDtypeStruct((height, wi...  2.15 us
    pallas_call x1, Pallas kernels, local(): pl.pallas_call(functools.partial(stack_kernel, blocks, windows, capacity,...  1.25 us
    unnamed x11, local copies, waits for them, and re-layouts  1.13 us
  transfers between devices with their start and end apart: 10, of which 6 were waited for; matrix products, arithmetic and copies ran while one was open for 0% of the time, Pallas kernels for 0%

profile of v8, /device:TPU:0, one launch (start us, length us, event | category | flops | bytes accessed | tf_op | source)
XLA Modules:
  0.0 23.5 jit_solution(5722273205185925342)
XLA Ops:
  0.7 2.2 %whiten.1 = (bf16[16,512]{1,0:T(8,128)(2,1)S(1)}, bf16[16,512]{1,0:T(8,128)(2,1)S(1)}, bf16[16,512]{1,0:T(8,128)(2,1)S(1)}, bf16[16,512]{1,0:T(8,128)(2,1)S(1)}) custom-call(s32[1]{0:T(128)} %bitcast.4.place_ref, f32[8,12288]{1,0:T(8,128)} %traces_far.1, s32[1]{0:T(128)S(6)} %copy.14.offsets_far, f32[480,128]{1,0:T(8,128)} %constant.15.clone.table_far), custom_call_target="tpu_custom_call" | custom-call | tf_op jit(solution)/shard_map/whiten/pallas_call | solution.py:268
  2.8 3.0 %collective-permute-start = (bf16[16,512]{1,0:T(8,128)(2,1)S(1)}, bf16[16,512]{1,0:T(8,128)(2,1)S(1)}, u32[]{:S(2)}, u32[]{:S(2)}) collective-permute-start(bf16[16,512]{1,0:T(8,128)(2,1)S(1)} %get-tuple-element.10), channel_id=1, source_target_pairs={{0,2},{1,3},{2,0},{3,1},{4,6},{5,7},{6,4},{7,5},{8,10},{9,11},{10,... | collective-permute-start | bytes 49160 | tf_op jit(solution)/shard_map/ppermute | solution.py:252
  5.8 0.0 collective-permute-start.1
  5.8 0.2 collective-permute-start.2
  6.0 0.5 %copy-done.3 = s32[24,1]{0,1:T(1,128)S(1)} copy-done((s32[24,1]{0,1:T(1,128)S(1)}, s32[24,1]{0,1:T(1,128)}, u32[]{:S(2)}) %copy-start.3) | copy-done | bytes 120
  6.5 0.1 convert_reduce_fusion
  6.6 0.0 copy-start.1
  6.6 0.0 copy-start.2
  6.6 0.6 %copy-done = s32[1,24]{1,0:T(1,128)S(1)} copy-done((s32[1,24]{1,0:T(1,128)S(1)}, s32[1,24]{1,0:T(1,128)}, u32[]{:S(2)}) %copy-start) | copy-done | bytes 120
  7.2 0.0 copy-done.1
  7.2 0.0 copy-done.2
  7.3 0.3 %collective-permute-done = bf16[16,512]{1,0:T(8,128)(2,1)S(1)} collective-permute-done((bf16[16,512]{1,0:T(8,128)(2,1)S(1)}, bf16[16,512]{1,0:T(8,128)(2,1)S(1)}, u32[]{:S(2)}, u32[]{:S(2)}) %collective-permute-start) | collective-permute-done | bytes 16416 | tf_op jit(solution)/shard_map/ppermute | solution.py:252
  7.5 1.4 %collective-permute-done.1 = bf16[16,512]{1,0:T(8,128)(2,1)S(1)} collective-permute-done((bf16[16,512]{1,0:T(8,128)(2,1)S(1)}, bf16[16,512]{1,0:T(8,128)(2,1)S(1)}, u32[]{:S(2)}, u32[]{:S(2)}) %collective-permute-start.1) | collective-permute-done | bytes 16416 | tf_op jit(solution)/shard_map/ppermute | solution.py:252
  9.0 3.7 %collective-permute-start.3 = (bf16[16,2176]{1,0:T(8,128)(2,1)S(1)}, bf16[16,2176]{1,0:T(8,128)(2,1)S(1)}, u32[]{:S(2)}, u32[]{:S(2)}) collective-permute-start(bf16[16,2176]{1,0:T(8,128)(2,1)S(1)} %constant_dynamic-update-slice_fusion.rest_7_), channel_id=1, source_target_pairs={{0,24},{4,28},{8,16},{12,20},{16,8},{20,12},{24,0},{28,4},{1,25},{... | collective-permute-start | bytes 208904 | tf_op jit(solution)/shard_map/ppermute | solution.py:252
  12.7 1.5 %collective-permute-start.9 = (bf16[16,2176]{1,0:T(8,128)(2,1)S(1)}, bf16[16,2176]{1,0:T(8,128)(2,1)S(1)}, u32[]{:S(2)}, u32[]{:S(2)}) collective-permute-start(bf16[16,2176]{1,0:T(8,128)(2,1)S(1)} %constant_dynamic-update-slice_fusion.rest_7_), channel_id=1, source_target_pairs={{0,4},{4,0},{8,12},{12,8},{16,20},{20,16},{24,28},{28,24},{1,5},{5... | collective-permute-start | bytes 208904 | tf_op jit(solution)/shard_map/ppermute | solution.py:252
  14.2 2.0 %collective-permute-start.7 = (bf16[16,2176]{1,0:T(8,128)(2,1)S(1)}, bf16[16,2176]{1,0:T(8,128)(2,1)S(1)}, u32[]{:S(2)}, u32[]{:S(2)}) collective-permute-start(bf16[16,2176]{1,0:T(8,128)(2,1)S(1)} %constant_dynamic-update-slice_fusion.rest_7_), channel_id=1, source_target_pairs={{0,12},{4,8},{8,4},{12,0},{16,28},{20,24},{24,20},{28,16},{1,13},{... | collective-permute-start | bytes 208904 | tf_op jit(solution)/shard_map/ppermute | solution.py:252
  16.1 1.0 %collective-permute-start.6 = (bf16[16,2176]{1,0:T(8,128)(2,1)S(1)}, bf16[16,2176]{1,0:T(8,128)(2,1)S(1)}, u32[]{:S(2)}, u32[]{:S(2)}) collective-permute-start(bf16[16,2176]{1,0:T(8,128)(2,1)S(1)} %collective-permute-done.3.rest_3_), channel_id=1, source_target_pairs={{0,12},{4,8},{8,4},{12,0},{16,28},{20,24},{24,20},{28,16},{1,13},{... | collective-permute-start | bytes 208904 | tf_op jit(solution)/shard_map/ppermute | solution.py:252
  17.1 0.6 %collective-permute-start.5 = (bf16[16,2176]{1,0:T(8,128)(2,1)S(1)}, bf16[16,2176]{1,0:T(8,128)(2,1)S(1)}, u32[]{:S(2)}, u32[]{:S(2)}) collective-permute-start(bf16[16,2176]{1,0:T(8,128)(2,1)S(1)} %collective-permute-done.3.rest_3_), channel_id=1, source_target_pairs={{0,4},{4,0},{8,12},{12,8},{16,20},{20,16},{24,28},{28,24},{1,5},{5... | collective-permute-start | bytes 208904 | tf_op jit(solution)/shard_map/ppermute | solution.py:252
  17.7 1.9 %collective-permute-start.4 = (bf16[16,2176]{1,0:T(8,128)(2,1)S(1)}, bf16[16,2176]{1,0:T(8,128)(2,1)S(1)}, u32[]{:S(2)}, u32[]{:S(2)}) collective-permute-start(bf16[16,2176]{1,0:T(8,128)(2,1)S(1)} %collective-permute-done.3.rest_3_), channel_id=1, source_target_pairs={{0,8},{4,12},{8,0},{12,4},{16,24},{20,28},{24,16},{28,20},{1,9},{5... | collective-permute-start | bytes 208904 | tf_op jit(solution)/shard_map/ppermute | solution.py:252
  19.6 0.8 %collective-permute-done.7.rest_4_ = bf16[16,2176]{1,0:T(8,128)(2,1)S(1)} collective-permute-done((bf16[16,2176]{1,0:T(8,128)(2,1)S(1)}, bf16[16,2176]{1,0:T(8,128)(2,1)S(1)}, u32[]{:S(2)}, u32[]{:S(2)}) %collective-permute-start.7) | collective-permute-done | bytes 69664 | tf_op jit(solution)/shard_map/ppermute | solution.py:252
  20.5 1.1 %collective-permute-done.6.rest_2_ = bf16[16,2176]{1,0:T(8,128)(2,1)S(1)} collective-permute-done((bf16[16,2176]{1,0:T(8,128)(2,1)S(1)}, bf16[16,2176]{1,0:T(8,128)(2,1)S(1)}, u32[]{:S(2)}, u32[]{:S(2)}) %collective-permute-start.6) | collective-permute-done | bytes 69664 | tf_op jit(solution)/shard_map/ppermute | solution.py:252
  21.5 0.6 %collective-permute-done.5.rest_1_ = bf16[16,2176]{1,0:T(8,128)(2,1)S(1)} collective-permute-done((bf16[16,2176]{1,0:T(8,128)(2,1)S(1)}, bf16[16,2176]{1,0:T(8,128)(2,1)S(1)}, u32[]{:S(2)}, u32[]{:S(2)}) %collective-permute-start.5) | collective-permute-done | bytes 69664 | tf_op jit(solution)/shard_map/ppermute | solution.py:252
  22.2 0.1 collective-permute-done.4.rest_0_
  22.2 1.3 %stack.1 = f32[384,128]{1,0:T(8,128)} custom-call(s32[1]{0:T(128)} %bitcast.scalars, bf16[16,2176]{1,0:T(8,128)(2,1)S(1)} %collective-permute-done.4.rest_0_, bf16[16,2176]{1,0:T(8,128)(2,1)S(1)} %collective-permute-done.5.rest_1_, bf16[16,2176]{1,0:T(8,128)(2,1)S(1)} %collective-permute-done.6.rest_2_, bf16[16,2176]{1,0:T(8,128)(2,1)S(1)} %collective-permute-done.3.rest_3_, ...), custom_call_target="tpu_custom_call" | custom-call | tf_op jit(solution)/shard_map/stack/pallas_call | solution.py:310
  (13 shorter events, 0.0 us)
Async XLA Ops:
  2.8 4.7 %collective-permute-start = (bf16[16,512]{1,0:T(8,128)(2,1)S(1)}, bf16[16,512]{1,0:T(8,128)(2,1)S(1)}, u32[]{:S(2)}, u32[]{:S(2)}) collective-permute-start(bf16[16,512]{1,0:T(8,128)(2,1)S(1)} %get-tuple-element.10), channel_id=1, source_target_pairs={{0,2},{1,3},{2,0},{3,1},{4,6},{5,7},{6,4},{7,5},{8,10},{9,11},{10,... | collective-permute-start | bytes 49160 | tf_op jit(solution)/shard_map/ppermute | solution.py:252
  5.8 3.2 %collective-permute-start.1 = (bf16[16,512]{1,0:T(8,128)(2,1)S(1)}, bf16[16,512]{1,0:T(8,128)(2,1)S(1)}, u32[]{:S(2)}, u32[]{:S(2)}) collective-permute-start(bf16[16,512]{1,0:T(8,128)(2,1)S(1)} %get-tuple-element.11), channel_id=1, source_target_pairs={{0,3},{1,2},{2,1},{3,0},{4,7},{5,6},{6,5},{7,4},{8,11},{9,10},{10,... | collective-permute-start | bytes 49160 | tf_op jit(solution)/shard_map/ppermute | solution.py:252
  5.8 0.7 %copy-start.3 = (s32[24,1]{0,1:T(1,128)S(1)}, s32[24,1]{0,1:T(1,128)}, u32[]{:S(2)}) copy-start(s32[24,1]{0,1:T(1,128)} %param.12) | copy-start | bytes 292
  5.8 3.2 %collective-permute-start.2 = (bf16[16,512]{1,0:T(8,128)(2,1)S(1)}, bf16[16,512]{1,0:T(8,128)(2,1)S(1)}, u32[]{:S(2)}, u32[]{:S(2)}) collective-permute-start(bf16[16,512]{1,0:T(8,128)(2,1)S(1)} %get-tuple-element.12), channel_id=1, source_target_pairs={{0,1},{1,0},{2,3},{3,2},{4,5},{5,4},{6,7},{7,6},{8,9},{9,8},{10,11... | collective-permute-start | bytes 49160 | tf_op jit(solution)/shard_map/ppermute | solution.py:252
  6.6 0.7 %copy-start = (s32[1,24]{1,0:T(1,128)S(1)}, s32[1,24]{1,0:T(1,128)}, u32[]{:S(2)}) copy-start(s32[1,24]{1,0:T(1,128)} %param.11) | copy-start | bytes 292
  6.6 0.7 %copy-start.1 = (s32[1,24]{1,0:T(1,128)S(1)}, s32[1,24]{1,0:T(1,128)}, u32[]{:S(2)}) copy-start(s32[1,24]{1,0:T(1,128)} %param.10) | copy-start | bytes 292
  6.6 0.7 %copy-start.2 = (s32[1,24]{1,0:T(1,128)S(1)}, s32[1,24]{1,0:T(1,128)}, u32[]{:S(2)}) copy-start(s32[1,24]{1,0:T(1,128)} %param.9) | copy-start | bytes 292
  9.0 7.2 %collective-permute-start.3 = (bf16[16,2176]{1,0:T(8,128)(2,1)S(1)}, bf16[16,2176]{1,0:T(8,128)(2,1)S(1)}, u32[]{:S(2)}, u32[]{:S(2)}) collective-permute-start(bf16[16,2176]{1,0:T(8,128)(2,1)S(1)} %constant_dynamic-update-slice_fusion.rest_7_), channel_id=1, source_target_pairs={{0,24},{4,28},{8,16},{12,20},{16,8},{20,12},{24,0},{28,4},{1,25},{... | collective-permute-start | bytes 208904 | tf_op jit(solution)/shard_map/ppermute | solution.py:252
  12.7 5.1 %collective-permute-start.9 = (bf16[16,2176]{1,0:T(8,128)(2,1)S(1)}, bf16[16,2176]{1,0:T(8,128)(2,1)S(1)}, u32[]{:S(2)}, u32[]{:S(2)}) collective-permute-start(bf16[16,2176]{1,0:T(8,128)(2,1)S(1)} %constant_dynamic-update-slice_fusion.rest_7_), channel_id=1, source_target_pairs={{0,4},{4,0},{8,12},{12,8},{16,20},{20,16},{24,28},{28,24},{1,5},{5... | collective-permute-start | bytes 208904 | tf_op jit(solution)/shard_map/ppermute | solution.py:252
  14.2 5.5 %collective-permute-start.8 = (bf16[16,2176]{1,0:T(8,128)(2,1)S(1)}, bf16[16,2176]{1,0:T(8,128)(2,1)S(1)}, u32[]{:S(2)}, u32[]{:S(2)}) collective-permute-start(bf16[16,2176]{1,0:T(8,128)(2,1)S(1)} %constant_dynamic-update-slice_fusion.rest_7_), channel_id=1, source_target_pairs={{0,8},{4,12},{8,0},{12,4},{16,24},{20,28},{24,16},{28,20},{1,9},{5... | collective-permute-start | bytes 208904 | tf_op jit(solution)/shard_map/ppermute | solution.py:252
  14.2 6.3 %collective-permute-start.7 = (bf16[16,2176]{1,0:T(8,128)(2,1)S(1)}, bf16[16,2176]{1,0:T(8,128)(2,1)S(1)}, u32[]{:S(2)}, u32[]{:S(2)}) collective-permute-start(bf16[16,2176]{1,0:T(8,128)(2,1)S(1)} %constant_dynamic-update-slice_fusion.rest_7_), channel_id=1, source_target_pairs={{0,12},{4,8},{8,4},{12,0},{16,28},{20,24},{24,20},{28,16},{1,13},{... | collective-permute-start | bytes 208904 | tf_op jit(solution)/shard_map/ppermute | solution.py:252
  16.1 5.4 %collective-permute-start.6 = (bf16[16,2176]{1,0:T(8,128)(2,1)S(1)}, bf16[16,2176]{1,0:T(8,128)(2,1)S(1)}, u32[]{:S(2)}, u32[]{:S(2)}) collective-permute-start(bf16[16,2176]{1,0:T(8,128)(2,1)S(1)} %collective-permute-done.3.rest_3_), channel_id=1, source_target_pairs={{0,12},{4,8},{8,4},{12,0},{16,28},{20,24},{24,20},{28,16},{1,13},{... | collective-permute-start | bytes 208904 | tf_op jit(solution)/shard_map/ppermute | solution.py:252
  17.1 5.1 %collective-permute-start.5 = (bf16[16,2176]{1,0:T(8,128)(2,1)S(1)}, bf16[16,2176]{1,0:T(8,128)(2,1)S(1)}, u32[]{:S(2)}, u32[]{:S(2)}) collective-permute-start(bf16[16,2176]{1,0:T(8,128)(2,1)S(1)} %collective-permute-done.3.rest_3_), channel_id=1, source_target_pairs={{0,4},{4,0},{8,12},{12,8},{16,20},{20,16},{24,28},{28,24},{1,5},{5... | collective-permute-start | bytes 208904 | tf_op jit(solution)/shard_map/ppermute | solution.py:252
  17.7 4.5 %collective-permute-start.4 = (bf16[16,2176]{1,0:T(8,128)(2,1)S(1)}, bf16[16,2176]{1,0:T(8,128)(2,1)S(1)}, u32[]{:S(2)}, u32[]{:S(2)}) collective-permute-start(bf16[16,2176]{1,0:T(8,128)(2,1)S(1)} %collective-permute-done.3.rest_3_), channel_id=1, source_target_pairs={{0,8},{4,12},{8,0},{12,4},{16,24},{20,28},{24,16},{28,20},{1,9},{5... | collective-permute-start | bytes 208904 | tf_op jit(solution)/shard_map/ppermute | solution.py:252
